TPU v7x, 32 devices: a whole 2x2x4 slice. The times are simulated.
32 devices in a mesh: dp: 4 (over z), mp: 8 (over y, x, core).
Axes of the slice: x: 2, y: 2, z: 4, core: 2. Of those that a mesh axis runs over, the one named last changes fastest.
Arguments:
- tokens: int32 [8, 1024], P('dp'), may hold values from 0 to 49151
- targets: int32 [8, 256], P('dp'), may hold values from 0 to 49151
- pair_order: int32 [8], replicated, may hold values from 0 to 7, each once
- lengths: int32 [8], P('dp'), may hold values from 1 to 256
- loss_mask: int32 [8, 256], P('dp'), may hold values 0 or 1
- start_pos: int32 [8], P('dp'), may hold values from 0 to 4095
- owner_map: int32 [8, 512], P('mp'), may hold values from 0 to 511, as said below
- block_master: float32 [8, 512, 128, 128], P('mp', 'dp')
- left_stat: float32 [8, 512, 128, 128], P('mp', 'dp')
- right_stat: float32 [8, 512, 128, 128], P('mp', 'dp')
- left_root: float32 [8, 512, 128, 128], P('mp', 'dp')
- right_root: float32 [8, 512, 128, 128], P('mp', 'dp')
- table_master: float32 [49152, 2048], P('mp', 'dp')
- table_moment: float32 [49152, 2048], P('mp', 'dp')
- table_second: float32 [49152, 2048], P('mp', 'dp')
- gain_master: float32 [3, 2048], P(None, 'dp')
- gain_moment: float32 [3, 2048], P(None, 'dp')
- gain_second: float32 [3, 2048], P(None, 'dp')
Outputs:
- loss_total: float32 [], replicated
- clip_norm: float32 [], replicated
- block_new: float32 [8, 512, 128, 128], P('mp', 'dp')
- block_copy: bfloat16 [8, 512, 128, 128], P('mp', 'dp')
- block_grad: float32 [8, 512, 128, 128], P('mp', 'dp')
- left_new: float32 [8, 512, 128, 128], P('mp', 'dp')
- right_new: float32 [8, 512, 128, 128], P('mp', 'dp')
- table_new: float32 [49152, 2048], P('mp', 'dp')
- table_copy: bfloat16 [49152, 2048], P('mp', 'dp')
- table_moment_new: float32 [49152, 2048], P('mp', 'dp')
- table_second_new: float32 [49152, 2048], P('mp', 'dp')
- gain_new: float32 [3, 2048], P(None, 'dp')
- gain_moment_new: float32 [3, 2048], P(None, 'dp')
- gain_second_new: float32 [3, 2048], P(None, 'dp')
Inputs may be any that keep to these rules, and one draw needn't show every extreme that they name: Items whose pair_order values share the quotient by 2 form a pair. `owner_map`: each row is a permutation of 0 to 511.
All inputs are finite; a program needn't handle non-finite values. No bound on the sum of `loss_mask` on one device may be relied on, other than what follows from the above.
Results may differ from a plain program's by a relative error of at most 0.012.
The roundings to bfloat16 on the way count: a program that leaves them out, or rounds other values in their place, can miss the bound.
Values may be sent and summed in bfloat16 or wider, within the bound.
A program may use at most 512 MiB of HBM per device.

v0:
```python
import functools

import jax
import jax.numpy as jnp
from jax import lax
from jax.experimental import pallas as pl
from jax.experimental.pallas import tpu as pltpu
from jax.sharding import PartitionSpec as P

D = 2048
HD = 64
FF = 8192
ANS = 256
STEP = 5


EPS_NORM = 1e-05
ROPE_BASE = 130000.0
CLIP_NORM = 0.01
STAT_DECAY = 0.95
LR_MATRIX = 0.05
DECAY_MATRIX = 0.1
LR_TABLE = 0.03
DECAY_TABLE = 0.1
LR_GAIN = 0.2
ADAM_ONE = 0.9
ADAM_TWO = 0.95
ADAM_EPS = 1e-08
MASKED = -1e30
F32 = jnp.float32
BF16 = jnp.bfloat16


def dot(spec, a, b):
    return jnp.einsum(spec, a, b, preferred_element_type=F32)


def cube_bits(n):
    bits = [1 << i for i in range(n.bit_length() - 1)]
    return bits[1:] + bits[:1]


def cube_order(n):
    order = [0]
    for bit in cube_bits(n):
        order = order + [o ^ bit for o in order]
    return order


def swap(x, axis, bit):
    n = lax.axis_size(axis)
    return lax.ppermute(x, axis, [(i, i ^ bit) for i in range(n)])


def cube_gather(x):
    n = lax.axis_size("mp")
    if n != 8:
        held = x[None]
        for bit in cube_bits(n):
            held = jnp.concatenate([held, swap(held, "mp", bit)])
        return held
    half = x.shape[0] // 2
    over_x = swap(x, "mp", 2)
    over_y = swap(x, "mp", 4)
    far = jnp.concatenate([swap(over_x[:half], "mp", 4), swap(over_y[half:], "mp", 2)])
    held = jnp.stack([x, over_x, over_y, far])
    return jnp.concatenate([held, swap(held, "mp", 1)])


def cube_scatter(parts):
    n = lax.axis_size("mp")
    if n != 8:
        held = parts
        for bit in reversed(cube_bits(n)):
            keep = held.shape[0] // 2
            other = swap(held[keep:].astype(BF16), "mp", bit)
            held = held[:keep].astype(F32) + other.astype(F32)
        return held[0]
    got = swap(parts[4:], "mp", 1)
    held = (parts[:4].astype(F32) + got.astype(F32)).astype(BF16)
    half = held.shape[1] // 2
    one, two = held[:, :half], held[:, half:]
    one_x = swap(one[1::2], "mp", 2)
    two_y = swap(two[2:], "mp", 4)
    one = one[0::2].astype(F32) + one_x.astype(F32)
    two = two[:2].astype(F32) + two_y.astype(F32)
    one_y = swap(one[1].astype(BF16), "mp", 4)
    two_x = swap(two[1].astype(BF16), "mp", 2)
    return jnp.concatenate([one[0] + one_y.astype(F32), two[0] + two_x.astype(F32)])


def line_gather(x):
    return [x] + [swap(x, "dp", o) for o in range(1, lax.axis_size("dp"))]


def line_exchange(parts):
    return [parts[0]] + [swap(parts[o], "dp", o) for o in range(1, len(parts))]


def combine_stats(a, b):
    top = jnp.maximum(a[0], b[0])
    total = a[1] * jnp.exp(a[0] - top) + b[1] * jnp.exp(b[0] - top)
    return jnp.stack([top, total, a[2] + b[2]])


def everywhere(x, op):
    for axis in ("mp", "dp"):
        bit = 1
        while bit < lax.axis_size(axis):
            x = op(x, swap(x, axis, bit))
            bit *= 2
    return x


def stats_everywhere(x, rows):
    n_mp, n_dp = lax.axis_size("mp"), lax.axis_size("dp")
    bits = cube_bits(n_mp)
    split = (3,) + (2,) * len(bits) + (n_dp * rows,)
    x = x.reshape(split)
    for i, bit in enumerate(bits):
        x = combine_stats(x, jnp.flip(swap(x, "mp", bit), len(bits) - i))
    x = x.reshape(3, n_mp, n_dp, rows)
    total = x
    for o, other in enumerate(line_gather(x)):
        if o:
            order = [e ^ o for e in range(n_dp)]
            total = combine_stats(total, jnp.stack([other[:, :, e] for e in order], axis=2))
    return total.reshape(3, -1)


def peer_copy(src, dst, sems, k, **device):
    return pltpu.make_async_remote_copy(
        src_ref=src,
        dst_ref=dst,
        send_sem=sems.at[0, k],
        recv_sem=sems.at[1, k],
        device_id=device,
        device_id_type=pl.DeviceIdType.MESH,
    )


def greet(n_dp, bits=(1, 2, 4)):
    me = lax.axis_index("mp")
    a = lax.axis_index("dp")
    barrier = pltpu.get_barrier_semaphore()
    partners = [{"mp": me ^ bit} for bit in bits]
    partners += [{"dp": a ^ o} for o in range(1, n_dp)]
    for partner in partners:
        pl.semaphore_signal(barrier, 1, device_id=partner, device_id_type=pl.DeviceIdType.MESH)
    pl.semaphore_wait(barrier, len(partners))


def by_rows(count, step):
    @pl.loop(0, count // 16)
    def _(i):
        step(pl.multiple_of(i * 16, 16))


class PlaneSum:
    def __init__(self, parts, own, core, held, near, last, sems, first, blocks):
        me = lax.axis_index("mp")
        self.refs = parts, own, core, held, near, last
        self.rows = own.shape[0] // blocks
        self.half = half = self.rows // 2
        self.at_core = []
        self.blocks = []
        for b in range(blocks):
            whole = pl.ds(b * self.rows, self.rows)
            top, low = pl.ds(b * self.rows, half), pl.ds(b * self.rows + half, half)
            spot = pl.ds(b * half, half)
            k = first + 7 * b
            self.at_core.append(
                peer_copy(parts.at[4:8, whole], core.at[:, whole], sems, k, mp=me ^ 1)
            )
            sends = (
                (3, top, near, 0, 2),
                (3, low, near, 1, 4),
                (1, top, near, 2, 2),
                (2, low, near, 3, 4),
                (2, top, last, 0, 4),
                (1, low, last, 1, 2),
            )
            self.blocks.append(
                [
                    peer_copy(held.at[s, rows], to.at[at, spot], sems, k + 1 + e, mp=me ^ bit)
                    for e, (s, rows, to, at, bit) in enumerate(sends)
                ]
            )

    def first_sends(self, b):
        self.at_core[b].wait_recv()
        parts, _, core, held, _, _ = self.refs
        copies = self.blocks[b]
        for s, sent in ((3, copies[:2]), (1, copies[2:3]), (2, copies[3:4])):

            def add(at, s=s):
                rows = pl.ds(b * self.rows + at, 16)
                value = parts[s, rows].astype(F32) + core[s, rows].astype(F32)
                held[s, rows] = value.astype(BF16)

            by_rows(self.rows, add)
            for copy in sent:
                copy.start()

    def second_sends(self, b):
        _, _, _, held, near, _ = self.refs
        copies = self.blocks[b]
        for e, s, offset in ((0, 2, 0), (1, 1, self.half)):
            copies[e].wait_recv()

            def add(at, e=e, s=s, offset=offset):
                rows = pl.ds(b * self.rows + offset + at, 16)
                value = held[s, rows].astype(F32) + near[e, pl.ds(b * self.half + at, 16)].astype(F32)
                held[s, rows] = value.astype(BF16)

            by_rows(self.half, add)
            copies[4 + e].start()

    def finish(self, b):
        parts, own, core, _, near, last = self.refs
        for copy in self.blocks[b][2:]:
            copy.wait_recv()

        def total(at):
            spot = pl.ds(b * self.half + at, 16)
            for e, offset in ((0, 0), (1, self.half)):
                rows = pl.ds(b * self.rows + offset + at, 16)
                own[rows] = (
                    (parts[0, rows].astype(F32) + core[0, rows].astype(F32))
                    + near[2 + e, spot].astype(F32)
                    + last[e, spot].astype(F32)
                )

        by_rows(self.half, total)

    def close(self):
        for core, copies in zip(self.at_core, self.blocks):
            core.wait_send()
            for copy in copies:
                copy.wait_send()

    def run(self):
        for b in range(len(self.blocks)):
            self.at_core[b].start()
        for step in (self.first_sends, self.second_sends, self.finish):
            for b in range(len(self.blocks)):
                step(b)
        self.close()


class PlaneSpread:
    def __init__(self, x, out, sems, k, start, rows):
        me = lax.axis_index("mp")
        half = rows // 2
        top, low, whole = pl.ds(start, half), pl.ds(start + half, half), pl.ds(start, rows)
        self.own = x, out, start, rows

        def copy(src, slot, part, e, bit):
            return peer_copy(src, out.at[slot, part], sems, k + e, mp=me ^ bit)

        self.x_top = copy(x.at[top], 1, top, 0, 2)
        self.y_low = copy(x.at[low], 2, low, 1, 4)
        self.x_low = copy(x.at[low], 1, low, 2, 2)
        self.y_top = copy(x.at[top], 2, top, 3, 4)
        self.core = copy(x.at[whole], 4, whole, 4, 1)
        self.far_y = copy(out.at[1, top], 3, top, 5, 4)
        self.far_x = copy(out.at[2, low], 3, low, 6, 2)
        self.to_core = {
            (s, r): copy(out.at[s, part], 4 + s, part, 7 + 2 * (s - 1) + r, 1)
            for s in (1, 2, 3)
            for r, part in enumerate((top, low))
        }

    def begin(self):
        for c in (self.x_top, self.y_low, self.x_low, self.y_top, self.core):
            c.start()
        x, out, start, rows = self.own

        def keep(at):
            part = pl.ds(start + at, 16)
            out[0, part] = x[part]

        by_rows(rows, keep)

    def relay(self):
        self.x_top.wait_recv()
        self.far_y.start()
        self.to_core[1, 0].start()
        self.y_low.wait_recv()
        self.far_x.start()
        self.to_core[2, 1].start()
        self.x_low.wait_recv()
        self.to_core[1, 1].start()
        self.y_top.wait_recv()
        self.to_core[2, 0].start()

    def relay_far(self):
        self.far_y.wait_recv()
        self.to_core[3, 0].start()
        self.far_x.wait_recv()
        self.to_core[3, 1].start()

    def arrive(self):
        self.core.wait_recv()
        for c in self.to_core.values():
            c.wait_recv()

    def close(self):
        sent = (self.x_top, self.y_low, self.x_low, self.y_top, self.core, self.far_y, self.far_x)
        for c in (*sent, *self.to_core.values()):
            c.wait_send()

    def run(self):
        self.begin()
        self.relay()
        self.relay_far()
        self.arrive()
        self.close()


def norm_step(x, gain):
    return (x * lax.rsqrt(jnp.mean(x * x, axis=1, keepdims=True) + EPS_NORM)) * gain


def norm_back_step(grad, x, gain):
    inverse = lax.rsqrt(jnp.mean(x * x, axis=1, keepdims=True) + EPS_NORM)
    normed = x * inverse
    scaled = grad * gain
    dx = inverse * (scaled - normed * jnp.mean(scaled * normed, axis=1, keepdims=True))
    return dx, jnp.sum(grad * normed, axis=0, keepdims=True)


def by_columns(step, width=512):
    for c in range(D // width):
        step(pl.ds(c * width, width))


def forward_step(refs, res, gain, x_out):
    own, core, held, near, last, parts, _, sems = refs
    PlaneSum(parts, own, core, held, near, last, sems, 0, 1).run()
    x = res[...] + own[...]
    x_out[...] = x
    return norm_step(x, gain[...]).astype(BF16)


def attend_sum_kernel(o, wout, res, gain, x_out, out, *refs):
    *_, parts, mine, sems = refs
    greet(1)

    def make(c):
        parts[:, :, c] = mm(flat(o[...]), wout[:, c]).astype(BF16).reshape(8, -1, c.size)

    by_columns(make)
    mine[...] = forward_step(refs, res, gain, x_out)
    PlaneSpread(mine, out, sems, 7, 0, mine.shape[0]).run()


def units_sum_kernel(h2, wgate, wdown, res, gain, x_out, gate_up, hidden, out, *refs):
    *_, parts, _, _ = refs
    units = wdown.shape[0]
    greet(1)
    x = flat(h2[...])
    step = min(units, 512)
    for c in range(2 * units // step):
        at = pl.ds(c * step, step)
        gate_up[:, at] = mm(x, wgate[:, at])
    for c in range(units // step):
        at, up = pl.ds(c * step, step), pl.ds(units + c * step, step)
        gate = gate_up[:, at]
        hidden[:, at] = (gate / (1.0 + jnp.exp(-gate)) * gate_up[:, up]).astype(BF16)

    def make(c):
        parts[:, :, c] = mm(hidden[...], wdown[:, c]).astype(BF16).reshape(8, -1, c.size)

    by_columns(make)
    out[...] = forward_step(refs, res, gain, x_out)


def gate_sum_kernel(
    down_in, wdown, wgate, gate_up, x_in, gain, res, dx_out, dgain, dgate_up, out, *refs
):
    own, core, held, near, last, parts, mine, sems = refs
    units = wdown.shape[0]
    greet(1)
    x = flat(down_in[...])
    step = min(units, 512)
    for c in range(units // step):
        at, up = pl.ds(c * step, step), pl.ds(units + c * step, step)
        grad = mm(x, wdown[at, :], CONTRACT_LAST)
        gate, upward = gate_up[:, at], gate_up[:, up]
        sigma = 1.0 / (1.0 + jnp.exp(-gate))
        dgate = grad * upward * sigma * (1.0 + gate * (1.0 - sigma))
        dgate_up[:, at] = dgate.astype(BF16)
        dgate_up[:, up] = (grad * gate * sigma).astype(BF16)

    def make(c):
        value = mm(dgate_up[...], wgate[c, :], CONTRACT_LAST)
        parts[:, :, c] = value.astype(BF16).reshape(8, -1, c.size)

    by_columns(make)
    PlaneSum(parts, own, core, held, near, last, sems, 0, 1).run()
    dx, dg = norm_back_step(own[...], x_in[...], gain[...])
    dx = dx + res[...]
    dx_out[...] = dx
    dgain[...] = dg
    mine[...] = dx.astype(BF16)
    PlaneSpread(mine, out, sems, 7, 0, mine.shape[0]).run()


def head_kernel(n_dp, rows_ref, target_ref, scale_ref, *refs):
    head_ref, final_out, dlogits, seen, final, head, mine, logits, *refs = refs
    stats, plane, mid, line, sems, own_sems = refs
    rows, vocab = rows_ref.shape[0], logits.shape[2]
    wide = head.shape[2]
    load = pltpu.make_async_copy(head_ref, head, own_sems.at[0])
    store = pltpu.make_async_copy(final, final_out, own_sems.at[1])
    load.start()
    a = lax.axis_index("dp")
    greet(n_dp, range(1, 8))
    mine[pl.ds(0, rows)] = rows_ref[...]
    block = [pl.ds(o * rows, rows) for o in range(4)]
    across = [
        peer_copy(rows_ref, mine.at[block[1]], sems, 53, dp=a ^ 1),
        peer_copy(rows_ref, mine.at[block[2]], sems, 54, dp=a ^ 2),
        peer_copy(mine.at[block[2]], mine.at[block[3]], sems, 55, dp=a ^ 1),
    ]
    across[0].start()
    across[1].start()
    blocks = [PlaneSpread(mine, final, sems, 13 * o, o * rows, rows) for o in range(n_dp)]
    tile = 512 if vocab % 512 == 0 else vocab

    def use(b):
        part = pl.ds(b * rows, rows)

        @pl.loop(0, vocab // tile)
        def _(v):
            at = pl.ds(pl.multiple_of(v * tile, tile), tile)
            value = None
            for p in range(n_dp):
                x = flat(final[:, part, pl.ds(p * wide, wide)])
                term = mm(x, head[p, at, :], CONTRACT_LAST)
                value = term if value is None else value + term
            logits[:, part, at] = value.reshape(8, rows, tile)

        value = flat(logits[:, part, :])
        top = jnp.max(value, axis=1, keepdims=True)
        expo = jnp.sum(jnp.exp(value - top), axis=1, keepdims=True)
        column = lax.broadcasted_iota(jnp.int32, value.shape, 1)
        hit = jnp.sum(jnp.where(column == target_ref[b], value, 0.0), axis=1, keepdims=True)
        lane = lax.broadcasted_iota(jnp.int32, (8 * rows, 128), 1)
        packed = jnp.where(lane == 0, top, jnp.where(lane == 1, expo, hit)).T
        for k in range(3):
            stats[k, b : b + 1, :] = packed[k : k + 1]

    blocks[0].begin()
    across[0].wait_recv()
    blocks[1].begin()
    blocks[0].relay()
    across[1].wait_recv()
    across[2].start()
    blocks[2].begin()
    blocks[1].relay()
    blocks[0].relay_far()
    across[2].wait_recv()
    blocks[3].begin()
    blocks[2].relay()
    blocks[1].relay_far()
    blocks[0].arrive()
    load.wait()
    use(0)
    blocks[3].relay()
    blocks[2].relay_far()
    blocks[1].arrive()
    use(1)
    blocks[3].relay_far()
    blocks[2].arrive()
    use(2)
    blocks[3].arrive()
    store.start()
    use(3)
    stats_steps(n_dp, stats, seen, plane, mid, line, sems, 14 * n_dp)

    @pl.loop(0, n_dp)
    def _(b):
        part = pl.ds(pl.multiple_of(b * rows, rows), rows)
        lse = jnp.broadcast_to(seen[0, pl.ds(b, 1), :], (128, 8 * rows)).T[:, :1]
        value = flat(logits[:, part, :])
        column = lax.broadcasted_iota(jnp.int32, value.shape, 1)
        hit = (column == target_ref[b]).astype(F32)
        grad = (scale_ref[b] * (jnp.exp(value - lse) - hit)).astype(BF16)
        dlogits[:, part, :] = grad.reshape(8, rows, vocab)

    for copy in across:
        copy.wait_send()
    for each in blocks:
        each.close()
    store.wait()


def head_call(n_dp, rows, head, target, scale):
    total = n_dp * rows.shape[0]
    vocab = head.shape[1]
    stats = (3, n_dp, 8 * rows.shape[0])
    outs = [((8, total, D), BF16), ((8, total, vocab), BF16), ((2,) + stats[1:], F32)]
    anywhere = pl.BlockSpec(memory_space=pl.ANY)
    return pl.pallas_call(
        functools.partial(head_kernel, n_dp),
        out_shape=[jax.ShapeDtypeStruct(shape, dtype) for shape, dtype in outs],
        in_specs=[pl.BlockSpec(memory_space=pltpu.VMEM)] * 3 + [anywhere],
        out_specs=[anywhere] + [pl.BlockSpec(memory_space=pltpu.VMEM)] * 2,
        scratch_shapes=[
            pltpu.VMEM((8, total, D), BF16),
            pltpu.VMEM(head.shape, BF16),
            pltpu.VMEM((total, D), BF16),
            pltpu.VMEM((8, total, vocab), F32),
            pltpu.VMEM(stats, F32),
            pltpu.VMEM((7,) + stats, F32),
            pltpu.VMEM(stats, F32),
            pltpu.VMEM((n_dp - 1,) + stats, F32),
            pltpu.SemaphoreType.DMA((2, 14 * n_dp + 6 + n_dp)),
            pltpu.SemaphoreType.DMA((2,)),
        ],
        compiler_params=pltpu.CompilerParams(
            collective_id=5, has_side_effects=True, vmem_limit_bytes=56 << 20
        ),
        cost_estimate=pl.CostEstimate(flops=0, bytes_accessed=1 << 20, transcendentals=0),
        name="head",
    )(rows, target, scale, head)


def head_back_kernel(n_dp, cut, dlogits, head, x_in, gain, final_ref, *refs):
    dx_out, dgain, out, early, grads, own, core, held, near, last, parts, *refs = refs
    mine, sent, got, final, ready, sems, own_sem = refs
    a = lax.axis_index("dp")
    rows = x_in.shape[0]
    _, vocab, wide = head.shape
    load = pltpu.make_async_copy(final_ref, final, own_sem)
    load.start()
    greet(n_dp)
    plan = PlaneSum(parts, own, core, held, near, last, sems, 0, n_dp)

    def make(b):
        part = pl.ds(b * rows, rows)
        x = flat(dlogits[:, part, :])
        for p in range(n_dp):
            value = mm(x, head[p]).astype(BF16)
            parts[:, part, pl.ds(p * wide, wide)] = value.reshape(8, rows, wide)
        plan.at_core[b].start()

    def table_part(p, first, number):
        x = flat(final[:, :, pl.ds(pl.multiple_of(p * wide, 128), wide)])
        return mm(flat(dlogits[:, :, pl.ds(first, number)]), x, CONTRACT_FIRST).astype(BF16)

    left = [(p, v) for p in range(n_dp) for v in range(cut, vocab, 256)]

    def fill(count):
        for _ in range(min(count, len(left))):
            p, v = left.pop(0)
            grads[p, pl.ds(v - cut, 256), :] = table_part(p, v, 256)

    first_rows = [
        peer_copy(ready.at[o - 1], early.at[a], sems, 12 + 8 * n_dp + o, dp=a ^ o)
        for o in range(1, n_dp)
    ]
    across = {
        b: peer_copy(
            sent.at[pl.ds(b * rows, rows)], got.at[b - 1], sems, 13 + 7 * n_dp + b, dp=a ^ b
        )
        for b in range(1, n_dp)
    }

    def finish(b):
        plan.finish(b)
        if b:
            part = pl.ds(b * rows, rows)
            sent[part] = own[part].astype(BF16)
            across[b].start()

    make(2)
    load.wait()
    for o in range(1, n_dp):
        ready[o - 1] = table_part(a ^ o, 0, cut)
        first_rows[o - 1].start()
    plan.first_sends(2)
    make(3)
    plan.second_sends(2)
    plan.first_sends(3)
    make(1)
    early[a] = table_part(a, 0, cut)
    plan.first_sends(1)
    plan.second_sends(3)
    make(0)
    finish(2)
    plan.first_sends(0)
    fill(2)
    plan.second_sends(1)
    finish(3)
    fill(6)
    plan.second_sends(0)
    finish(1)
    fill(7)
    finish(0)
    fill(len(left))
    for copy in first_rows:
        copy.wait()
    for copy in across.values():
        copy.wait()
    grad = own[pl.ds(0, rows)]
    for o in range(1, n_dp):
        grad = grad + got[o - 1].astype(F32)
    dx, dg = norm_back_step(grad, x_in[...], gain[...])
    dx_out[...] = dx
    dgain[...] = dg
    mine[...] = dx.astype(BF16)
    PlaneSpread(mine, out, sems, 7 * n_dp, 0, rows).run()
    plan.close()


def input_back_kernel(dqkv, wqkv, h1, x_in, gain, res, dx_out, dgain, grads, *refs):
    own, core, held, near, last, parts, _, sems = refs
    rows = res.shape[0]
    blocks = x_in.shape[0] // rows
    greet(1)
    plan = PlaneSum(parts, own, core, held, near, last, sems, 0, blocks)

    def make(b):
        part = pl.ds(b * rows, rows)
        x = flat(dqkv[:, part, :])
        for c in range(D // 512):
            value = mm(x, wqkv[pl.ds(c * 512, 512), :], CONTRACT_LAST).astype(BF16)
            parts[:, part, pl.ds(c * 512, 512)] = value.reshape(8, rows, 512)
        plan.at_core[b].start()

    left = list(range(D // 512))

    def fill():
        c = pl.ds(left.pop(0) * 512, 512)
        grads[c, :] = mm(flat(h1[:, :, c]), flat(dqkv[...]), CONTRACT_FIRST).astype(BF16)

    def close(b):
        plan.finish(b)
        part = pl.ds(b * rows, rows)
        dx, dg = norm_back_step(own[part], x_in[part], gain[...])
        if b == 0:
            dx = dx + res[...]
            dgain[...] = dg
        else:
            dgain[...] += dg
        dx_out[part] = dx.astype(BF16)

    make(0)
    make(1)
    plan.first_sends(0)
    make(2)
    plan.first_sends(1)
    plan.second_sends(0)
    make(3)
    plan.first_sends(2)
    plan.second_sends(1)
    plan.first_sends(3)
    fill()
    close(0)
    plan.second_sends(2)
    fill()
    close(1)
    plan.second_sends(3)
    fill()
    close(2)
    fill()
    close(3)
    plan.close()


def exchange(kernel, name, number, n_dp, total, outs, *args, more=(), sems=20, far=0):
    half = total // 2
    rows = outs[0][0][0]
    scratch = [
        pltpu.VMEM((total, D), F32),
        pltpu.VMEM((4, total, D), BF16),
        pltpu.VMEM((4, total, D), BF16),
        pltpu.VMEM((4, half, D), BF16),
        pltpu.VMEM((2, half, D), BF16),
        pltpu.VMEM((8, total, D), BF16),
        pltpu.VMEM((rows, D), BF16),
    ]
    scratch += [pltpu.VMEM(shape, BF16) for shape in more]
    return pl.pallas_call(
        kernel,
        out_shape=[jax.ShapeDtypeStruct(shape, dtype) for shape, dtype in outs],
        in_specs=[pl.BlockSpec(memory_space=pltpu.VMEM)] * (len(args) - far)
        + [pl.BlockSpec(memory_space=pl.ANY)] * far,
        out_specs=[pl.BlockSpec(memory_space=pltpu.VMEM)] * len(outs),
        scratch_shapes=scratch
        + [pltpu.SemaphoreType.DMA((2, sems))]
        + [pltpu.SemaphoreType.DMA] * far,
        compiler_params=pltpu.CompilerParams(
            collective_id=number, has_side_effects=True, vmem_limit_bytes=62 << 20
        ),
        cost_estimate=pl.CostEstimate(flops=0, bytes_accessed=1 << 10, transcendentals=0),
        name=name,
    )(*args)


def stats_steps(n_dp, x_ref, out_ref, plane, mid, line, sems, first):
    me = lax.axis_index("mp")
    a = lax.axis_index("dp")
    order = cube_order(8)
    rows = x_ref.shape[2] // 8
    copies = [
        peer_copy(x_ref, plane.at[s - 1], sems, first + s - 1, mp=me ^ order[s])
        for s in range(1, 8)
    ]
    for copy in copies:
        copy.start()

    def join(have, new):
        top = jnp.maximum(have[0], new[0])
        total = have[1] * jnp.exp(have[0] - top) + new[1] * jnp.exp(new[0] - top)
        return top, total, have[2] + new[2]

    have = tuple(x_ref[k] for k in range(3))
    for s in range(1, 8):
        copies[s - 1].wait_recv()
        got = [plane[s - 1, k] for k in range(3)]
        got = [
            jnp.concatenate([v[:, (e ^ s) * rows : (e ^ s) * rows + rows] for e in range(8)], axis=1)
            for v in got
        ]
        have = join(have, got)
    for k in range(3):
        mid[k] = have[k]
    across = [
        peer_copy(mid, line.at[o - 1], sems, first + 6 + o, dp=a ^ o) for o in range(1, n_dp)
    ]
    for copy in across:
        copy.start()
    for o in range(1, n_dp):
        across[o - 1].wait_recv()
        got = [line[o - 1, k] for k in range(3)]
        got = [jnp.concatenate([v[e ^ o : (e ^ o) + 1] for e in range(n_dp)], axis=0) for v in got]
        have = join(have, got)
    out_ref[0] = have[0] + jnp.log(have[1])
    out_ref[1] = have[2]
    for copy in copies + across:
        copy.wait_send()


def total_kernel(n_dp, slots_ref, more_ref, out_ref, plane, line, sems):
    me = lax.axis_index("mp")
    a = lax.axis_index("dp")
    greet(n_dp, range(1, 8))

    def add(k, have):
        g = slots_ref[pl.ds(k * 8, 8)].astype(F32)
        return have + jnp.sum((g * g).reshape(-1, 8, 128), axis=0)

    start = jnp.zeros((8, 128), F32)
    plane[me, 0] = lax.fori_loop(0, slots_ref.shape[0] // 8, add, start) + more_ref[0]
    plane[me, 1] = more_ref[1]
    copies = [peer_copy(plane.at[me], plane.at[me], sems, k - 1, mp=me ^ k) for k in range(1, 8)]
    for copy in copies:
        copy.start()
    for copy in copies:
        copy.wait()
    line[a] = jnp.sum(plane[...], axis=0)
    across = [
        peer_copy(line.at[a], line.at[a], sems, 6 + o, dp=a ^ o)
        for o in range(1, n_dp)
    ]
    for copy in across:
        copy.start()
    for copy in across:
        copy.wait()
    out_ref[...] = jnp.sum(line[...], axis=0)


def total_exchange(slots, more, n_dp):
    return pl.pallas_call(
        functools.partial(total_kernel, n_dp),
        out_shape=jax.ShapeDtypeStruct(more.shape, F32),
        in_specs=[pl.BlockSpec(memory_space=pltpu.VMEM)] * 2,
        out_specs=pl.BlockSpec(memory_space=pltpu.VMEM),
        scratch_shapes=[
            pltpu.VMEM((8,) + more.shape, F32),
            pltpu.VMEM((n_dp,) + more.shape, F32),
            pltpu.SemaphoreType.DMA((2, 6 + n_dp)),
        ],
        compiler_params=pltpu.CompilerParams(collective_id=6, has_side_effects=True),
        name="total",
    )(slots, more)


def mat_shapes(n_mp):
    width, units = D // n_mp, FF // n_mp
    return ((D, 3 * width), (width, D), (D, 2 * units), (units, D))


def each_tile(shape, size, first, step):
    rows, cols = shape

    @pl.loop(0, rows // size)
    def _(r):
        row = pl.ds(pl.multiple_of(r * size, size), size)
        for c in range(cols // size):
            step(first + r * (cols // size) + c, (row, pl.ds(c * size, size)))


def first_tiles(shapes, size):
    firsts = [0]
    for rows, cols in shapes:
        firsts.append(firsts[-1] + rows * cols // (size * size))
    return firsts


def place_kernel(shapes, slot_ref, slots_ref, *refs):
    count = len(shapes)
    outs, mats, sems = refs[:count], refs[count : 2 * count], refs[-1]
    size = slots_ref.shape[1]
    for k, (shape, first) in enumerate(zip(shapes, first_tiles(shapes, size))):

        def fetch(tile, view, k=k):
            pltpu.make_async_copy(
                slots_ref.at[slot_ref[tile]], mats[k].at[view], sems.at[0, k]
            ).start()

        each_tile(shape, size, first, fetch)
    for k in range(count):
        pltpu.make_async_copy(mats[k], mats[k], sems.at[0, k]).wait()
        pltpu.make_async_copy(mats[k], outs[k], sems.at[1, k]).start()
    for k in range(count):
        pltpu.make_async_copy(mats[k], outs[k], sems.at[1, k]).wait()


def place_tiles(slot_of, slots, shapes):
    anywhere = pl.BlockSpec(memory_space=pl.ANY)
    return pl.pallas_call(
        functools.partial(place_kernel, shapes),
        out_shape=[jax.ShapeDtypeStruct(shape, slots.dtype) for shape in shapes],
        in_specs=[pl.BlockSpec(memory_space=pltpu.SMEM), anywhere],
        out_specs=[anywhere] * len(shapes),
        scratch_shapes=[pltpu.VMEM(shape, slots.dtype) for shape in shapes]
        + [pltpu.SemaphoreType.DMA((2, len(shapes)))],
        compiler_params=pltpu.CompilerParams(vmem_limit_bytes=40 << 20),
        cost_estimate=pl.CostEstimate(flops=0, bytes_accessed=1 << 20, transcendentals=0),
        name="place_tiles",
    )(slot_of, slots)


def collect_kernel(shapes, chosen, slot_ref, *refs):
    mats = refs[: len(chosen)]
    slots_ref, sem = refs[-2:]
    size = slots_ref.shape[1]
    firsts = first_tiles(shapes, size)
    for k, ref in zip(chosen, mats):

        def send(tile, view, ref=ref):
            pltpu.make_async_copy(ref.at[view], slots_ref.at[slot_ref[tile]], sem).start()

        each_tile(shapes[k], size, firsts[k], send)
    for ref in mats:
        pltpu.make_async_copy(ref, ref, sem).wait()


def collect_tiles(slot_of, mats, shapes, chosen, given=()):
    size = 128
    anywhere = pl.BlockSpec(memory_space=pl.ANY)
    return pl.pallas_call(
        functools.partial(collect_kernel, shapes, chosen),
        out_shape=jax.ShapeDtypeStruct((slot_of.shape[0], size, size), BF16),
        in_specs=[pl.BlockSpec(memory_space=pltpu.SMEM)]
        + [pl.BlockSpec(memory_space=pltpu.VMEM)] * len(mats)
        + [anywhere] * len(given),
        out_specs=anywhere,
        scratch_shapes=[pltpu.SemaphoreType.DMA],
        compiler_params=pltpu.CompilerParams(vmem_limit_bytes=40 << 20),
        input_output_aliases={1 + len(mats): 0} if given else {},
        cost_estimate=pl.CostEstimate(flops=0, bytes_accessed=1 << 20, transcendentals=0),
        name="collect_tiles",
    )(slot_of, *mats, *given)


def after(x, *others):
    anywhere = pl.BlockSpec(memory_space=pl.ANY)
    return pl.pallas_call(
        lambda *refs: None,
        out_shape=jax.ShapeDtypeStruct(x.shape, x.dtype),
        in_specs=[anywhere] * (1 + len(others)),
        out_specs=anywhere,
        input_output_aliases={0: 0},
        cost_estimate=pl.CostEstimate(flops=0, bytes_accessed=0, transcendentals=0),
        name="after",
    )(x, *others)


def split(x):
    high = x.astype(BF16)
    return high, (x - high.astype(F32)).astype(BF16)


def adam(master, moment, second, grad, rate, decay):
    moment_new = ADAM_ONE * moment + (1.0 - ADAM_ONE) * grad
    second_new = ADAM_TWO * second + (1.0 - ADAM_TWO) * grad * grad
    corrected = (
        moment_new
        / (1.0 - ADAM_ONE**STEP)
        / (jnp.sqrt(second_new / (1.0 - ADAM_TWO**STEP)) + ADAM_EPS)
    )
    return (master - rate * (corrected + decay * master), moment_new, second_new)


def owner_step_kernel(steps, factor_ref, *refs):
    g_ref, master, left, right, l_root, r_root = refs[:6]
    t_grad, t_master, t_moment, t_second = refs[6:10]
    new, copy, grad, left_new, right_new = refs[10:15]
    t_new, t_copy, t_moment_new, t_second_new = refs[15:]
    factor = factor_ref[0, 0]

    @pl.when(pl.program_id(0) < steps)
    def _():
        for k in range(g_ref.shape[0]):
            g = g_ref[k]
            grad[k] = factor * g.astype(F32)
            outer = (mm(g, g, CONTRACT_LAST) * factor) * factor
            inner = (mm(g, g, CONTRACT_FIRST) * factor) * factor
            left_new[k] = STAT_DECAY * left[k] + (1.0 - STAT_DECAY) * outer
            right_new[k] = STAT_DECAY * right[k] + (1.0 - STAT_DECAY) * inner
            l_high, l_low = split(l_root[k])
            r_high, r_low = split(r_root[k])
            t_high, t_low = split((mm(l_high, g) + mm(l_low, g)) * factor)
            direction = mm(t_high, r_high) + (mm(t_low, r_high) + mm(t_high, r_low))
            value = master[k] - LR_MATRIX * (direction + DECAY_MATRIX * master[k])
            new[k] = value
            copy[k] = value.astype(BF16)

    @pl.when(pl.program_id(0) >= steps)
    def _():
        value, moment, second = adam(
            t_master[...],
            t_moment[...],
            t_second[...],
            factor * t_grad[...],
            LR_TABLE,
            DECAY_TABLE,
        )
        t_new[...] = value
        t_copy[...] = value.astype(BF16)
        t_moment_new[...] = moment
        t_second_new[...] = second


def owner_step(factor, tiles, table):
    number, size, _ = tiles[0].shape
    rows, cols = table[0].shape
    group, band = 16, 512
    steps = number // group

    tile = pl.BlockSpec((group, size, size), lambda i: (jnp.minimum(i, steps - 1), 0, 0))
    part = pl.BlockSpec((band, cols), lambda i: (jnp.maximum(i - steps, 0), 0))
    kinds = (F32, BF16, F32, F32, F32)
    out_shape = [jax.ShapeDtypeStruct((number, size, size), kind) for kind in kinds]
    out_shape += [jax.ShapeDtypeStruct((rows, cols), kind) for kind in kinds[:4]]
    return pl.pallas_call(
        functools.partial(owner_step_kernel, steps),
        grid=(steps + rows // band,),
        out_shape=out_shape,
        in_specs=[pl.BlockSpec(memory_space=pltpu.SMEM)] + [tile] * 6 + [part] * 4,
        out_specs=[tile] * 5 + [part] * 4,
        compiler_params=pltpu.CompilerParams(vmem_limit_bytes=56 << 20),
        name="owner_step",
    )(factor, *tiles, *table)


CONTRACT_LAST = (((1,), (1,)), ((), ()))
CONTRACT_FIRST = (((0,), (0,)), ((), ()))


def mm(a, b, dims=(((1,), (0,)), ((), ()))):
    return lax.dot_general(a, b, dims, preferred_element_type=F32)


def turn(x, cosine, sine):
    lane = lax.broadcasted_iota(jnp.int32, x.shape, 1)
    other = jnp.where(
        lax.rem(lane, HD) < HD // 2, pltpu.roll(x, 128 - HD // 2, 1), pltpu.roll(x, HD // 2, 1)
    )
    return x * cosine + other * sine


def flat(x):
    return x.reshape(x.shape[0] * x.shape[1], x.shape[2])


def head_probs(q, k_ctx, k_ans, causal):
    s_ctx = mm(q, k_ctx, CONTRACT_LAST) * HD ** (-0.5)
    s_ans = jnp.where(causal, mm(q, k_ans, CONTRACT_LAST) * HD ** (-0.5), MASKED)
    top = jnp.maximum(
        jnp.max(s_ctx, axis=1, keepdims=True), jnp.max(s_ans, axis=1, keepdims=True)
    )
    e_ctx = jnp.exp(s_ctx - top)
    e_ans = jnp.exp(s_ans - top)
    total = jnp.sum(e_ctx, axis=1, keepdims=True) + jnp.sum(e_ans, axis=1, keepdims=True)
    return e_ctx / total, e_ans / total


def attend_kernel(items, h1_ref, w_ref, cos_ref, sin_ref, col_ref, row_ref, *outs):
    o_ref, qo_ref, ko_ref, vo_ref, qkv_ref = outs

    @pl.loop(0, h1_ref.shape[0])
    def _(s):
        qkv_ref[s] = mm(h1_ref[s], w_ref[...])

    n, rows_ans, width = o_ref.shape
    n_ans = rows_ans // items
    n_ctx = qkv_ref.shape[1] // items - n_ans
    causal = col_ref[...] >= row_ref[...]
    lane = lax.broadcasted_iota(jnp.int32, (1, 128), 1)

    for item in range(items):
        ans = pl.ds(item * n_ans, n_ans)
        ctx = pl.ds(rows_ans + item * n_ctx, n_ctx)
        turns = [(flat(cos_ref[:, r]), flat(sin_ref[:, r])) for r in (ans, ctx)]
        for g in range(width // 128):
            lanes = pl.ds(g * 128, 128)
            klanes = pl.ds(width + g * 128, 128)
            vlanes = pl.ds(2 * width + g * 128, 128)
            q = turn(flat(qkv_ref[:, ans, lanes]), *turns[0]).astype(BF16)
            k_ans = turn(flat(qkv_ref[:, ans, klanes]), *turns[0]).astype(BF16)
            k_ctx = turn(flat(qkv_ref[:, ctx, klanes]), *turns[1]).astype(BF16)
            v_ans = flat(qkv_ref[:, ans, vlanes]).astype(BF16)
            v_ctx = flat(qkv_ref[:, ctx, vlanes]).astype(BF16)
            qo_ref[:, ans, lanes] = q.reshape(n, n_ans, 128)
            ko_ref[:, ans, lanes] = k_ans.reshape(n, n_ans, 128)
            ko_ref[:, ctx, lanes] = k_ctx.reshape(n, n_ctx, 128)
            vo_ref[:, ans, lanes] = v_ans.reshape(n, n_ans, 128)
            vo_ref[:, ctx, lanes] = v_ctx.reshape(n, n_ctx, 128)
            got = []
            for first in (True, False):
                own = (lane < HD) == first
                p_ctx, p_ans = head_probs(jnp.where(own, q, 0), k_ctx, k_ans, causal)
                got.append(mm(p_ctx.astype(BF16), v_ctx) + mm(p_ans.astype(BF16), v_ans))
            o = jnp.where(lane < HD, got[0], got[1]).astype(BF16)
            o_ref[:, ans, lanes] = o.reshape(n, n_ans, 128)


def attend_back_kernel(items, *refs):
    q_ref, k_ref, v_ref, dx_ref, w_ref, cos_ref, sin_ref, col_ref, row_ref, d_ref, do_ref = refs
    n, rows_ans, width = q_ref.shape
    do_ref[...] = mm(flat(dx_ref[...]), w_ref[...], CONTRACT_LAST).astype(BF16).reshape(q_ref.shape)
    n_ans = rows_ans // items
    n_ctx = k_ref.shape[1] // items - n_ans
    causal = col_ref[...] >= row_ref[...]
    lane = lax.broadcasted_iota(jnp.int32, (1, 128), 1)
    root = HD ** (-0.5)

    for item in range(items):
        ans = pl.ds(item * n_ans, n_ans)
        ctx = pl.ds(rows_ans + item * n_ctx, n_ctx)
        turns = [(flat(cos_ref[:, r]), -flat(sin_ref[:, r])) for r in (ans, ctx)]
        d_ref[:, ctx, pl.ds(0, width)] = jnp.zeros((n, n_ctx, width), BF16)
        for g in range(width // 128):
            lanes = pl.ds(g * 128, 128)
            klanes = pl.ds(width + g * 128, 128)
            vlanes = pl.ds(2 * width + g * 128, 128)
            q, do = flat(q_ref[:, ans, lanes]), flat(do_ref[:, ans, lanes])
            k_ans, k_ctx = flat(k_ref[:, ans, lanes]), flat(k_ref[:, ctx, lanes])
            v_ans, v_ctx = flat(v_ref[:, ans, lanes]), flat(v_ref[:, ctx, lanes])
            dq, sums = [], None
            for first in (True, False):
                own = (lane < HD) == first
                q_own, do_own = jnp.where(own, q, 0), jnp.where(own, do, 0)
                p_ctx, p_ans = head_probs(q_own, k_ctx, k_ans, causal)
                dp_ctx = mm(do_own, v_ctx, CONTRACT_LAST)
                dp_ans = mm(do_own, v_ans, CONTRACT_LAST)
                mean = jnp.sum(p_ctx * dp_ctx, axis=1, keepdims=True) + jnp.sum(
                    p_ans * dp_ans, axis=1, keepdims=True
                )
                ds_ctx = (p_ctx * (dp_ctx - mean)).astype(BF16)
                ds_ans = (p_ans * (dp_ans - mean)).astype(BF16)
                dq.append(mm(ds_ctx, k_ctx) + mm(ds_ans, k_ans))
                new = [
                    mm(ds_ctx, q_own, CONTRACT_FIRST),
                    mm(ds_ans, q_own, CONTRACT_FIRST),
                    mm(p_ctx.astype(BF16), do_own, CONTRACT_FIRST),
                    mm(p_ans.astype(BF16), do_own, CONTRACT_FIRST),
                ]
                sums = new if sums is None else [a + b for a, b in zip(sums, new)]
            dq = turn(jnp.where(lane < HD, dq[0], dq[1]) * root, *turns[0])
            dk_ctx = turn(sums[0] * root, *turns[1])
            dk_ans = turn(sums[1] * root, *turns[0])
            d_ref[:, ans, lanes] = dq.astype(BF16).reshape(n, n_ans, 128)
            d_ref[:, ans, klanes] = dk_ans.astype(BF16).reshape(n, n_ans, 128)
            d_ref[:, ctx, klanes] = dk_ctx.astype(BF16).reshape(n, n_ctx, 128)
            d_ref[:, ans, vlanes] = sums[3].astype(BF16).reshape(n, n_ans, 128)
            d_ref[:, ctx, vlanes] = sums[2].astype(BF16).reshape(n, n_ctx, 128)


def in_vmem(kernel, name, outs, scratch, *args):
    return pl.pallas_call(
        kernel,
        out_shape=[jax.ShapeDtypeStruct(shape, dtype) for shape, dtype in outs],
        in_specs=[pl.BlockSpec(memory_space=pltpu.VMEM)] * len(args),
        out_specs=[pl.BlockSpec(memory_space=pltpu.VMEM)] * len(outs),
        scratch_shapes=[pltpu.VMEM(shape, dtype) for shape, dtype in scratch],
        compiler_params=pltpu.CompilerParams(vmem_limit_bytes=48 << 20),
        cost_estimate=pl.CostEstimate(flops=0, bytes_accessed=1 << 10, transcendentals=0),
        name=name,
    )(*args)


def norm_forward(x):
    inverse = lax.rsqrt(jnp.mean(x * x, axis=-1, keepdims=True) + EPS_NORM)
    return (x * inverse, inverse)


def norm_backward(grad, normed, inverse, gain):
    scaled = grad * gain
    dgain = jnp.sum(grad * normed, axis=0)
    dx = inverse * (scaled - normed * jnp.mean(scaled * normed, axis=-1, keepdims=True))
    return (dx, dgain)


def body(
    tokens,
    targets,
    pair_order,
    lengths,
    loss_mask,
    start_pos,
    owner_map,
    block_master,
    left_stat,
    right_stat,
    left_root,
    right_root,
    table_master,
    table_moment,
    table_second,
    gain_master,
    gain_moment,
    gain_second,
):
    dp = lax.axis_index("dp")
    mp = lax.axis_index("mp")
    n_mp = lax.axis_size("mp")
    n_dp = lax.axis_size("dp")
    fused = (n_mp, n_dp) == (8, 4)
    items, length = tokens.shape
    context = length - ANS
    n_ans = ANS // n_mp
    n_ctx = context // n_mp
    rows_ans = items * n_ans
    rows_own = items * (n_ans + n_ctx)
    width = D // n_mp
    units = FF // n_mp
    heads = width // HD
    vocab_part, cols = table_master.shape
    sub = vocab_part // n_dp
    perm = owner_map[0]
    who = mp ^ jnp.array(cube_order(n_mp), jnp.int32)
    near = dp ^ jnp.arange(n_dp, dtype=jnp.int32)

    slots = lax.all_gather(block_master[0].astype(BF16), "dp", axis=0, tiled=True)
    gains = line_gather(gain_master.astype(BF16))
    wide = jnp.zeros((3, D), BF16)
    for o in range(n_dp):
        wide = lax.dynamic_update_slice(wide, gains[o], (0, near[o] * cols))
    gains = wide.astype(F32)
    table_low = table_master.astype(BF16)

    packed = jnp.concatenate([tokens, targets, loss_mask, lengths[:, None]], axis=1)
    packed = jnp.stack(line_gather(packed))
    all_tokens = packed[:, :, :length]
    all_targets = packed[:, :, length : length + ANS]
    all_mask = packed[:, :, length + ANS : length + 2 * ANS]
    all_lengths = packed[:, :, -1]
    column = jnp.arange(ANS)
    weights = jnp.where(
        column == 0,
        1.0,
        jnp.where(column < all_lengths[..., None], all_mask.astype(F32), 0.0),
    )
    pairs_all = pair_order.shape[0] // 2
    pairs = (pair_order // 2).reshape(n_dp, items)[near]
    member = (pairs[..., None] == jnp.arange(pairs_all)).astype(F32)
    counts = jnp.einsum("oip,oi->p", member, jnp.sum(weights, axis=-1))
    scale = weights / (jnp.sum(member * counts, axis=-1)[..., None] * pairs_all)

    def by_owner(x):
        split = x.reshape(n_dp, items, n_mp, n_ans)[:, :, who]
        return split.transpose(2, 0, 1, 3)

    row_scale = by_owner(scale).reshape(-1)
    row_target = by_owner(all_targets).reshape(-1)
    tok_ans = all_tokens[:, :, context:].reshape(n_dp, items, n_mp, n_ans)[:, :, who]
    tok_ctx = all_tokens[:, :, :context].reshape(n_dp, items, n_mp, n_ctx)[:, :, who]
    tok = jnp.concatenate(
        [
            tok_ans.transpose(2, 0, 1, 3).reshape(n_mp, n_dp, -1),
            tok_ctx.transpose(2, 0, 1, 3).reshape(n_mp, n_dp, -1),
        ],
        axis=2,
    )

    shapes = mat_shapes(n_mp)
    number = perm.shape[0]
    slot_of = jnp.zeros_like(perm).at[perm].set(jnp.arange(number, dtype=jnp.int32))

    local = tok - mp * vocab_part
    valid = (local >= 0) & (local < vocab_part)
    safe = jnp.clip(local, 0, vocab_part - 1)
    looked = jnp.where(valid[..., None], jnp.take(table_low, safe, axis=0), 0)
    own_cols = cube_scatter(looked).astype(BF16)
    pieces = line_exchange([own_cols[o] for o in range(n_dp)])
    x0 = jnp.zeros((rows_own, D), BF16)
    for o in range(n_dp):
        x0 = lax.dynamic_update_slice(x0, pieces[o], (0, near[o] * cols))
    x0 = x0.astype(F32)
    normed1, inverse1 = norm_forward(x0)
    h1 = cube_gather((normed1 * gains[0]).astype(BF16))
    h1_all = h1.reshape(-1, D)

    wqkv, wout, wgate, wdown = place_tiles(slot_of, slots, shapes)

    table_late = after(table_low, slots, h1)
    head_parts = lax.all_to_all(table_late.reshape(n_dp, sub, cols), "dp", 0, 0)

    half = HD // 2
    freq = ROPE_BASE ** (-jnp.arange(half).astype(F32) * 2.0 / HD)
    t_ans = context + who[:, None] * n_ans + jnp.arange(n_ans)
    t_ctx = who[:, None] * n_ctx + jnp.arange(n_ctx)

    def angles(t):
        place = (start_pos[None, :, None] + t[:, None, :]).astype(F32)
        angle = place.reshape(n_mp, -1)[..., None] * freq
        return jnp.cos(angle), jnp.sin(angle)

    cosine, sine = (jnp.concatenate(pair, axis=1) for pair in zip(angles(t_ans), angles(t_ctx)))
    cosine = jnp.concatenate([cosine] * 4, axis=-1)
    sine = jnp.concatenate([-sine, sine] * 2, axis=-1)
    t_query = t_ans.reshape(-1)
    place = (t_query[:, None], t_query[None, :])

    ans_shape = ((n_mp, rows_ans, width), BF16)
    key_shape = ((n_mp, rows_own, width), BF16)
    o_rows, query, key, value = in_vmem(
        functools.partial(attend_kernel, items),
        "attend",
        (ans_shape, ans_shape, key_shape, key_shape),
        (((n_mp, rows_own, 3 * width), F32),),
        *(h1, wqkv, cosine, sine, *place),
    )
    own = ((rows_ans, D), F32)
    gain_row = ((1, D), F32)
    plane = ((n_mp, rows_ans, D), BF16)
    if fused:
        x1, h2 = exchange(
            attend_sum_kernel, "attend_sum", 1, n_dp, rows_ans, (own, plane),
            *(o_rows, wout, x0[:rows_ans], gains[1:2]),
        )
    else:
        parts = dot("tw,wd->td", o_rows.reshape(-1, width), wout).astype(BF16)
        x1 = x0[:rows_ans] + cube_scatter(parts.reshape(n_mp, rows_ans, D))
        h2 = cube_gather((norm_forward(x1)[0] * gains[1]).astype(BF16))
    o_rows = o_rows.reshape(-1, width)

    if fused:
        flat_units = n_mp * rows_ans
        x2, gate_up, hidden, final = exchange(
            units_sum_kernel, "units_sum", 2, n_dp, rows_ans,
            (
                own,
                ((flat_units, 2 * units), F32),
                ((flat_units, units), BF16),
                ((rows_ans, D), BF16),
            ),
            *(h2, wgate, wdown, x1, gains[2:3]),
        )
        h2 = h2.reshape(-1, D)
    else:
        h2 = h2.reshape(-1, D)
        gate_up = dot("td,df->tf", h2, wgate)
        gate, upward = gate_up[:, :units], gate_up[:, units:]
        hidden = (jax.nn.silu(gate) * upward).astype(BF16)
        parts = dot("tf,fd->td", hidden, wdown).astype(BF16)
        x2 = x1 + cube_scatter(parts.reshape(n_mp, rows_ans, D))

    def by_line(x):
        return x.reshape(n_mp, n_dp, rows_ans).transpose(1, 0, 2).reshape(n_dp, -1, 1)

    first = mp * vocab_part + dp * sub
    if fused:
        final, dlogits, seen = head_call(
            n_dp, final, head_parts, by_line(row_target - first), by_line(row_scale)
        )
        lse, picked = seen[0, 0], seen[1, 0]
        dlogits = dlogits.reshape(-1, sub)
        final = final.reshape(-1, D)
    else:
        head = jnp.concatenate([head_parts[a] for a in range(n_dp)], axis=1)
        final = (norm_forward(x2)[0] * gains[2]).astype(BF16)
        final = cube_gather(jnp.stack(line_gather(final)).reshape(-1, D))
        final = final.reshape(-1, D)
        logits = dot("rd,vd->rv", final, head)
        hit = jnp.arange(sub, dtype=jnp.int32)[None, :] == (row_target - first)[:, None]
        top = jnp.max(logits, axis=1)
        total = jnp.sum(jnp.exp(logits - top[:, None]), axis=1)
        picked = jnp.sum(jnp.where(hit, logits, 0.0), axis=1)
        top, total, picked = stats_everywhere(jnp.stack([top, total, picked]), rows_ans)
        lse = top + jnp.log(total)
        dlogits = (
            row_scale[:, None] * (jnp.exp(logits - lse[:, None]) - hit.astype(F32))
        ).astype(BF16)
    loss_own = jnp.sum(row_scale[:rows_ans] * (lse - picked)[:rows_ans]) * pairs_all

    if fused:
        cut = 256
        total = n_dp * rows_ans
        dx2, dgain3, down_in, early_grad, head_grad = exchange(
            functools.partial(head_back_kernel, n_dp, cut), "head_sum", 3, n_dp, total,
            (
                own,
                gain_row,
                plane,
                ((n_dp, cut, cols), BF16),
                ((n_dp, sub - cut, cols), BF16),
            ),
            *(dlogits.reshape(n_mp, -1, sub), head_parts, x2, gains[2:3]),
            final.reshape(n_mp, -1, D),
            more=(
                (total, D),
                (n_dp - 1, rows_ans, D),
                (n_mp, total, D),
                (n_dp - 1, cut, cols),
            ),
            sems=13 + 9 * n_dp,
            far=1,
        )
        dgain3 = dgain3[0]
    else:
        parts = dot("rv,vd->rd", dlogits, head).astype(BF16)
        mine = cube_scatter(parts.reshape(n_mp, n_dp * rows_ans, D)).astype(BF16)
        mine = line_exchange(list(mine.reshape(n_dp, rows_ans, D)))
        dfinal = sum(piece.astype(F32) for piece in mine)
        dx2, dgain3 = norm_backward(dfinal, *norm_forward(x2), gains[2])
        down_in = cube_gather(dx2.astype(BF16))
        head_grad = jnp.stack(
            [
                dot("rv,rd->vd", dlogits, final[:, a * cols : (a + 1) * cols]).astype(BF16)
                for a in range(n_dp)
            ]
        )
    table_grad = lax.all_to_all(head_grad, "dp", 0, 0)
    if fused:
        dx1, dgain2, dgate_up, out_in = exchange(
            gate_sum_kernel, "gate_sum", 4, n_dp, rows_ans,
            (own, gain_row, (gate_up.shape, BF16), plane),
            *(down_in, wdown, wgate, gate_up, x1, gains[1:2], dx2),
        )
        dgain2 = dgain2[0]
        down_in = down_in.reshape(-1, D)
    else:
        down_in = down_in.reshape(-1, D)
        dhidden = dot("td,fd->tf", down_in, wdown)
        sigma = jax.nn.sigmoid(gate)
        dgate = dhidden * upward * sigma * (1.0 + gate * (1.0 - sigma))
        dgate_up = jnp.concatenate([dgate, dhidden * gate * sigma], axis=-1).astype(BF16)
        parts = dot("tf,df->td", dgate_up, wgate).astype(BF16)
        dnormed2 = cube_scatter(parts.reshape(n_mp, rows_ans, D))
        dx_mlp, dgain2 = norm_backward(dnormed2, *norm_forward(x1), gains[1])
        dx1 = dx2 + dx_mlp
        out_in = cube_gather(dx1.astype(BF16))
    grad_down = dot("tf,td->fd", hidden, down_in).astype(BF16)
    grad_gate = dot("td,tf->df", h2, dgate_up).astype(BF16)
    grad_out = dot("tw,td->wd", o_rows, out_in.reshape(-1, D)).astype(BF16)
    (dqkv,) = in_vmem(
        functools.partial(attend_back_kernel, items),
        "attend_back",
        (((n_mp, rows_own, 3 * width), BF16),),
        (ans_shape,),
        *(query, key, value, out_in, wout, cosine, sine, *place),
    )
    dqkv = dqkv.reshape(-1, 3 * width)
    if fused:
        dx0, dgain1, grad_qkv = exchange(
            input_back_kernel, "input_sum", 7, n_dp, rows_own,
            (((rows_own, D), BF16), gain_row, (wqkv.shape, BF16)),
            *(dqkv.reshape(n_mp, rows_own, -1), wqkv, h1, x0, gains[:1], dx1),
            sems=7 * (rows_own // rows_ans),
        )
        dgain1 = dgain1[0]
    else:
        dh1 = dot("te,de->td", dqkv, wqkv).astype(BF16).reshape(n_mp, rows_own, D)
        grad_qkv = dot("td,te->de", h1_all, dqkv).astype(BF16)
        dx0, dgain1 = norm_backward(cube_scatter(dh1), *norm_forward(x0), gains[0])
        dx0 = jnp.concatenate([dx0[:rows_ans] + dx1, dx0[rows_ans:]]).astype(BF16)

    rows_over = line_exchange(
        [lax.dynamic_slice_in_dim(dx0, near[o] * cols, cols, 1) for o in range(n_dp)]
    )

    slots = collect_tiles(slot_of, (grad_gate, grad_down), shapes, (2, 3))
    slots = collect_tiles(slot_of, (grad_qkv, grad_out), shapes, (0, 1), (slots,))
    slots = after(slots, table_grad, *rows_over)
    own_slots = lax.psum_scatter(slots, "dp", scatter_dimension=0, tiled=True)

    if fused:
        table_grad = jnp.concatenate([early_grad, table_grad], axis=1)
    rows_back = cube_gather(jnp.stack(rows_over).reshape(-1, cols)).reshape(safe.shape + (cols,))
    picked_rows = jnp.where(valid[..., None], rows_back, 0).astype(F32)
    own_table = table_grad.reshape(vocab_part, cols).astype(F32).at[safe.reshape(-1)].add(picked_rows.reshape(-1, cols))

    gain_grad = jnp.stack([dgain1, dgain2, dgain3])
    gain_total = everywhere(gain_grad, jnp.add)
    own_gain = lax.dynamic_slice_in_dim(gain_total, dp * cols, cols, 1)
    first_mp = (mp == 0).astype(F32)
    squares = jnp.sum(own_table * own_table) + first_mp * jnp.sum(own_gain * own_gain)
    if fused:
        more = jnp.zeros((2, 8, 128), F32).at[:, 0, 0].set(jnp.stack([squares, loss_own]))
        squares_all, loss_total = jnp.sum(total_exchange(own_slots, more, n_dp), axis=(1, 2))
    else:
        squares = squares + jnp.sum(jnp.square(own_slots.astype(F32)))
        more = everywhere(jnp.stack([squares, loss_own])[None], jnp.add)[0]
        squares_all, loss_total = more
    norm = jnp.sqrt(squares_all)
    factor = CLIP_NORM / jnp.maximum(norm, CLIP_NORM)
    roots = (left_stat[0], right_stat[0], left_root[0], right_root[0])
    block_new, block_copy, grad_slots, left_new, right_new, *table_step = owner_step(
        factor.reshape(1, 1),
        (own_slots, block_master[0], *roots),
        (own_table, table_master, table_moment, table_second),
    )
    table_new, table_copy, table_moment_new, table_second_new = table_step
    gain_new, gain_moment_new, gain_second_new = adam(
        gain_master, gain_moment, gain_second, factor * own_gain, LR_GAIN, 0.0
    )
    return (
        loss_total,
        norm,
        block_new[None],
        block_copy[None],
        grad_slots[None],
        left_new[None],
        right_new[None],
        table_new,
        table_copy,
        table_moment_new,
        table_second_new,
        gain_new,
        gain_moment_new,
        gain_second_new,
    )


def solution(mesh):
    in_specs = (
        P("dp", None),
        P("dp", None),
        P(),
        P("dp"),
        P("dp", None),
        P("dp"),
        P("mp", None),
        P("mp", "dp", None, None),
        P("mp", "dp", None, None),
        P("mp", "dp", None, None),
        P("mp", "dp", None, None),
        P("mp", "dp", None, None),
        P("mp", "dp"),
        P("mp", "dp"),
        P("mp", "dp"),
        P(None, "dp"),
        P(None, "dp"),
        P(None, "dp"),
    )
    out_specs = (
        P(),
        P(),
        P("mp", "dp", None, None),
        P("mp", "dp", None, None),
        P("mp", "dp", None, None),
        P("mp", "dp", None, None),
        P("mp", "dp", None, None),
        P("mp", "dp"),
        P("mp", "dp"),
        P("mp", "dp"),
        P("mp", "dp"),
        P(None, "dp"),
        P(None, "dp"),
        P(None, "dp"),
    )
    return jax.shard_map(body, mesh=mesh, in_specs=in_specs, out_specs=out_specs, check_vma=False)
```

profile of v0, /device:TPU:0, one launch (start us, length us, event | category | flops | bytes accessed | tf_op | source)
XLA Modules:
  0.0 1140.5 jit_solution(2625466880667116962)
XLA Ops:
  7.3 6.4 bitcast_convert_fusion.1
  19.6 9.3 convert_element_type.104.refs_0_
  31.6 38.1 %gather_fusion.2 = bf16[8192,512]{1,0:T(8,128)(2,1)} fusion(bf16[6144,512]{1,0:T(8,128)(2,1)} %convert_element_type.104.refs_0_, s32[8192]{0:T(1024)S(1)} %broadcast_clamp_fusion), kind=kCustom, calls=%fused_computation.2 | custom fusion | bytes 16809984 | tf_op jit(solution)/shard_map/jit(_take)/gather | solution.py:1211
  75.5 7.1 collective-permute-done.3
  103.0 8.8 collective-permute-done.4
  120.6 7.4 collective-permute-done.5
  135.8 22.3 %collective-permute-done.6 = bf16[256,512]{1,0:T(8,128)(2,1)S(1)} collective-permute-done((bf16[256,512]{1,0:T(8,128)(2,1)S(1)}, bf16[256,512]{1,0:T(8,128)(2,1)S(1)}, u32[]{:S(2)}, u32[]{:S(2)}) %collective-permute-start.6) | collective-permute-done | bytes 262176 | tf_op jit(solution)/shard_map/ppermute | solution.py:52
  158.2 8.3 collective-permute-done.10
  170.8 21.6 %collective-permute-done.15 = bf16[256,2048]{1,0:T(8,128)(2,1)S(1)} collective-permute-done((bf16[256,2048]{1,0:T(8,128)(2,1)S(1)}, bf16[256,2048]{1,0:T(8,128)(2,1)S(1)}, u32[]{:S(2)}, u32[]{:S(2)}) %collective-permute-start.15) | collective-permute-done | bytes 1048608 | tf_op jit(solution)/shard_map/ppermute | solution.py:52
  194.6 10.4 collective-permute-done.17
  215.3 110.8 %all-gather.2.cloned.1.call-done.slots_ref.refs_1_ = bf16[512,128,128]{2,1,0:T(8,128)(2,1)} async-done(((bf16[128,128,128]{2,1,0:T(8,128)(2,1)}), bf16[512,128,128]{2,1,0:T(8,128)(2,1)}) %all-gather.2.cloned.1.call-update) | async-done | bytes 16777232 | tf_op jit(solution)/shard_map/all_gather | solution.py:1162
  353.4 9.0 place_tiles.1
  367.1 18.0 %attend.1 = (bf16[8,64,256]{2,1,0:T(8,128)(2,1)S(1)}, bf16[8,64,256]{2,1,0:T(8,128)(2,1)S(1)}, bf16[8,256,256]{2,1,0:T(8,128)(2,1)S(1)}, bf16[8,256,256]{2,1,0:T(8,128)(2,1)S(1)}) custom-call(bf16[8,256,2048]{2,1,0:T(8,128)(2,1)} %constant_dynamic-update-slice_fusion.h1_ref.refs_2_.h1, bf16[2048,768]{1,0:T(8,128)(2,1)} %copy-done.1, ...), custom_call_target="tpu_custom_call" | custom-call | bytes 1024 | tf_op jit(solution)/shard_map/attend/pallas_call | solution.py:1098
  387.7 30.2 %attend_sum.1 = (f32[64,2048]{1,0:T(8,128)}, bf16[8,64,2048]{2,1,0:T(8,128)(2,1)}) custom-call(bf16[8,64,256]{2,1,0:T(8,128)(2,1)} %copy-done.7, bf16[256,2048]{1,0:T(8,128)(2,1)} %copy-done.4, f32[64,2048]{1,0:T(8,128)} %slice.219.res, f32[1,2048]{1,0:T(1,128)} %get-tuple-element.129.gain), custom_call_target="tpu_custom_call" | custom-call | bytes 1024 | tf_op jit(solution)/shard_map/attend_sum/pallas_call | solution.py:687
  417.9 29.5 %units_sum.1 = (f32[64,2048]{1,0:T(8,128)}, f32[512,2048]{1,0:T(8,128)}, bf16[512,1024]{1,0:T(8,128)(2,1)}, bf16[64,2048]{1,0:T(8,128)(2,1)}) custom-call(bf16[8,64,2048]{2,1,0:T(8,128)(2,1)} %get-tuple-element.70.h2, bf16[2048,2048]{1,0:T(8,128)(2,1)} %get-tuple-element.71.wgate, bf16[1024,2048]{1,0:T(8,128)(2,1)} %copy-done, ...), custom_call_target="tpu_custom_call" | custom-call | bytes 1024 | tf_op jit(solution)/shard_map/units_sum/pallas_call | solution.py:687
  447.4 22.9 %all-to-all-done.refs_0_.head = bf16[4,1536,512]{2,1,0:T(8,128)(2,1)} async-done(((bf16[4,1536,512]{2,1,0:T(8,128)(2,1)}), bf16[4,1536,512]{2,1,0:T(8,128)(2,1)}, u32[]{:S(2)}, u32[]{:S(2)}) %all-to-all-start) | async-done | bytes 6291488 | tf_op jit(solution)/shard_map/all_to_all | solution.py:1225
  470.3 75.6 %head.1 = (bf16[8,256,2048]{2,1,0:T(8,128)(2,1)}, bf16[8,256,1536]{2,1,0:T(8,128)(2,1)}, f32[2,4,512]{2,1,0:T(4,128)}) custom-call(bf16[64,2048]{1,0:T(8,128)(2,1)} %get-tuple-element.74.rows_ref, s32[4,512,1]{2,1,0:T(8,128)} %reshape.510.target_ref, f32[4,512,1]{2,1,0:T(8,128)} %reshape.511.scale_ref, bf16[4,1536,512]{2,1,0:T(8,128)(2,1)} %all-to-all-done.refs_0_.head), custom_call_target="tpu_custom_call" | custom-call | bytes 1048576 | tf_op jit(solution)/shard_map/head/pallas_call | solution.py:506
  545.9 72.2 %head_sum.1 = (f32[64,2048]{1,0:T(8,128)}, f32[1,2048]{1,0:T(1,128)}, bf16[8,64,2048]{2,1,0:T(8,128)(2,1)}, bf16[4,256,512]{2,1,0:T(8,128)(2,1)}, bf16[4,1280,512]{2,1,0:T(8,128)(2,1)}) custom-call(bf16[8,256,1536]{2,1,0:T(8,128)(2,1)} %get-tuple-element.75.dlogits, bf16[4,1536,512]{2,1,0:T(8,128)(2,1)} %all-to-all-done.refs_0_.head, ...), custom_call_target="tpu_custom_call" | custom-call | bytes 1024 | tf_op jit(solution)/shard_map/head_sum/pallas_call | solution.py:687
  624.9 42.9 %gate_sum.1 = (f32[64,2048]{1,0:T(8,128)}, f32[1,2048]{1,0:T(1,128)}, bf16[512,2048]{1,0:T(8,128)(2,1)}, bf16[8,64,2048]{2,1,0:T(8,128)(2,1)}) custom-call(bf16[8,64,2048]{2,1,0:T(8,128)(2,1)} %get-tuple-element.78.down_in, bf16[1024,2048]{1,0:T(8,128)(2,1)} %copy-done, bf16[2048,2048]{1,0:T(8,128)(2,1)} %get-tuple-element.71.wgate, ...), custom_call_target="tpu_custom_call" | custom-call | bytes 1024 | tf_op jit(solution)/shard_map/gate_sum/pallas_call | solution.py:687
  672.7 13.9 %attend_back.1.dqkv = bf16[8,256,768]{2,1,0:T(8,128)(2,1)} custom-call(bf16[8,64,256]{2,1,0:T(8,128)(2,1)S(1)} %get-tuple-element.65.refs_0_, bf16[8,256,256]{2,1,0:T(8,128)(2,1)S(1)} %copy-done.10, bf16[8,256,256]{2,1,0:T(8,128)(2,1)S(1)} %copy-done.12, bf16[8,64,2048]{2,1,0:T(8,128)(2,1)} %get-tuple-element.81.refs_3_, bf16[256,2048]{1,0:T(8,128)(2,1)S(1)} %copy-done.5, ...), custom_call_target="tpu_custom_call" | custom-call | bytes 1024 | tf_op jit(solution)/shard_map/attend_back/pallas_call | solution.py:1098
  686.6 50.5 %input_sum.1 = (bf16[256,2048]{1,0:T(8,128)(2,1)}, f32[1,2048]{1,0:T(1,128)}, bf16[2048,768]{1,0:T(8,128)(2,1)}) custom-call(bf16[8,256,768]{2,1,0:T(8,128)(2,1)} %attend_back.1.dqkv, bf16[2048,768]{1,0:T(8,128)(2,1)} %copy-done.1, bf16[8,256,2048]{2,1,0:T(8,128)(2,1)} %constant_dynamic-update-slice_fusion.h1_ref.refs_2_.h1, ...), custom_call_target="tpu_custom_call" | custom-call | bytes 1024 | tf_op jit(solution)/shard_map/input_sum/pallas_call | solution.py:687
  752.9 5.6 collect_tiles.2.refs_2_
  767.0 21.5 %collective-permute-done.22 = bf16[1024,512]{1,0:T(8,128)(2,1)S(1)} collective-permute-done((bf16[1024,512]{1,0:T(8,128)(2,1)S(1)}, bf16[1024,512]{1,0:T(8,128)(2,1)S(1)}, u32[]{:S(2)}, u32[]{:S(2)}) %collective-permute-start.22) | collective-permute-done | bytes 1048608 | tf_op jit(solution)/shard_map/ppermute | solution.py:52
  790.8 9.2 collective-permute-done.24
  804.3 6.3 collective-permute-done.27
  832.1 5.7 collective-permute-done.31
  850.7 6.8 bitcast_convert_fusion
  857.5 62.7 %scatter_custom_fusion.1.refs_6_ = f32[6144,512]{1,0:T(8,128)} fusion(f32[6144,512]{1,0:T(8,128)} %bitcast_convert_fusion, s32[8192]{0:T(1024)} %bitcast.183, bf16[8192,512]{1,0:T(8,128)(2,1)} %bitcast_select_fusion), kind=kCustom, calls=%fused_computation.8 | custom fusion | flops 8388608 | bytes 20971520 | tf_op jit(solution)/shard_map/scatter-add | solution.py:1410
  920.2 8.5 multiply_reduce_fusion
  930.2 117.4 %reduce-scatter.2.cloned.1.call-done.slots_ref.refs_0_ = bf16[128,128,128]{2,1,0:T(8,128)(2,1)} async-done(((bf16[512,128,128]{2,1,0:T(8,128)(2,1)}), bf16[128,128,128]{2,1,0:T(8,128)(2,1)}) %reduce-scatter.2.cloned.1.call-update) | async-done | bytes 4194320 | tf_op jit(solution)/shard_map/reduce_scatter | solution.py:1404
  1047.6 15.8 %total.1 = f32[2,8,128]{2,1,0:T(8,128)} custom-call(bf16[128,128,128]{2,1,0:T(8,128)(2,1)} %reduce-scatter.2.cloned.1.call-done.slots_ref.refs_0_, f32[2,8,128]{2,1,0:T(8,128)} %scatter.13.more_ref), custom_call_target="tpu_custom_call" | custom-call | tf_op jit(solution)/shard_map/total/pallas_call | solution.py:778
  1066.1 66.3 %owner_step.1 = (f32[128,128,128]{2,1,0:T(8,128)}, bf16[128,128,128]{2,1,0:T(8,128)(2,1)}, f32[128,128,128]{2,1,0:T(8,128)}, f32[128,128,128]{2,1,0:T(8,128)}, f...) custom-call(f32[1,1]{1,0:T(1,128)} %bitcast.59.factor_ref, ...), custom_call_target="tpu_custom_call" | custom-call | tf_op jit(solution)/shard_map/owner_step/pallas_call | solution.py:962
  (321 shorter events, 177.7 us)
Async XLA Ops:
  7.2 318.9 %all-gather.2.cloned.1.call-start = ((), (), s32[]{:S(2)}) async-start(), calls=%async_computation.3 | async-start | bytes 20971520 | tf_op jit(solution)/shard_map/all_gather | solution.py:1162
  13.8 15.1 %collective-permute-start.2 = (s32[2,1537]{1,0:T(2,128)S(1)}, s32[2,1537]{1,0:T(2,128)S(1)}, u32[]{:S(2)}, u32[]{:S(2)}) collective-permute-start(s32[2,1537]{1,0:T(2,128)S(1)} %pad_add_fusion.1), channel_id=1, source_target_pairs={{0,24},{8,16},{16,8},{24,0},{1,25},{9,17},{17,9},{25,1},{2,26},{10... | collective-permute-start | bytes 36896 | tf_op jit(solution)/shard_map/ppermute | solution.py:52
  19.0 10.0 collective-permute-start.1
  19.0 10.0 collective-permute-start
  75.4 7.2 collective-permute-start.3
  86.4 25.4 %collective-permute-start.4 = (bf16[2,2,256,512]{3,2,1,0:T(8,128)(2,1)S(1)}, bf16[2,2,256,512]{3,2,1,0:T(8,128)(2,1)}, u32[]{:S(2)}, u32[]{:S(2)}) collective-permute-start(bf16[2,2,256,512]{3,2,1,0:T(8,128)(2,1)S(1)} %slice.159), channel_id=1, source_target_pairs={{0,2},{1,3},{2,0},{3,1},{4,6},{5,7},{6,4},{7,5},{8,10},{9,11},{10,... | collective-permute-start | bytes 3145736 | tf_op jit(solution)/shard_map/ppermute | solution.py:52
  91.6 26.4 %collective-permute-start.7 = (bf16[2,2,256,512]{3,2,1,0:T(8,128)(2,1)}, bf16[2,2,256,512]{3,2,1,0:T(8,128)(2,1)}, u32[]{:S(2)}, u32[]{:S(2)}) collective-permute-start(bf16[2,2,256,512]{3,2,1,0:T(8,128)(2,1)} %slice.211), channel_id=1, source_target_pairs={{0,4},{1,5},{2,6},{3,7},{4,0},{5,1},{6,2},{7,3},{8,12},{9,13},{10,... | collective-permute-start | bytes 3145736 | tf_op jit(solution)/shard_map/ppermute | solution.py:52
  93.1 7.4 collective-permute-start.11
  113.4 14.6 %collective-permute-start.5 = (bf16[2,256,512]{2,1,0:T(8,128)(2,1)S(1)}, bf16[2,256,512]{2,1,0:T(8,128)(2,1)S(1)}, u32[]{:S(2)}, u32[]{:S(2)}) collective-permute-start(bf16[2,256,512]{2,1,0:T(8,128)(2,1)S(1)} %fusion.7), channel_id=1, source_target_pairs={{0,4},{1,5},{2,6},{3,7},{4,0},{5,1},{6,2},{7,3},{8,12},{9,13},{10,... | collective-permute-start | bytes 1572872 | tf_op jit(solution)/shard_map/ppermute | solution.py:52
  119.9 11.8 %collective-permute-start.8 = (bf16[2,256,512]{2,1,0:T(8,128)(2,1)S(1)}, bf16[2,256,512]{2,1,0:T(8,128)(2,1)S(1)}, u32[]{:S(2)}, u32[]{:S(2)}) collective-permute-start(bf16[2,256,512]{2,1,0:T(8,128)(2,1)S(1)} %fusion.8), channel_id=1, source_target_pairs={{0,2},{1,3},{2,0},{3,1},{4,6},{5,7},{6,4},{7,5},{8,10},{9,11},{10,... | collective-permute-start | bytes 1572872 | tf_op jit(solution)/shard_map/ppermute | solution.py:52
  128.1 30.0 %collective-permute-start.6 = (bf16[256,512]{1,0:T(8,128)(2,1)S(1)}, bf16[256,512]{1,0:T(8,128)(2,1)S(1)}, u32[]{:S(2)}, u32[]{:S(2)}) collective-permute-start(bf16[256,512]{1,0:T(8,128)(2,1)S(1)} %slice_bitcast_fusion.4), channel_id=1, source_target_pairs={{0,8},{8,0},{16,24},{24,16},{1,9},{9,1},{17,25},{25,17},{2,10},{10... | collective-permute-start | bytes 786440 | tf_op jit(solution)/shard_map/ppermute | solution.py:52
  131.9 26.3 %collective-permute-start.9 = (bf16[256,512]{1,0:T(8,128)(2,1)S(1)}, bf16[256,512]{1,0:T(8,128)(2,1)S(1)}, u32[]{:S(2)}, u32[]{:S(2)}) collective-permute-start(bf16[256,512]{1,0:T(8,128)(2,1)S(1)} %get-tuple-element.122), channel_id=1, source_target_pairs={{0,16},{8,24},{16,0},{24,8},{1,17},{9,25},{17,1},{25,9},{2,18},{10... | collective-permute-start | bytes 786440 | tf_op jit(solution)/shard_map/ppermute | solution.py:52
  134.0 32.6 %collective-permute-start.10 = (bf16[256,512]{1,0:T(8,128)(2,1)S(1)}, bf16[256,512]{1,0:T(8,128)(2,1)S(1)}, u32[]{:S(2)}, u32[]{:S(2)}) collective-permute-start(bf16[256,512]{1,0:T(8,128)(2,1)S(1)} %get-tuple-element.121), channel_id=1, source_target_pairs={{0,24},{8,16},{16,8},{24,0},{1,25},{9,17},{17,9},{25,1},{2,26},{10... | collective-permute-start | bytes 786440 | tf_op jit(solution)/shard_map/ppermute | solution.py:52
  168.8 23.6 %collective-permute-start.15 = (bf16[256,2048]{1,0:T(8,128)(2,1)S(1)}, bf16[256,2048]{1,0:T(8,128)(2,1)S(1)}, u32[]{:S(2)}, u32[]{:S(2)}) collective-permute-start(bf16[256,2048]{1,0:T(8,128)(2,1)S(1)} %get-tuple-element.112), channel_id=1, source_target_pairs={{0,4},{1,5},{2,6},{3,7},{4,0},{5,1},{6,2},{7,3},{8,12},{9,13},{10,... | collective-permute-start | bytes 3145736 | tf_op jit(solution)/shard_map/ppermute | solution.py:52
  170.3 24.1 %collective-permute-start.14 = (bf16[256,2048]{1,0:T(8,128)(2,1)S(1)}, bf16[256,2048]{1,0:T(8,128)(2,1)S(1)}, u32[]{:S(2)}, u32[]{:S(2)}) collective-permute-start(bf16[256,2048]{1,0:T(8,128)(2,1)S(1)} %get-tuple-element.112), channel_id=1, source_target_pairs={{0,2},{1,3},{2,0},{3,1},{4,6},{5,7},{6,4},{7,5},{8,10},{9,11},{10,... | collective-permute-start | bytes 3145736 | tf_op jit(solution)/shard_map/ppermute | solution.py:52
  192.5 12.4 %collective-permute-start.17 = (bf16[128,2048]{1,0:T(8,128)(2,1)S(1)}, bf16[128,2048]{1,0:T(8,128)(2,1)S(1)}, u32[]{:S(2)}, u32[]{:S(2)}) collective-permute-start(bf16[128,2048]{1,0:T(8,128)(2,1)S(1)} %slice.218), channel_id=1, source_target_pairs={{0,2},{1,3},{2,0},{3,1},{4,6},{5,7},{6,4},{7,5},{8,10},{9,11},{10,... | collective-permute-start | bytes 1572872 | tf_op jit(solution)/shard_map/ppermute | solution.py:52
  194.5 10.6 collective-permute-start.16
  205.7 7.2 collective-permute-start.18
  326.1 144.2 %all-to-all-start = ((bf16[4,1536,512]{2,1,0:T(8,128)(2,1)}), bf16[4,1536,512]{2,1,0:T(8,128)(2,1)}, u32[]{:S(2)}, u32[]{:S(2)}) async-start(bf16[4,1536,512]{2,1,0:T(8,128)(2,1)} %bitcast.137), calls=%async_computation | async-start | bytes 12582912 | tf_op jit(solution)/shard_map/all_to_all | solution.py:1225
  618.1 144.6 %all-to-all-start.1 = ((bf16[4,1280,512]{2,1,0:T(8,128)(2,1)}), bf16[4,1280,512]{2,1,0:T(8,128)(2,1)}, u32[]{:S(2)}, u32[]{:S(2)}) async-start(bf16[4,1280,512]{2,1,0:T(8,128)(2,1)} %get-tuple-element.86), calls=%async_computation.1 | async-start | bytes 10485760 | tf_op jit(solution)/shard_map/all_to_all | solution.py:1352
  623.3 424.3 %reduce-scatter.2.cloned.1.call-start = ((), (), s32[]{:S(2)}) async-start(), calls=%async_computation.4 | async-start | bytes 20971520 | tf_op jit(solution)/shard_map/reduce_scatter | solution.py:1404
  739.1 22.8 %collective-permute-start.19 = (bf16[256,512]{1,0:T(8,128)(2,1)S(1)}, bf16[256,512]{1,0:T(8,128)(2,1)S(1)}, u32[]{:S(2)}, u32[]{:S(2)}) collective-permute-start(bf16[256,512]{1,0:T(8,128)(2,1)S(1)} %get-tuple-element.119), channel_id=1, source_target_pairs={{0,8},{8,0},{16,24},{24,16},{1,9},{9,1},{17,25},{25,17},{2,10},{10... | collective-permute-start | bytes 786440 | tf_op jit(solution)/shard_map/ppermute | solution.py:52
  741.3 21.4 %collective-permute-start.20 = (bf16[256,512]{1,0:T(8,128)(2,1)S(1)}, bf16[256,512]{1,0:T(8,128)(2,1)S(1)}, u32[]{:S(2)}, u32[]{:S(2)}) collective-permute-start(bf16[256,512]{1,0:T(8,128)(2,1)S(1)} %get-tuple-element.118), channel_id=1, source_target_pairs={{0,16},{8,24},{16,0},{24,8},{1,17},{9,25},{17,1},{25,9},{2,18},{10... | collective-permute-start | bytes 786440 | tf_op jit(solution)/shard_map/ppermute | solution.py:52
  743.7 19.0 %collective-permute-start.21 = (bf16[256,512]{1,0:T(8,128)(2,1)S(1)}, bf16[256,512]{1,0:T(8,128)(2,1)S(1)}, u32[]{:S(2)}, u32[]{:S(2)}) collective-permute-start(bf16[256,512]{1,0:T(8,128)(2,1)S(1)} %get-tuple-element.117), channel_id=1, source_target_pairs={{0,24},{8,16},{16,8},{24,0},{1,25},{9,17},{17,9},{25,1},{2,26},{10... | collective-permute-start | bytes 786440 | tf_op jit(solution)/shard_map/ppermute | solution.py:52
  764.9 23.6 %collective-permute-start.22 = (bf16[1024,512]{1,0:T(8,128)(2,1)S(1)}, bf16[1024,512]{1,0:T(8,128)(2,1)S(1)}, u32[]{:S(2)}, u32[]{:S(2)}) collective-permute-start(bf16[1024,512]{1,0:T(8,128)(2,1)S(1)} %bitcast.154), channel_id=1, source_target_pairs={{0,2},{1,3},{2,0},{3,1},{4,6},{5,7},{6,4},{7,5},{8,10},{9,11},{10,... | collective-permute-start | bytes 3145736 | tf_op jit(solution)/shard_map/ppermute | solution.py:52
  765.4 23.8 %collective-permute-start.23 = (bf16[1024,512]{1,0:T(8,128)(2,1)S(1)}, bf16[1024,512]{1,0:T(8,128)(2,1)S(1)}, u32[]{:S(2)}, u32[]{:S(2)}) collective-permute-start(bf16[1024,512]{1,0:T(8,128)(2,1)S(1)} %bitcast.155), channel_id=1, source_target_pairs={{0,4},{1,5},{2,6},{3,7},{4,0},{5,1},{6,2},{7,3},{8,12},{9,13},{10,... | collective-permute-start | bytes 3145736 | tf_op jit(solution)/shard_map/ppermute | solution.py:52
  788.5 11.6 %collective-permute-start.24 = (bf16[512,512]{1,0:T(8,128)(2,1)S(1)}, bf16[512,512]{1,0:T(8,128)(2,1)S(1)}, u32[]{:S(2)}, u32[]{:S(2)}) collective-permute-start(bf16[512,512]{1,0:T(8,128)(2,1)S(1)} %slice.222), channel_id=1, source_target_pairs={{0,4},{1,5},{2,6},{3,7},{4,0},{5,1},{6,2},{7,3},{8,12},{9,13},{10,... | collective-permute-start | bytes 1572872 | tf_op jit(solution)/shard_map/ppermute | solution.py:52
  789.3 11.4 %collective-permute-start.25 = (bf16[512,512]{1,0:T(8,128)(2,1)S(1)}, bf16[512,512]{1,0:T(8,128)(2,1)S(1)}, u32[]{:S(2)}, u32[]{:S(2)}) collective-permute-start(bf16[512,512]{1,0:T(8,128)(2,1)S(1)} %slice.223), channel_id=1, source_target_pairs={{0,2},{1,3},{2,0},{3,1},{4,6},{5,7},{6,4},{7,5},{8,10},{9,11},{10,... | collective-permute-start | bytes 1572872 | tf_op jit(solution)/shard_map/ppermute | solution.py:52
  803.0 37.5 %collective-permute-start.26 = (bf16[4,1024,512]{2,1,0:T(8,128)(2,1)}, bf16[4,1024,512]{2,1,0:T(8,128)(2,1)}, u32[]{:S(2)}, u32[]{:S(2)}) collective-permute-start(bf16[4,1024,512]{2,1,0:T(8,128)(2,1)} %pad_maximum_fusion.2), channel_id=1, source_target_pairs={{0,1},{1,0},{2,3},{3,2},{4,5},{5,4},{6,7},{7,6},{8,9},{9,8},{10,11... | collective-permute-start | bytes 12582920 | tf_op jit(solution)/shard_map/ppermute | solution.py:52
  803.7 6.9 collective-permute-start.27
  820.2 10.6 collective-permute-start.30
  830.8 7.1 collective-permute-start.31
  (52 other events, 1005.1 us)
Sparse Core Ops, SparseCore 0:
  13.8 312.2 all-gather.1
  763.7 283.8 reduce-scatter.1
where the time goes:
time: 1150 us; the launch traced here: 1140 us
  Pallas kernels  432 us (38%)
  waiting for transfers between devices  404 us (35%)
  other arithmetic  134 us (12%)
  local copies, waits for them, and re-layouts  88.7 us (8%)
  starting transfers between devices  50.4 us (4%)
  between operations  21.8 us (2%)
    pallas_call x5, Pallas kernels, exchange(): pl.pallas_call(kernel, out_shape=[jax.ShapeDtypeStruct(shape, dtype) for...  225 us
    ppermute x32, waiting for transfers between devices, swap(): return lax.ppermute(x, axis, [(i, i ^ bit) for i in range(n)])  153 us
    reduce_scatter x1, waiting for transfers between devices, body(): own_slots = lax.psum_scatter(slots, 'dp', scatter_dimension=0, tiled=True)  117 us
    all_gather x1, waiting for transfers between devices, body(): lax.all_gather(block_master[0].astype(BF16), 'dp', axis=0, tiled=True)  111 us
    pallas_call x1, Pallas kernels, head_call(): pl.pallas_call(functools.partial(head_kernel, n_dp), out_shape=[jax.Shape...  75.6 us
    pallas_call x1, Pallas kernels, owner_step(): pl.pallas_call(functools.partial(owner_step_kernel, steps), grid=(steps +...  66.3 us
    scatter-add x1, other arithmetic, body(): table_grad.reshape(vocab_part, cols).astype(F32).at[safe.reshape(-1)]  62.7 us
    ppermute x32, starting transfers between devices, swap(): return lax.ppermute(x, axis, [(i, i ^ bit) for i in range(n)])  39.6 us
  transfers between devices with their start and end apart: 36, of which 26 were waited for; matrix products, arithmetic and copies ran while one was open for 18% of the time, Pallas kernels for 18%

commit v1 on v0

--- a/solution.py
+++ b/solution.py
@@ -239,10 +239,11 @@
             for copy in copies:
                 copy.wait_send()
 
-    def run(self):
+    def run(self, fill=lambda: None):
         for b in range(len(self.blocks)):
             self.at_core[b].start()
         for step in (self.first_sends, self.second_sends, self.finish):
+            fill()
             for b in range(len(self.blocks)):
                 step(b)
         self.close()
@@ -310,9 +311,11 @@
         for c in (*sent, *self.to_core.values()):
             c.wait_send()
 
-    def run(self):
+    def run(self, fill=lambda: None):
         self.begin()
+        fill()
         self.relay()
+        fill()
         self.relay_far()
         self.arrive()
         self.close()
@@ -376,11 +379,21 @@
     out[...] = forward_step(refs, res, gain, x_out)
 
 
-def gate_sum_kernel(
-    down_in, wdown, wgate, gate_up, x_in, gain, res, dx_out, dgain, dgate_up, out, *refs
-):
-    own, core, held, near, last, parts, mine, sems = refs
+def gate_sum_kernel(down_in, wdown, wgate, gate_up, x_in, gain, res, h2_ref, hidden_ref, *refs):
+    dx_out, dgain, dgate_up, out, down_out, gate_out, *refs = refs
+    own, core, held, near, last, parts, mine, *refs = refs
+    h2, hidden, down_grad, gate_grad, sems, h2_sem, hidden_sem, store_sems = refs
     units = wdown.shape[0]
+    loads = [
+        pltpu.make_async_copy(h2_ref, h2, h2_sem),
+        pltpu.make_async_copy(hidden_ref, hidden, hidden_sem),
+    ]
+    stores = [
+        pltpu.make_async_copy(down_grad, down_out, store_sems.at[0]),
+        pltpu.make_async_copy(gate_grad, gate_out, store_sems.at[1]),
+    ]
+    for copy in loads:
+        copy.start()
     greet(1)
     x = flat(down_in[...])
     step = min(units, 512)
@@ -398,18 +411,40 @@
         parts[:, :, c] = value.astype(BF16).reshape(8, -1, c.size)
 
     by_columns(make)
-    PlaneSum(parts, own, core, held, near, last, sems, 0, 1).run()
+    left = [(down_grad, c) for c in range(0, D, step)]
+    left += [(gate_grad, c) for c in range(0, 2 * units, step)]
+
+    def fill(count=2):
+        for _ in range(min(count, len(left))):
+            grad, c = left.pop(0)
+            at = pl.ds(c, step)
+            if grad is down_grad:
+                value = mm(hidden[...], flat(down_in[:, :, at]), CONTRACT_FIRST)
+            else:
+                value = mm(flat(h2[...]), dgate_up[:, at], CONTRACT_FIRST)
+            grad[:, at] = value.astype(BF16)
+            if not left:
+                stores[1].start()
+            elif grad is down_grad and left[0][0] is gate_grad:
+                stores[0].start()
+
+    for copy in loads:
+        copy.wait()
+    PlaneSum(parts, own, core, held, near, last, sems, 0, 1).run(fill)
     dx, dg = norm_back_step(own[...], x_in[...], gain[...])
     dx = dx + res[...]
     dx_out[...] = dx
     dgain[...] = dg
     mine[...] = dx.astype(BF16)
-    PlaneSpread(mine, out, sems, 7, 0, mine.shape[0]).run()
+    PlaneSpread(mine, out, sems, 7, 0, mine.shape[0]).run(fill)
+    fill(len(left))
+    for copy in stores:
+        copy.wait()
 
 
 def head_kernel(n_dp, rows_ref, target_ref, scale_ref, *refs):
-    head_ref, final_out, dlogits, seen, final, head, mine, logits, *refs = refs
-    stats, plane, mid, line, sems, own_sems = refs
+    head_ref, final_out, dlogits_out, seen, final, head, mine, logits, *refs = refs
+    stats, plane, mid, line, dlogits, sems, own_sems = refs
     rows, vocab = rows_ref.shape[0], logits.shape[2]
     wide = head.shape[2]
     load = pltpu.make_async_copy(head_ref, head, own_sems.at[0])
@@ -489,7 +524,15 @@
         hit = (column == target_ref[b]).astype(F32)
         grad = (scale_ref[b] * (jnp.exp(value - lse) - hit)).astype(BF16)
         dlogits[:, part, :] = grad.reshape(8, rows, vocab)
-
+        pltpu.make_async_copy(
+            dlogits.at[:, part, :], dlogits_out.at[:, part, :], own_sems.at[2 + b]
+        ).start()
+
+    for b in range(n_dp):
+        part = pl.ds(b * rows, rows)
+        pltpu.make_async_copy(
+            dlogits.at[:, part, :], dlogits_out.at[:, part, :], own_sems.at[2 + b]
+        ).wait()
     for copy in across:
         copy.wait_send()
     for each in blocks:
@@ -507,7 +550,7 @@
         functools.partial(head_kernel, n_dp),
         out_shape=[jax.ShapeDtypeStruct(shape, dtype) for shape, dtype in outs],
         in_specs=[pl.BlockSpec(memory_space=pltpu.VMEM)] * 3 + [anywhere],
-        out_specs=[anywhere] + [pl.BlockSpec(memory_space=pltpu.VMEM)] * 2,
+        out_specs=[anywhere, anywhere, pl.BlockSpec(memory_space=pltpu.VMEM)],
         scratch_shapes=[
             pltpu.VMEM((8, total, D), BF16),
             pltpu.VMEM(head.shape, BF16),
@@ -517,8 +560,9 @@
             pltpu.VMEM((7,) + stats, F32),
             pltpu.VMEM(stats, F32),
             pltpu.VMEM((n_dp - 1,) + stats, F32),
+            pltpu.VMEM((8, total, vocab), BF16),
             pltpu.SemaphoreType.DMA((2, 14 * n_dp + 6 + n_dp)),
-            pltpu.SemaphoreType.DMA((2,)),
+            pltpu.SemaphoreType.DMA((2 + n_dp,)),
         ],
         compiler_params=pltpu.CompilerParams(
             collective_id=5, has_side_effects=True, vmem_limit_bytes=56 << 20
@@ -551,16 +595,30 @@
         x = flat(final[:, :, pl.ds(pl.multiple_of(p * wide, 128), wide)])
         return mm(flat(dlogits[:, :, pl.ds(first, number)]), x, CONTRACT_FIRST).astype(BF16)
 
-    left = [(p, v) for p in range(n_dp) for v in range(cut, vocab, 256)]
+    whole = cut[0] + cut[1]
+    left = [(p, v) for p in range(n_dp) for v in range(whole, vocab, 384)]
 
     def fill(count):
         for _ in range(min(count, len(left))):
             p, v = left.pop(0)
-            grads[p, pl.ds(v - cut, 256), :] = table_part(p, v, 256)
-
-    first_rows = [
-        peer_copy(ready.at[o - 1], early.at[a], sems, 12 + 8 * n_dp + o, dp=a ^ o)
-        for o in range(1, n_dp)
+            number = min(384, vocab - v)
+            grads[p, pl.ds(v - whole, number), :] = table_part(p, v, number)
+
+    def rows_of(e):
+        return pl.ds(e * cut[0], cut[e])
+
+    early_sends = [
+        [
+            peer_copy(
+                ready.at[o - 1, rows_of(e)],
+                early.at[a, rows_of(e)],
+                sems,
+                12 + (8 + e) * n_dp + o,
+                dp=a ^ o,
+            )
+            for o in range(1, n_dp)
+        ]
+        for e in range(2)
     ]
     across = {
         b: peer_copy(
@@ -579,14 +637,14 @@
     make(2)
     load.wait()
     for o in range(1, n_dp):
-        ready[o - 1] = table_part(a ^ o, 0, cut)
-        first_rows[o - 1].start()
+        ready[o - 1, rows_of(0)] = table_part(a ^ o, 0, cut[0])
+        early_sends[0][o - 1].start()
     plan.first_sends(2)
     make(3)
     plan.second_sends(2)
     plan.first_sends(3)
     make(1)
-    early[a] = table_part(a, 0, cut)
+    early[a, rows_of(0)] = table_part(a, 0, cut[0])
     plan.first_sends(1)
     plan.second_sends(3)
     make(0)
@@ -595,14 +653,16 @@
     fill(2)
     plan.second_sends(1)
     finish(3)
-    fill(6)
+    for o in range(1, n_dp):
+        ready[o - 1, rows_of(1)] = table_part(a ^ o, *cut)
+    early[a, rows_of(1)] = table_part(a, *cut)
     plan.second_sends(0)
     finish(1)
+    for copy in early_sends[1]:
+        copy.start()
     fill(7)
     finish(0)
     fill(len(left))
-    for copy in first_rows:
-        copy.wait()
     for copy in across.values():
         copy.wait()
     grad = own[pl.ds(0, rows)]
@@ -614,14 +674,21 @@
     mine[...] = dx.astype(BF16)
     PlaneSpread(mine, out, sems, 7 * n_dp, 0, rows).run()
     plan.close()
-
-
-def input_back_kernel(dqkv, wqkv, h1, x_in, gain, res, dx_out, dgain, grads, *refs):
-    own, core, held, near, last, parts, _, sems = refs
-    rows = res.shape[0]
+    for copies in early_sends:
+        for copy in copies:
+            copy.wait()
+
+
+def input_back_kernel(n_dp, dqkv, wqkv, x_in, gain, res, h1_ref, over, dgain, grads, *refs):
+    own, core, held, near, last, parts, _, dx_out, h1, sems, h1_sem = refs
+    rows, wide = res.shape[0], over.shape[2]
     blocks = x_in.shape[0] // rows
-    greet(1)
+    a = lax.axis_index("dp")
+    load = pltpu.make_async_copy(h1_ref, h1, h1_sem)
+    load.start()
+    greet(n_dp)
     plan = PlaneSum(parts, own, core, held, near, last, sems, 0, blocks)
+    sent = []
 
     def make(b):
         part = pl.ds(b * rows, rows)
@@ -648,6 +715,17 @@
             dgain[...] += dg
         dx_out[part] = dx.astype(BF16)
 
+        def columns(o):
+            return pl.ds(pl.multiple_of((a ^ o) * wide, 128), wide)
+
+        over[0, part] = dx_out[part, columns(0)]
+        for o in range(1, n_dp):
+            copy = peer_copy(
+                dx_out.at[part, columns(o)], over.at[o, part], sems, 7 * blocks + len(sent), dp=a ^ o
+            )
+            copy.start()
+            sent.append(copy)
+
     make(0)
     make(1)
     plan.first_sends(0)
@@ -658,6 +736,7 @@
     plan.first_sends(2)
     plan.second_sends(1)
     plan.first_sends(3)
+    load.wait()
     fill()
     close(0)
     plan.second_sends(2)
@@ -669,9 +748,11 @@
     fill()
     close(3)
     plan.close()
-
-
-def exchange(kernel, name, number, n_dp, total, outs, *args, more=(), sems=20, far=0):
+    for copy in sent:
+        copy.wait()
+
+
+def exchange(kernel, name, number, n_dp, total, outs, *args, more=(), sems=20, far=0, stored=0):
     half = total // 2
     rows = outs[0][0][0]
     scratch = [
@@ -689,10 +770,12 @@
         out_shape=[jax.ShapeDtypeStruct(shape, dtype) for shape, dtype in outs],
         in_specs=[pl.BlockSpec(memory_space=pltpu.VMEM)] * (len(args) - far)
         + [pl.BlockSpec(memory_space=pl.ANY)] * far,
-        out_specs=[pl.BlockSpec(memory_space=pltpu.VMEM)] * len(outs),
+        out_specs=[pl.BlockSpec(memory_space=pltpu.VMEM)] * (len(outs) - stored)
+        + [pl.BlockSpec(memory_space=pl.ANY)] * stored,
         scratch_shapes=scratch
         + [pltpu.SemaphoreType.DMA((2, sems))]
-        + [pltpu.SemaphoreType.DMA] * far,
+        + [pltpu.SemaphoreType.DMA] * far
+        + [pltpu.SemaphoreType.DMA((stored,))] * (stored > 0),
         compiler_params=pltpu.CompilerParams(
             collective_id=number, has_side_effects=True, vmem_limit_bytes=62 << 20
         ),
@@ -951,7 +1034,7 @@
 def owner_step(factor, tiles, table):
     number, size, _ = tiles[0].shape
     rows, cols = table[0].shape
-    group, band = 16, 512
+    group, band = min(32, number), 512
     steps = number // group
 
     tile = pl.BlockSpec((group, size, size), lambda i: (jnp.minimum(i, steps - 1), 0, 0))
@@ -965,7 +1048,7 @@
         out_shape=out_shape,
         in_specs=[pl.BlockSpec(memory_space=pltpu.SMEM)] + [tile] * 6 + [part] * 4,
         out_specs=[tile] * 5 + [part] * 4,
-        compiler_params=pltpu.CompilerParams(vmem_limit_bytes=56 << 20),
+        compiler_params=pltpu.CompilerParams(vmem_limit_bytes=62 << 20),
         name="owner_step",
     )(factor, *tiles, *table)
 
@@ -1042,9 +1125,19 @@
             o_ref[:, ans, lanes] = o.reshape(n, n_ans, 128)
 
 
-def attend_back_kernel(items, *refs):
-    q_ref, k_ref, v_ref, dx_ref, w_ref, cos_ref, sin_ref, col_ref, row_ref, d_ref, do_ref = refs
+def attend_back_kernel(items, shapes, slot_ref, *refs):
+    q_ref, k_ref, v_ref, dx_ref, w_ref, o_ref, cos_ref, sin_ref, col_ref, row_ref, *refs = refs
+    gate_ref, down_ref, d_ref, grad_ref, slots_ref, do_ref, gate, down, load_sems, sem = refs
+    loads = [
+        pltpu.make_async_copy(gate_ref, gate, load_sems.at[0]),
+        pltpu.make_async_copy(down_ref, down, load_sems.at[1]),
+    ]
+    for copy in loads:
+        copy.start()
     n, rows_ans, width = q_ref.shape
+    for c in range(D // 512):
+        at = pl.ds(c * 512, 512)
+        grad_ref[:, at] = mm(o_ref[...], flat(dx_ref[:, :, at]), CONTRACT_FIRST).astype(BF16)
     do_ref[...] = mm(flat(dx_ref[...]), w_ref[...], CONTRACT_LAST).astype(BF16).reshape(q_ref.shape)
     n_ans = rows_ans // items
     n_ctx = k_ref.shape[1] // items - n_ans
@@ -1052,7 +1145,20 @@
     lane = lax.broadcasted_iota(jnp.int32, (1, 128), 1)
     root = HD ** (-0.5)
 
+    def collect():
+        size = slots_ref.shape[1]
+        firsts = first_tiles(shapes, size)
+        for load, k, ref in zip(loads, (2, 3), (gate, down)):
+            load.wait()
+
+            def send(tile, view, ref=ref):
+                pltpu.make_async_copy(ref.at[view], slots_ref.at[slot_ref[tile]], sem).start()
+
+            each_tile(shapes[k], size, firsts[k], send)
+
     for item in range(items):
+        if item == 1 or items == 1:
+            collect()
         ans = pl.ds(item * n_ans, n_ans)
         ctx = pl.ds(rows_ans + item * n_ctx, n_ctx)
         turns = [(flat(cos_ref[:, r]), -flat(sin_ref[:, r])) for r in (ans, ctx)]
@@ -1092,6 +1198,31 @@
             d_ref[:, ctx, klanes] = dk_ctx.astype(BF16).reshape(n, n_ctx, 128)
             d_ref[:, ans, vlanes] = sums[3].astype(BF16).reshape(n, n_ans, 128)
             d_ref[:, ctx, vlanes] = sums[2].astype(BF16).reshape(n, n_ctx, 128)
+    for ref in (gate, down):
+        pltpu.make_async_copy(ref, ref, sem).wait()
+
+
+def attend_back(items, shapes, slot_of, grads, size, *args):
+    query, key = args[:2]
+    n, rows, width = key.shape
+    anywhere = pl.BlockSpec(memory_space=pl.ANY)
+    vmem = pl.BlockSpec(memory_space=pltpu.VMEM)
+    return pl.pallas_call(
+        functools.partial(attend_back_kernel, items, shapes),
+        out_shape=[
+            jax.ShapeDtypeStruct((n, rows, 3 * width), BF16),
+            jax.ShapeDtypeStruct(shapes[1], BF16),
+            jax.ShapeDtypeStruct((slot_of.shape[0], size, size), BF16),
+        ],
+        in_specs=[pl.BlockSpec(memory_space=pltpu.SMEM)] + [vmem] * len(args) + [anywhere] * 2,
+        out_specs=[vmem, vmem, anywhere],
+        scratch_shapes=[pltpu.VMEM(query.shape, BF16)]
+        + [pltpu.VMEM(grad.shape, BF16) for grad in grads]
+        + [pltpu.SemaphoreType.DMA((2,)), pltpu.SemaphoreType.DMA],
+        compiler_params=pltpu.CompilerParams(vmem_limit_bytes=62 << 20),
+        cost_estimate=pl.CostEstimate(flops=0, bytes_accessed=1 << 10, transcendentals=0),
+        name="attend_back",
+    )(slot_of, *args, *grads)
 
 
 def in_vmem(kernel, name, outs, scratch, *args):
@@ -1101,7 +1232,7 @@
         in_specs=[pl.BlockSpec(memory_space=pltpu.VMEM)] * len(args),
         out_specs=[pl.BlockSpec(memory_space=pltpu.VMEM)] * len(outs),
         scratch_shapes=[pltpu.VMEM(shape, dtype) for shape, dtype in scratch],
-        compiler_params=pltpu.CompilerParams(vmem_limit_bytes=48 << 20),
+        compiler_params=pltpu.CompilerParams(vmem_limit_bytes=62 << 20),
         cost_estimate=pl.CostEstimate(flops=0, bytes_accessed=1 << 10, transcendentals=0),
         name=name,
     )(*args)
@@ -1313,7 +1444,7 @@
     loss_own = jnp.sum(row_scale[:rows_ans] * (lse - picked)[:rows_ans]) * pairs_all
 
     if fused:
-        cut = 256
+        cut = (256, 128)
         total = n_dp * rows_ans
         dx2, dgain3, down_in, early_grad, head_grad = exchange(
             functools.partial(head_back_kernel, n_dp, cut), "head_sum", 3, n_dp, total,
@@ -1321,8 +1452,8 @@
                 own,
                 gain_row,
                 plane,
-                ((n_dp, cut, cols), BF16),
-                ((n_dp, sub - cut, cols), BF16),
+                ((n_dp, sum(cut), cols), BF16),
+                ((n_dp, sub - sum(cut), cols), BF16),
             ),
             *(dlogits.reshape(n_mp, -1, sub), head_parts, x2, gains[2:3]),
             final.reshape(n_mp, -1, D),
@@ -1330,9 +1461,9 @@
                 (total, D),
                 (n_dp - 1, rows_ans, D),
                 (n_mp, total, D),
-                (n_dp - 1, cut, cols),
+                (n_dp - 1, sum(cut), cols),
             ),
-            sems=13 + 9 * n_dp,
+            sems=13 + 10 * n_dp,
             far=1,
         )
         dgain3 = dgain3[0]
@@ -1351,10 +1482,21 @@
         )
     table_grad = lax.all_to_all(head_grad, "dp", 0, 0)
     if fused:
-        dx1, dgain2, dgate_up, out_in = exchange(
+        dx1, dgain2, dgate_up, out_in, grad_down, grad_gate = exchange(
             gate_sum_kernel, "gate_sum", 4, n_dp, rows_ans,
-            (own, gain_row, (gate_up.shape, BF16), plane),
+            (
+                own,
+                gain_row,
+                (gate_up.shape, BF16),
+                plane,
+                (wdown.shape, BF16),
+                (wgate.shape, BF16),
+            ),
             *(down_in, wdown, wgate, gate_up, x1, gains[1:2], dx2),
+            *(h2.reshape(n_mp, rows_ans, D), hidden),
+            more=((n_mp, rows_ans, D), hidden.shape, wdown.shape, wgate.shape),
+            far=2,
+            stored=2,
         )
         dgain2 = dgain2[0]
         down_in = down_in.reshape(-1, D)
@@ -1369,23 +1511,22 @@
         dx_mlp, dgain2 = norm_backward(dnormed2, *norm_forward(x1), gains[1])
         dx1 = dx2 + dx_mlp
         out_in = cube_gather(dx1.astype(BF16))
-    grad_down = dot("tf,td->fd", hidden, down_in).astype(BF16)
-    grad_gate = dot("td,tf->df", h2, dgate_up).astype(BF16)
-    grad_out = dot("tw,td->wd", o_rows, out_in.reshape(-1, D)).astype(BF16)
-    (dqkv,) = in_vmem(
-        functools.partial(attend_back_kernel, items),
-        "attend_back",
-        (((n_mp, rows_own, 3 * width), BF16),),
-        (ans_shape,),
-        *(query, key, value, out_in, wout, cosine, sine, *place),
+        grad_down = dot("tf,td->fd", hidden, down_in).astype(BF16)
+        grad_gate = dot("td,tf->df", h2, dgate_up).astype(BF16)
+    dqkv, grad_out, slots = attend_back(
+        items, shapes, slot_of, (grad_gate, grad_down), block_master.shape[-1],
+        *(query, key, value, out_in, wout, o_rows, cosine, sine, *place),
     )
     dqkv = dqkv.reshape(-1, 3 * width)
+
     if fused:
-        dx0, dgain1, grad_qkv = exchange(
-            input_back_kernel, "input_sum", 7, n_dp, rows_own,
-            (((rows_own, D), BF16), gain_row, (wqkv.shape, BF16)),
-            *(dqkv.reshape(n_mp, rows_own, -1), wqkv, h1, x0, gains[:1], dx1),
-            sems=7 * (rows_own // rows_ans),
+        rows_over, dgain1, grad_qkv = exchange(
+            functools.partial(input_back_kernel, n_dp), "input_sum", 7, n_dp, rows_own,
+            (((n_dp, rows_own, cols), BF16), gain_row, (wqkv.shape, BF16)),
+            *(dqkv.reshape(n_mp, rows_own, -1), wqkv, x0, gains[:1], dx1, h1),
+            more=((rows_own, D), (n_mp, rows_own, D)),
+            sems=(7 + n_dp - 1) * (rows_own // rows_ans),
+            far=1,
         )
         dgain1 = dgain1[0]
     else:
@@ -1393,19 +1534,16 @@
         grad_qkv = dot("td,te->de", h1_all, dqkv).astype(BF16)
         dx0, dgain1 = norm_backward(cube_scatter(dh1), *norm_forward(x0), gains[0])
         dx0 = jnp.concatenate([dx0[:rows_ans] + dx1, dx0[rows_ans:]]).astype(BF16)
-
-    rows_over = line_exchange(
-        [lax.dynamic_slice_in_dim(dx0, near[o] * cols, cols, 1) for o in range(n_dp)]
-    )
-
-    slots = collect_tiles(slot_of, (grad_gate, grad_down), shapes, (2, 3))
+        parts = [lax.dynamic_slice_in_dim(dx0, near[o] * cols, cols, 1) for o in range(n_dp)]
+        rows_over = jnp.stack(line_exchange(parts))
+
     slots = collect_tiles(slot_of, (grad_qkv, grad_out), shapes, (0, 1), (slots,))
-    slots = after(slots, table_grad, *rows_over)
+    slots = after(slots, table_grad, rows_over)
     own_slots = lax.psum_scatter(slots, "dp", scatter_dimension=0, tiled=True)
 
     if fused:
         table_grad = jnp.concatenate([early_grad, table_grad], axis=1)
-    rows_back = cube_gather(jnp.stack(rows_over).reshape(-1, cols)).reshape(safe.shape + (cols,))
+    rows_back = cube_gather(rows_over.reshape(-1, cols)).reshape(safe.shape + (cols,))
     picked_rows = jnp.where(valid[..., None], rows_back, 0).astype(F32)
     own_table = table_grad.reshape(vocab_part, cols).astype(F32).at[safe.reshape(-1)].add(picked_rows.reshape(-1, cols))
 

time: 1150 us -> 1140 us (level)
  Pallas kernels: 432 us -> 446 us
    pallas_call x5, Pallas kernels: 225 us -> 244 us  [exchange(): pl.pallas_call(kernel, out_shape=[jax.ShapeDtypeStruct(shape, dtype) for...]
    pallas_call x0 -> x1, Pallas kernels: none -> 17.7 us  [attend_back(): pl.pallas_call(functools.partial(attend_back_kernel, items, shapes), out_...]
    pallas_call x2 -> x1, Pallas kernels: 31.9 us -> 19.3 us  [in_vmem(): pl.pallas_call(kernel, out_shape=[jax.ShapeDtypeStruct(shape, dtype) for...]
    ppermute x32 -> x29, starting transfers between devices: 39.6 us -> 31.5 us  [swap(): return lax.ppermute(x, axis, [(i, i ^ bit) for i in range(n)])]
    ppermute x32 -> x29, waiting for transfers between devices: 153 us -> 156 us  [swap(): return lax.ppermute(x, axis, [(i, i ^ bit) for i in range(n)])]
  transfers between devices with their start and end apart: 36 -> 33, of which waited for: 26 -> 25; matrix products, arithmetic and copies ran while one was open for 18% -> 18% of each run, Pallas kernels for 18% -> 19%
where the time goes in v1:
time: 1140 us; the launch traced here: 1130 us
  Pallas kernels  446 us (39%)
  waiting for transfers between devices  400 us (35%)
  other arithmetic  133 us (12%)
  local copies, waits for them, and re-layouts  87.2 us (8%)
  starting transfers between devices  44.1 us (4%)
  between operations  21.6 us (2%)
    pallas_call x5, Pallas kernels, exchange(): pl.pallas_call(kernel, out_shape=[jax.ShapeDtypeStruct(shape, dtype) for...  244 us
    ppermute x29, waiting for transfers between devices, swap(): return lax.ppermute(x, axis, [(i, i ^ bit) for i in range(n)])  156 us
    all_gather x1, waiting for transfers between devices, body(): lax.all_gather(block_master[0].astype(BF16), 'dp', axis=0, tiled=True)  112 us
    reduce_scatter x1, waiting for transfers between devices, body(): own_slots = lax.psum_scatter(slots, 'dp', scatter_dimension=0, tiled=True)  112 us
    pallas_call x1, Pallas kernels, head_call(): pl.pallas_call(functools.partial(head_kernel, n_dp), out_shape=[jax.Shape...  74.5 us
    pallas_call x1, Pallas kernels, owner_step(): pl.pallas_call(functools.partial(owner_step_kernel, steps), grid=(steps +...  63.1 us
    scatter-add x1, other arithmetic, body(): table_grad.reshape(vocab_part, cols).astype(F32).at[safe.reshape(-1)]  59.9 us
    gather x1, local copies, waits for them, and re-layouts, body(): looked = jnp.where(valid[..., None], jnp.take(table_low, safe, axis=0), 0)  38.1 us
  transfers between devices with their start and end apart: 33, of which 25 were waited for; matrix products, arithmetic and copies ran while one was open for 18% of the time, Pallas kernels for 19%

profile of v1, /device:TPU:0, one launch (start us, length us, event | category | flops | bytes accessed | tf_op | source)
XLA Modules:
  0.0 1131.2 jit_solution(18317402916516284160)
XLA Ops:
  7.3 6.4 bitcast_convert_fusion.1
  19.6 9.3 convert_element_type.95.refs_0_
  31.1 38.1 %gather_fusion.2 = bf16[8192,512]{1,0:T(8,128)(2,1)} fusion(bf16[6144,512]{1,0:T(8,128)(2,1)} %convert_element_type.95.refs_0_, s32[8192]{0:T(1024)S(1)} %broadcast_clamp_fusion), kind=kCustom, calls=%fused_computation.2 | custom fusion | bytes 16809984 | tf_op jit(solution)/shard_map/jit(_take)/gather | solution.py:1342
  74.9 7.1 collective-permute-done.3
  102.3 8.8 collective-permute-done.4
  120.0 7.3 collective-permute-done.5
  135.3 21.2 %collective-permute-done.6 = bf16[256,512]{1,0:T(8,128)(2,1)S(1)} collective-permute-done((bf16[256,512]{1,0:T(8,128)(2,1)S(1)}, bf16[256,512]{1,0:T(8,128)(2,1)S(1)}, u32[]{:S(2)}, u32[]{:S(2)}) %collective-permute-start.6) | collective-permute-done | bytes 262176 | tf_op jit(solution)/shard_map/ppermute | solution.py:52
  156.6 9.4 collective-permute-done.10
  169.5 21.6 %collective-permute-done.15 = bf16[256,2048]{1,0:T(8,128)(2,1)S(1)} collective-permute-done((bf16[256,2048]{1,0:T(8,128)(2,1)S(1)}, bf16[256,2048]{1,0:T(8,128)(2,1)S(1)}, u32[]{:S(2)}, u32[]{:S(2)}) %collective-permute-start.15) | collective-permute-done | bytes 1048608 | tf_op jit(solution)/shard_map/ppermute | solution.py:52
  193.3 10.4 collective-permute-done.17
  214.1 112.0 %all-gather.2.cloned.1.call-done.slots_ref.refs_1_ = bf16[512,128,128]{2,1,0:T(8,128)(2,1)} async-done(((bf16[128,128,128]{2,1,0:T(8,128)(2,1)}), bf16[512,128,128]{2,1,0:T(8,128)(2,1)}) %all-gather.2.cloned.1.call-update) | async-done | bytes 16777232 | tf_op jit(solution)/shard_map/all_gather | solution.py:1293
  357.3 9.0 place_tiles.1
  371.0 19.3 %attend.1 = (bf16[8,64,256]{2,1,0:T(8,128)(2,1)}, bf16[8,64,256]{2,1,0:T(8,128)(2,1)}, bf16[8,256,256]{2,1,0:T(8,128)(2,1)}, bf16[8,256,256]{2,1,0:T(8,128)(2,1)}) custom-call(bf16[8,256,2048]{2,1,0:T(8,128)(2,1)} %constant_dynamic-update-slice_fusion.h1_ref.refs_2_, bf16[2048,768]{1,0:T(8,128)(2,1)} %copy-done.1, ...), custom_call_target="tpu_custom_call" | custom-call | bytes 1024 | tf_op jit(solution)/shard_map/attend/pallas_call | solution.py:1229
  390.4 30.3 %attend_sum.1 = (f32[64,2048]{1,0:T(8,128)}, bf16[8,64,2048]{2,1,0:T(8,128)(2,1)}) custom-call(bf16[8,64,256]{2,1,0:T(8,128)(2,1)} %get-tuple-element.72.o, bf16[256,2048]{1,0:T(8,128)(2,1)} %copy-done.2, f32[64,2048]{1,0:T(8,128)} %slice.215.res, f32[1,2048]{1,0:T(1,128)} %get-tuple-element.133.gain), custom_call_target="tpu_custom_call" | custom-call | bytes 1024 | tf_op jit(solution)/shard_map/attend_sum/pallas_call | solution.py:768
  420.7 29.5 %units_sum.1 = (f32[64,2048]{1,0:T(8,128)}, f32[512,2048]{1,0:T(8,128)}, bf16[512,1024]{1,0:T(8,128)(2,1)}, bf16[64,2048]{1,0:T(8,128)(2,1)}) custom-call(bf16[8,64,2048]{2,1,0:T(8,128)(2,1)} %get-tuple-element.74.h2.h2_ref, bf16[2048,2048]{1,0:T(8,128)(2,1)} %get-tuple-element.75.wgate, bf16[1024,2048]{1,0:T(8,128)(2,1)} %copy-done, ...), custom_call_target="tpu_custom_call" | custom-call | bytes 1024 | tf_op jit(solution)/shard_map/units_sum/pallas_call | solution.py:768
  450.2 20.1 %all-to-all-done.refs_0_.head = bf16[4,1536,512]{2,1,0:T(8,128)(2,1)} async-done(((bf16[4,1536,512]{2,1,0:T(8,128)(2,1)}), bf16[4,1536,512]{2,1,0:T(8,128)(2,1)}, u32[]{:S(2)}, u32[]{:S(2)}) %all-to-all-start) | async-done | bytes 6291488 | tf_op jit(solution)/shard_map/all_to_all | solution.py:1356
  470.3 74.5 %head.1 = (bf16[8,256,2048]{2,1,0:T(8,128)(2,1)}, bf16[8,256,1536]{2,1,0:T(8,128)(2,1)}, f32[2,4,512]{2,1,0:T(4,128)}) custom-call(bf16[64,2048]{1,0:T(8,128)(2,1)} %get-tuple-element.78.rows_ref, s32[4,512,1]{2,1,0:T(8,128)} %reshape.503.target_ref, f32[4,512,1]{2,1,0:T(8,128)} %reshape.504.scale_ref, bf16[4,1536,512]{2,1,0:T(8,128)(2,1)} %all-to-all-done.refs_0_.head), custom_call_target="tpu_custom_call" | custom-call | bytes 1048576 | tf_op jit(solution)/shard_map/head/pallas_call | solution.py:549
  544.8 73.7 %head_sum.1 = (f32[64,2048]{1,0:T(8,128)}, f32[1,2048]{1,0:T(1,128)}, bf16[8,64,2048]{2,1,0:T(8,128)(2,1)}, bf16[4,384,512]{2,1,0:T(8,128)(2,1)}, bf16[4,1152,512]{2,1,0:T(8,128)(2,1)}) custom-call(bf16[8,256,1536]{2,1,0:T(8,128)(2,1)} %get-tuple-element.79.dlogits, bf16[4,1536,512]{2,1,0:T(8,128)(2,1)} %all-to-all-done.refs_0_.head, ...), custom_call_target="tpu_custom_call" | custom-call | bytes 1024 | tf_op jit(solution)/shard_map/head_sum/pallas_call | solution.py:768
  618.5 7.0 all-to-all-start.1
  627.1 43.2 %gate_sum.1 = (f32[64,2048]{1,0:T(8,128)}, f32[1,2048]{1,0:T(1,128)}, bf16[512,2048]{1,0:T(8,128)(2,1)}, bf16[8,64,2048]{2,1,0:T(8,128)(2,1)}, bf16[1024,2048]{1,0:T(8,128)(2,1)}, /*index=5*/bf16[2048,2048]{1,0:T(8,128)(2,1)}) custom-call(bf16[8,64,2048]{2,1,0:T(8,128)(2,1)} %get-tuple-element.82.down_in, bf16[1024,2048]{1,0:T(8,128)(2,1)} %copy-done, ...), custom_call_target="tpu_custom_call" | custom-call | bytes 1024 | tf_op jit(solution)/shard_map/gate_sum/pallas_call | solution.py:768
  670.3 17.7 %attend_back.1 = (bf16[8,256,768]{2,1,0:T(8,128)(2,1)}, bf16[256,2048]{1,0:T(8,128)(2,1)}, bf16[512,128,128]{2,1,0:T(8,128)(2,1)}) custom-call(s32[512]{0:T(512)} %copy-done.5, bf16[8,64,256]{2,1,0:T(8,128)(2,1)} %get-tuple-element.69.refs_0_, bf16[8,256,256]{2,1,0:T(8,128)(2,1)} %get-tuple-element.70.refs_1_, ...), custom_call_target="tpu_custom_call" | custom-call | bytes 1024 | tf_op jit(solution)/shard_map/attend_back/pallas_call | solution.py:1210
  688.1 67.0 %input_sum.1 = (bf16[4,256,512]{2,1,0:T(8,128)(2,1)}, f32[1,2048]{1,0:T(1,128)}, bf16[2048,768]{1,0:T(8,128)(2,1)}) custom-call(bf16[8,256,768]{2,1,0:T(8,128)(2,1)} %get-tuple-element.89.dqkv, bf16[2048,768]{1,0:T(8,128)(2,1)} %copy-done.1, f32[256,2048]{1,0:T(8,128)} %convert_element_type.107.x_in, f32[1,2048]{1,0:T(1,128)} %copy-done.11, ...), custom_call_target="tpu_custom_call" | custom-call | bytes 1024 | tf_op jit(solution)/shard_map/input_sum/pallas_call | solution.py:768
  763.0 23.1 %collective-permute-done.19 = bf16[1024,512]{1,0:T(8,128)(2,1)S(1)} collective-permute-done((bf16[1024,512]{1,0:T(8,128)(2,1)S(1)}, bf16[1024,512]{1,0:T(8,128)(2,1)S(1)}, u32[]{:S(2)}, u32[]{:S(2)}) %collective-permute-start.19) | collective-permute-done | bytes 1048608 | tf_op jit(solution)/shard_map/ppermute | solution.py:52
  788.3 11.0 collective-permute-done.21
  804.7 6.1 collective-permute-done.24
  842.5 7.6 bitcast_select_fusion
  852.9 6.7 bitcast_convert_fusion
  859.6 59.9 %scatter_custom_fusion.1.refs_6_ = f32[6144,512]{1,0:T(8,128)} fusion(f32[6144,512]{1,0:T(8,128)} %bitcast_convert_fusion, s32[8192]{0:T(1024)S(1)} %bitcast.159, bf16[8192,512]{1,0:T(8,128)(2,1)} %bitcast_select_fusion), kind=kCustom, calls=%fused_computation.8 | custom fusion | flops 8388608 | bytes 20971520 | tf_op jit(solution)/shard_map/scatter-add | solution.py:1548
  919.6 8.5 multiply_reduce_fusion
  929.5 112.0 %reduce-scatter.2.cloned.1.call-done.slots_ref.refs_0_ = bf16[128,128,128]{2,1,0:T(8,128)(2,1)} async-done(((bf16[512,128,128]{2,1,0:T(8,128)(2,1)}), bf16[128,128,128]{2,1,0:T(8,128)(2,1)}) %reduce-scatter.2.cloned.1.call-update) | async-done | bytes 4194320 | tf_op jit(solution)/shard_map/reduce_scatter | solution.py:1542
  1041.5 15.7 %total.1 = f32[2,8,128]{2,1,0:T(8,128)} custom-call(bf16[128,128,128]{2,1,0:T(8,128)(2,1)} %reduce-scatter.2.cloned.1.call-done.slots_ref.refs_0_, f32[2,8,128]{2,1,0:T(8,128)} %scatter.13.more_ref), custom_call_target="tpu_custom_call" | custom-call | tf_op jit(solution)/shard_map/total/pallas_call | solution.py:861
  1060.0 63.1 %owner_step.1 = (f32[128,128,128]{2,1,0:T(8,128)}, bf16[128,128,128]{2,1,0:T(8,128)(2,1)}, f32[128,128,128]{2,1,0:T(8,128)}, f32[128,128,128]{2,1,0:T(8,128)}, f...) custom-call(f32[1,1]{1,0:T(1,128)} %bitcast.53.factor_ref, ...), custom_call_target="tpu_custom_call" | custom-call | tf_op jit(solution)/shard_map/owner_step/pallas_call | solution.py:1045
  (265 shorter events, 152.7 us)
Async XLA Ops:
  7.2 318.9 %all-gather.2.cloned.1.call-start = ((), (), s32[]{:S(2)}) async-start(), calls=%async_computation.3 | async-start | bytes 20971520 | tf_op jit(solution)/shard_map/all_gather | solution.py:1293
  13.8 15.1 %collective-permute-start.2 = (s32[2,1537]{1,0:T(2,128)S(1)}, s32[2,1537]{1,0:T(2,128)S(1)}, u32[]{:S(2)}, u32[]{:S(2)}) collective-permute-start(s32[2,1537]{1,0:T(2,128)S(1)} %pad_add_fusion.1), channel_id=1, source_target_pairs={{0,24},{8,16},{16,8},{24,0},{1,25},{9,17},{17,9},{25,1},{2,26},{10... | collective-permute-start | bytes 36896 | tf_op jit(solution)/shard_map/ppermute | solution.py:52
  19.0 10.0 collective-permute-start.1
  19.0 10.0 collective-permute-start
  74.8 7.2 collective-permute-start.3
  85.8 25.4 %collective-permute-start.4 = (bf16[2,2,256,512]{3,2,1,0:T(8,128)(2,1)S(1)}, bf16[2,2,256,512]{3,2,1,0:T(8,128)(2,1)}, u32[]{:S(2)}, u32[]{:S(2)}) collective-permute-start(bf16[2,2,256,512]{3,2,1,0:T(8,128)(2,1)S(1)} %slice.155), channel_id=1, source_target_pairs={{0,2},{1,3},{2,0},{3,1},{4,6},{5,7},{6,4},{7,5},{8,10},{9,11},{10,... | collective-permute-start | bytes 3145736 | tf_op jit(solution)/shard_map/ppermute | solution.py:52
  91.0 26.4 %collective-permute-start.7 = (bf16[2,2,256,512]{3,2,1,0:T(8,128)(2,1)}, bf16[2,2,256,512]{3,2,1,0:T(8,128)(2,1)}, u32[]{:S(2)}, u32[]{:S(2)}) collective-permute-start(bf16[2,2,256,512]{3,2,1,0:T(8,128)(2,1)} %slice.207), channel_id=1, source_target_pairs={{0,4},{1,5},{2,6},{3,7},{4,0},{5,1},{6,2},{7,3},{8,12},{9,13},{10,... | collective-permute-start | bytes 3145736 | tf_op jit(solution)/shard_map/ppermute | solution.py:52
  92.5 7.5 collective-permute-start.11
  93.7 6.3 collective-permute-start.12
  96.8 5.5 collective-permute-start.13
  112.8 14.6 %collective-permute-start.5 = (bf16[2,256,512]{2,1,0:T(8,128)(2,1)S(1)}, bf16[2,256,512]{2,1,0:T(8,128)(2,1)S(1)}, u32[]{:S(2)}, u32[]{:S(2)}) collective-permute-start(bf16[2,256,512]{2,1,0:T(8,128)(2,1)S(1)} %fusion.6), channel_id=1, source_target_pairs={{0,4},{1,5},{2,6},{3,7},{4,0},{5,1},{6,2},{7,3},{8,12},{9,13},{10,... | collective-permute-start | bytes 1572872 | tf_op jit(solution)/shard_map/ppermute | solution.py:52
  119.3 11.8 %collective-permute-start.8 = (bf16[2,256,512]{2,1,0:T(8,128)(2,1)S(1)}, bf16[2,256,512]{2,1,0:T(8,128)(2,1)S(1)}, u32[]{:S(2)}, u32[]{:S(2)}) collective-permute-start(bf16[2,256,512]{2,1,0:T(8,128)(2,1)S(1)} %fusion.7), channel_id=1, source_target_pairs={{0,2},{1,3},{2,0},{3,1},{4,6},{5,7},{6,4},{7,5},{8,10},{9,11},{10,... | collective-permute-start | bytes 1572872 | tf_op jit(solution)/shard_map/ppermute | solution.py:52
  127.5 28.9 %collective-permute-start.6 = (bf16[256,512]{1,0:T(8,128)(2,1)S(1)}, bf16[256,512]{1,0:T(8,128)(2,1)S(1)}, u32[]{:S(2)}, u32[]{:S(2)}) collective-permute-start(bf16[256,512]{1,0:T(8,128)(2,1)S(1)} %slice_bitcast_fusion.4), channel_id=1, source_target_pairs={{0,8},{8,0},{16,24},{24,16},{1,9},{9,1},{17,25},{25,17},{2,10},{10... | collective-permute-start | bytes 786440 | tf_op jit(solution)/shard_map/ppermute | solution.py:52
  131.3 25.2 %collective-permute-start.9 = (bf16[256,512]{1,0:T(8,128)(2,1)S(1)}, bf16[256,512]{1,0:T(8,128)(2,1)S(1)}, u32[]{:S(2)}, u32[]{:S(2)}) collective-permute-start(bf16[256,512]{1,0:T(8,128)(2,1)S(1)} %get-tuple-element.126), channel_id=1, source_target_pairs={{0,16},{8,24},{16,0},{24,8},{1,17},{9,25},{17,1},{25,9},{2,18},{10... | collective-permute-start | bytes 786440 | tf_op jit(solution)/shard_map/ppermute | solution.py:52
  133.3 32.6 %collective-permute-start.10 = (bf16[256,512]{1,0:T(8,128)(2,1)S(1)}, bf16[256,512]{1,0:T(8,128)(2,1)S(1)}, u32[]{:S(2)}, u32[]{:S(2)}) collective-permute-start(bf16[256,512]{1,0:T(8,128)(2,1)S(1)} %get-tuple-element.125), channel_id=1, source_target_pairs={{0,24},{8,16},{16,8},{24,0},{1,25},{9,17},{17,9},{25,1},{2,26},{10... | collective-permute-start | bytes 786440 | tf_op jit(solution)/shard_map/ppermute | solution.py:52
  167.6 23.6 %collective-permute-start.15 = (bf16[256,2048]{1,0:T(8,128)(2,1)S(1)}, bf16[256,2048]{1,0:T(8,128)(2,1)S(1)}, u32[]{:S(2)}, u32[]{:S(2)}) collective-permute-start(bf16[256,2048]{1,0:T(8,128)(2,1)S(1)} %get-tuple-element.120), channel_id=1, source_target_pairs={{0,4},{1,5},{2,6},{3,7},{4,0},{5,1},{6,2},{7,3},{8,12},{9,13},{10,... | collective-permute-start | bytes 3145736 | tf_op jit(solution)/shard_map/ppermute | solution.py:52
  169.1 24.1 %collective-permute-start.14 = (bf16[256,2048]{1,0:T(8,128)(2,1)S(1)}, bf16[256,2048]{1,0:T(8,128)(2,1)S(1)}, u32[]{:S(2)}, u32[]{:S(2)}) collective-permute-start(bf16[256,2048]{1,0:T(8,128)(2,1)S(1)} %get-tuple-element.120), channel_id=1, source_target_pairs={{0,2},{1,3},{2,0},{3,1},{4,6},{5,7},{6,4},{7,5},{8,10},{9,11},{10,... | collective-permute-start | bytes 3145736 | tf_op jit(solution)/shard_map/ppermute | solution.py:52
  191.2 12.4 %collective-permute-start.17 = (bf16[128,2048]{1,0:T(8,128)(2,1)S(1)}, bf16[128,2048]{1,0:T(8,128)(2,1)S(1)}, u32[]{:S(2)}, u32[]{:S(2)}) collective-permute-start(bf16[128,2048]{1,0:T(8,128)(2,1)S(1)} %slice.214), channel_id=1, source_target_pairs={{0,2},{1,3},{2,0},{3,1},{4,6},{5,7},{6,4},{7,5},{8,10},{9,11},{10,... | collective-permute-start | bytes 1572872 | tf_op jit(solution)/shard_map/ppermute | solution.py:52
  193.2 10.6 collective-permute-start.16
  204.5 7.2 collective-permute-start.18
  326.1 144.2 %all-to-all-start = ((bf16[4,1536,512]{2,1,0:T(8,128)(2,1)}), bf16[4,1536,512]{2,1,0:T(8,128)(2,1)}, u32[]{:S(2)}, u32[]{:S(2)}) async-start(bf16[4,1536,512]{2,1,0:T(8,128)(2,1)} %bitcast.122), calls=%async_computation | async-start | bytes 12582912 | tf_op jit(solution)/shard_map/all_to_all | solution.py:1356
  618.5 141.2 %all-to-all-start.1 = ((bf16[4,1152,512]{2,1,0:T(8,128)(2,1)}), bf16[4,1152,512]{2,1,0:T(8,128)(2,1)}, u32[]{:S(2)}, u32[]{:S(2)}) async-start(bf16[4,1152,512]{2,1,0:T(8,128)(2,1)} %get-tuple-element.94), calls=%async_computation.1 | async-start | bytes 9437184 | tf_op jit(solution)/shard_map/all_to_all | solution.py:1483
  625.5 416.0 %reduce-scatter.2.cloned.1.call-start = ((), (), s32[]{:S(2)}) async-start(), calls=%async_computation.4 | async-start | bytes 20971520 | tf_op jit(solution)/shard_map/reduce_scatter | solution.py:1542
  761.0 25.1 %collective-permute-start.19 = (bf16[1024,512]{1,0:T(8,128)(2,1)S(1)}, bf16[1024,512]{1,0:T(8,128)(2,1)S(1)}, u32[]{:S(2)}, u32[]{:S(2)}) collective-permute-start(bf16[1024,512]{1,0:T(8,128)(2,1)S(1)} %bitcast.125), channel_id=1, source_target_pairs={{0,2},{1,3},{2,0},{3,1},{4,6},{5,7},{6,4},{7,5},{8,10},{9,11},{10,... | collective-permute-start | bytes 3145736 | tf_op jit(solution)/shard_map/ppermute | solution.py:52
  762.5 25.2 %collective-permute-start.20 = (bf16[1024,512]{1,0:T(8,128)(2,1)S(1)}, bf16[1024,512]{1,0:T(8,128)(2,1)S(1)}, u32[]{:S(2)}, u32[]{:S(2)}) collective-permute-start(bf16[1024,512]{1,0:T(8,128)(2,1)S(1)} %bitcast.126), channel_id=1, source_target_pairs={{0,4},{1,5},{2,6},{3,7},{4,0},{5,1},{6,2},{7,3},{8,12},{9,13},{10,... | collective-permute-start | bytes 3145736 | tf_op jit(solution)/shard_map/ppermute | solution.py:52
  786.1 13.1 %collective-permute-start.21 = (bf16[512,512]{1,0:T(8,128)(2,1)S(1)}, bf16[512,512]{1,0:T(8,128)(2,1)S(1)}, u32[]{:S(2)}, u32[]{:S(2)}) collective-permute-start(bf16[512,512]{1,0:T(8,128)(2,1)S(1)} %slice.218), channel_id=1, source_target_pairs={{0,4},{1,5},{2,6},{3,7},{4,0},{5,1},{6,2},{7,3},{8,12},{9,13},{10,... | collective-permute-start | bytes 1572872 | tf_op jit(solution)/shard_map/ppermute | solution.py:52
  787.8 12.9 %collective-permute-start.22 = (bf16[512,512]{1,0:T(8,128)(2,1)S(1)}, bf16[512,512]{1,0:T(8,128)(2,1)S(1)}, u32[]{:S(2)}, u32[]{:S(2)}) collective-permute-start(bf16[512,512]{1,0:T(8,128)(2,1)S(1)} %slice.219), channel_id=1, source_target_pairs={{0,2},{1,3},{2,0},{3,1},{4,6},{5,7},{6,4},{7,5},{8,10},{9,11},{10,... | collective-permute-start | bytes 1572872 | tf_op jit(solution)/shard_map/ppermute | solution.py:52
  803.9 33.8 %collective-permute-start.23 = (bf16[4,1024,512]{2,1,0:T(8,128)(2,1)}, bf16[4,1024,512]{2,1,0:T(8,128)(2,1)}, u32[]{:S(2)}, u32[]{:S(2)}) collective-permute-start(bf16[4,1024,512]{2,1,0:T(8,128)(2,1)} %pad_maximum_fusion.2), channel_id=1, source_target_pairs={{0,1},{1,0},{2,3},{3,2},{4,5},{5,4},{6,7},{7,6},{8,9},{9,8},{10,11... | collective-permute-start | bytes 12582920 | tf_op jit(solution)/shard_map/ppermute | solution.py:52
  804.1 6.7 collective-permute-start.24
  810.8 4.0 collective-permute-start.25
  818.8 6.1 collective-permute-start.27
  824.9 7.2 collective-permute-start.28
  (27 other events, 766.6 us)
Sparse Core Ops, SparseCore 0:
  13.8 312.2 all-gather.1
  759.9 281.5 reduce-scatter.1

commit v2 on v1

--- a/solution.py
+++ b/solution.py
@@ -147,7 +147,7 @@
     partners += [{"dp": a ^ o} for o in range(1, n_dp)]
     for partner in partners:
         pl.semaphore_signal(barrier, 1, device_id=partner, device_id_type=pl.DeviceIdType.MESH)
-    pl.semaphore_wait(barrier, len(partners))
+    return lambda: pl.semaphore_wait(barrier, len(partners))
 
 
 def by_rows(count, step):
@@ -348,12 +348,13 @@
 
 def attend_sum_kernel(o, wout, res, gain, x_out, out, *refs):
     *_, parts, mine, sems = refs
-    greet(1)
+    met = greet(1)
 
     def make(c):
         parts[:, :, c] = mm(flat(o[...]), wout[:, c]).astype(BF16).reshape(8, -1, c.size)
 
     by_columns(make)
+    met()
     mine[...] = forward_step(refs, res, gain, x_out)
     PlaneSpread(mine, out, sems, 7, 0, mine.shape[0]).run()
 
@@ -361,7 +362,7 @@
 def units_sum_kernel(h2, wgate, wdown, res, gain, x_out, gate_up, hidden, out, *refs):
     *_, parts, _, _ = refs
     units = wdown.shape[0]
-    greet(1)
+    met = greet(1)
     x = flat(h2[...])
     step = min(units, 512)
     for c in range(2 * units // step):
@@ -376,6 +377,7 @@
         parts[:, :, c] = mm(hidden[...], wdown[:, c]).astype(BF16).reshape(8, -1, c.size)
 
     by_columns(make)
+    met()
     out[...] = forward_step(refs, res, gain, x_out)
 
 
@@ -394,7 +396,7 @@
     ]
     for copy in loads:
         copy.start()
-    greet(1)
+    met = greet(1)
     x = flat(down_in[...])
     step = min(units, 512)
     for c in range(units // step):
@@ -430,6 +432,7 @@
 
     for copy in loads:
         copy.wait()
+    met()
     PlaneSum(parts, own, core, held, near, last, sems, 0, 1).run(fill)
     dx, dg = norm_back_step(own[...], x_in[...], gain[...])
     dx = dx + res[...]
@@ -451,7 +454,7 @@
     store = pltpu.make_async_copy(final, final_out, own_sems.at[1])
     load.start()
     a = lax.axis_index("dp")
-    greet(n_dp, range(1, 8))
+    greet(n_dp, range(1, 8))()
     mine[pl.ds(0, rows)] = rows_ref[...]
     block = [pl.ds(o * rows, rows) for o in range(4)]
     across = [
@@ -580,7 +583,7 @@
     _, vocab, wide = head.shape
     load = pltpu.make_async_copy(final_ref, final, own_sem)
     load.start()
-    greet(n_dp)
+    met = greet(n_dp)
     plan = PlaneSum(parts, own, core, held, near, last, sems, 0, n_dp)
 
     def make(b):
@@ -589,6 +592,8 @@
         for p in range(n_dp):
             value = mm(x, head[p]).astype(BF16)
             parts[:, part, pl.ds(p * wide, wide)] = value.reshape(8, rows, wide)
+        if b == 2:
+            met()
         plan.at_core[b].start()
 
     def table_part(p, first, number):
@@ -686,7 +691,7 @@
     a = lax.axis_index("dp")
     load = pltpu.make_async_copy(h1_ref, h1, h1_sem)
     load.start()
-    greet(n_dp)
+    met = greet(n_dp)
     plan = PlaneSum(parts, own, core, held, near, last, sems, 0, blocks)
     sent = []
 
@@ -696,6 +701,8 @@
         for c in range(D // 512):
             value = mm(x, wqkv[pl.ds(c * 512, 512), :], CONTRACT_LAST).astype(BF16)
             parts[:, part, pl.ds(c * 512, 512)] = value.reshape(8, rows, 512)
+        if b == 0:
+            met()
         plan.at_core[b].start()
 
     left = list(range(D // 512))
@@ -831,7 +838,7 @@
 def total_kernel(n_dp, slots_ref, more_ref, out_ref, plane, line, sems):
     me = lax.axis_index("mp")
     a = lax.axis_index("dp")
-    greet(n_dp, range(1, 8))
+    met = greet(n_dp, range(1, 8))
 
     def add(k, have):
         g = slots_ref[pl.ds(k * 8, 8)].astype(F32)
@@ -840,6 +847,7 @@
     start = jnp.zeros((8, 128), F32)
     plane[me, 0] = lax.fori_loop(0, slots_ref.shape[0] // 8, add, start) + more_ref[0]
     plane[me, 1] = more_ref[1]
+    met()
     copies = [peer_copy(plane.at[me], plane.at[me], sems, k - 1, mp=me ^ k) for k in range(1, 8)]
     for copy in copies:
         copy.start()

time: 1140 us -> 1140 us (level)
  no operation moved by 1% of the time
where the time goes in v2:
time: 1140 us; the launch traced here: 1130 us
  Pallas kernels  441 us (39%)
  waiting for transfers between devices  400 us (35%)
  other arithmetic  132 us (12%)
  local copies, waits for them, and re-layouts  87.2 us (8%)
  starting transfers between devices  45 us (4%)
  between operations  21.6 us (2%)
    pallas_call x5, Pallas kernels, exchange(): pl.pallas_call(kernel, out_shape=[jax.ShapeDtypeStruct(shape, dtype) for...  240 us
    ppermute x29, waiting for transfers between devices, swap(): return lax.ppermute(x, axis, [(i, i ^ bit) for i in range(n)])  154 us
    reduce_scatter x1, waiting for transfers between devices, body(): own_slots = lax.psum_scatter(slots, 'dp', scatter_dimension=0, tiled=True)  112 us
    all_gather x1, waiting for transfers between devices, body(): lax.all_gather(block_master[0].astype(BF16), 'dp', axis=0, tiled=True)  112 us
    pallas_call x1, Pallas kernels, head_call(): pl.pallas_call(functools.partial(head_kernel, n_dp), out_shape=[jax.Shape...  74.5 us
    pallas_call x1, Pallas kernels, owner_step(): pl.pallas_call(functools.partial(owner_step_kernel, steps), grid=(steps +...  63.1 us
    scatter-add x1, other arithmetic, body(): table_grad.reshape(vocab_part, cols).astype(F32).at[safe.reshape(-1)]  59.6 us
    gather x1, local copies, waits for them, and re-layouts, body(): looked = jnp.where(valid[..., None], jnp.take(table_low, safe, axis=0), 0)  38.1 us
  transfers between devices with their start and end apart: 33, of which 25 were waited for; matrix products, arithmetic and copies ran while one was open for 18% of the time, Pallas kernels for 19%

profile of v2, /device:TPU:0, one launch (start us, length us, event | category | flops | bytes accessed | tf_op | source)
XLA Modules:
  0.0 1127.0 jit_solution(522865352180889766)
XLA Ops:
  7.3 6.4 bitcast_convert_fusion.1
  19.6 9.3 convert_element_type.95.refs_0_
  31.1 38.1 %gather_fusion.2 = bf16[8192,512]{1,0:T(8,128)(2,1)} fusion(bf16[6144,512]{1,0:T(8,128)(2,1)} %convert_element_type.95.refs_0_, s32[8192]{0:T(1024)S(1)} %broadcast_clamp_fusion), kind=kCustom, calls=%fused_computation.2 | custom fusion | bytes 16809984 | tf_op jit(solution)/shard_map/jit(_take)/gather | solution.py:1350
  74.9 7.1 collective-permute-done.3
  102.3 8.8 collective-permute-done.4
  120.0 7.3 collective-permute-done.5
  135.3 21.2 %collective-permute-done.6 = bf16[256,512]{1,0:T(8,128)(2,1)S(1)} collective-permute-done((bf16[256,512]{1,0:T(8,128)(2,1)S(1)}, bf16[256,512]{1,0:T(8,128)(2,1)S(1)}, u32[]{:S(2)}, u32[]{:S(2)}) %collective-permute-start.6) | collective-permute-done | bytes 262176 | tf_op jit(solution)/shard_map/ppermute | solution.py:52
  156.6 9.4 collective-permute-done.10
  169.5 21.6 %collective-permute-done.15 = bf16[256,2048]{1,0:T(8,128)(2,1)S(1)} collective-permute-done((bf16[256,2048]{1,0:T(8,128)(2,1)S(1)}, bf16[256,2048]{1,0:T(8,128)(2,1)S(1)}, u32[]{:S(2)}, u32[]{:S(2)}) %collective-permute-start.15) | collective-permute-done | bytes 1048608 | tf_op jit(solution)/shard_map/ppermute | solution.py:52
  193.3 10.4 collective-permute-done.17
  214.1 112.0 %all-gather.2.cloned.1.call-done.slots_ref.refs_1_ = bf16[512,128,128]{2,1,0:T(8,128)(2,1)} async-done(((bf16[128,128,128]{2,1,0:T(8,128)(2,1)}), bf16[512,128,128]{2,1,0:T(8,128)(2,1)}) %all-gather.2.cloned.1.call-update) | async-done | bytes 16777232 | tf_op jit(solution)/shard_map/all_gather | solution.py:1301
  357.3 9.0 place_tiles.1
  371.0 19.3 %attend.1 = (bf16[8,64,256]{2,1,0:T(8,128)(2,1)}, bf16[8,64,256]{2,1,0:T(8,128)(2,1)}, bf16[8,256,256]{2,1,0:T(8,128)(2,1)}, bf16[8,256,256]{2,1,0:T(8,128)(2,1)}) custom-call(bf16[8,256,2048]{2,1,0:T(8,128)(2,1)} %constant_dynamic-update-slice_fusion.h1_ref.refs_2_, bf16[2048,768]{1,0:T(8,128)(2,1)} %copy-done.1, ...), custom_call_target="tpu_custom_call" | custom-call | bytes 1024 | tf_op jit(solution)/shard_map/attend/pallas_call | solution.py:1237
  390.4 29.8 %attend_sum.1 = (f32[64,2048]{1,0:T(8,128)}, bf16[8,64,2048]{2,1,0:T(8,128)(2,1)}) custom-call(bf16[8,64,256]{2,1,0:T(8,128)(2,1)} %get-tuple-element.72.o, bf16[256,2048]{1,0:T(8,128)(2,1)} %copy-done.2, f32[64,2048]{1,0:T(8,128)} %slice.215.res, f32[1,2048]{1,0:T(1,128)} %get-tuple-element.133.gain), custom_call_target="tpu_custom_call" | custom-call | bytes 1024 | tf_op jit(solution)/shard_map/attend_sum/pallas_call | solution.py:775
  420.1 28.9 %units_sum.1 = (f32[64,2048]{1,0:T(8,128)}, f32[512,2048]{1,0:T(8,128)}, bf16[512,1024]{1,0:T(8,128)(2,1)}, bf16[64,2048]{1,0:T(8,128)(2,1)}) custom-call(bf16[8,64,2048]{2,1,0:T(8,128)(2,1)} %get-tuple-element.74.h2.h2_ref, bf16[2048,2048]{1,0:T(8,128)(2,1)} %get-tuple-element.75.wgate, bf16[1024,2048]{1,0:T(8,128)(2,1)} %copy-done, ...), custom_call_target="tpu_custom_call" | custom-call | bytes 1024 | tf_op jit(solution)/shard_map/units_sum/pallas_call | solution.py:775
  449.0 21.3 %all-to-all-done.refs_0_.head = bf16[4,1536,512]{2,1,0:T(8,128)(2,1)} async-done(((bf16[4,1536,512]{2,1,0:T(8,128)(2,1)}), bf16[4,1536,512]{2,1,0:T(8,128)(2,1)}, u32[]{:S(2)}, u32[]{:S(2)}) %all-to-all-start) | async-done | bytes 6291488 | tf_op jit(solution)/shard_map/all_to_all | solution.py:1364
  470.3 74.5 %head.1 = (bf16[8,256,2048]{2,1,0:T(8,128)(2,1)}, bf16[8,256,1536]{2,1,0:T(8,128)(2,1)}, f32[2,4,512]{2,1,0:T(4,128)}) custom-call(bf16[64,2048]{1,0:T(8,128)(2,1)} %get-tuple-element.78.rows_ref, s32[4,512,1]{2,1,0:T(8,128)} %reshape.503.target_ref, f32[4,512,1]{2,1,0:T(8,128)} %reshape.504.scale_ref, bf16[4,1536,512]{2,1,0:T(8,128)(2,1)} %all-to-all-done.refs_0_.head), custom_call_target="tpu_custom_call" | custom-call | bytes 1048576 | tf_op jit(solution)/shard_map/head/pallas_call | solution.py:552
  544.8 70.9 %head_sum.1 = (f32[64,2048]{1,0:T(8,128)}, f32[1,2048]{1,0:T(1,128)}, bf16[8,64,2048]{2,1,0:T(8,128)(2,1)}, bf16[4,384,512]{2,1,0:T(8,128)(2,1)}, bf16[4,1152,512]{2,1,0:T(8,128)(2,1)}) custom-call(bf16[8,256,1536]{2,1,0:T(8,128)(2,1)} %get-tuple-element.79.dlogits, bf16[4,1536,512]{2,1,0:T(8,128)(2,1)} %all-to-all-done.refs_0_.head, ...), custom_call_target="tpu_custom_call" | custom-call | bytes 1024 | tf_op jit(solution)/shard_map/head_sum/pallas_call | solution.py:775
  615.7 8.1 all-to-all-start.1
  625.4 41.3 %gate_sum.1 = (f32[64,2048]{1,0:T(8,128)}, f32[1,2048]{1,0:T(1,128)}, bf16[512,2048]{1,0:T(8,128)(2,1)}, bf16[8,64,2048]{2,1,0:T(8,128)(2,1)}, bf16[1024,2048]{1,0:T(8,128)(2,1)}, /*index=5*/bf16[2048,2048]{1,0:T(8,128)(2,1)}) custom-call(bf16[8,64,2048]{2,1,0:T(8,128)(2,1)} %get-tuple-element.82.down_in, bf16[1024,2048]{1,0:T(8,128)(2,1)} %copy-done, ...), custom_call_target="tpu_custom_call" | custom-call | bytes 1024 | tf_op jit(solution)/shard_map/gate_sum/pallas_call | solution.py:775
  666.7 17.8 %attend_back.1 = (bf16[8,256,768]{2,1,0:T(8,128)(2,1)}, bf16[256,2048]{1,0:T(8,128)(2,1)}, bf16[512,128,128]{2,1,0:T(8,128)(2,1)}) custom-call(s32[512]{0:T(512)} %copy-done.5, bf16[8,64,256]{2,1,0:T(8,128)(2,1)} %get-tuple-element.69.refs_0_, bf16[8,256,256]{2,1,0:T(8,128)(2,1)} %get-tuple-element.70.refs_1_, ...), custom_call_target="tpu_custom_call" | custom-call | bytes 1024 | tf_op jit(solution)/shard_map/attend_back/pallas_call | solution.py:1218
  684.5 69.2 %input_sum.1 = (bf16[4,256,512]{2,1,0:T(8,128)(2,1)}, f32[1,2048]{1,0:T(1,128)}, bf16[2048,768]{1,0:T(8,128)(2,1)}) custom-call(bf16[8,256,768]{2,1,0:T(8,128)(2,1)} %get-tuple-element.89.dqkv, bf16[2048,768]{1,0:T(8,128)(2,1)} %copy-done.1, f32[256,2048]{1,0:T(8,128)} %convert_element_type.107.x_in, f32[1,2048]{1,0:T(1,128)} %copy-done.11, ...), custom_call_target="tpu_custom_call" | custom-call | bytes 1024 | tf_op jit(solution)/shard_map/input_sum/pallas_call | solution.py:775
  761.5 23.1 %collective-permute-done.19 = bf16[1024,512]{1,0:T(8,128)(2,1)S(1)} collective-permute-done((bf16[1024,512]{1,0:T(8,128)(2,1)S(1)}, bf16[1024,512]{1,0:T(8,128)(2,1)S(1)}, u32[]{:S(2)}, u32[]{:S(2)}) %collective-permute-start.19) | collective-permute-done | bytes 1048608 | tf_op jit(solution)/shard_map/ppermute | solution.py:52
  786.8 10.8 collective-permute-done.21
  803.2 6.1 collective-permute-done.24
  839.7 7.6 bitcast_select_fusion
  850.1 6.7 bitcast_convert_fusion
  856.9 59.6 %scatter_custom_fusion.1.refs_6_ = f32[6144,512]{1,0:T(8,128)} fusion(f32[6144,512]{1,0:T(8,128)} %bitcast_convert_fusion, s32[8192]{0:T(1024)S(1)} %bitcast.159, bf16[8192,512]{1,0:T(8,128)(2,1)} %bitcast_select_fusion), kind=kCustom, calls=%fused_computation.8 | custom fusion | flops 8388608 | bytes 20971520 | tf_op jit(solution)/shard_map/scatter-add | solution.py:1556
  916.5 8.5 multiply_reduce_fusion
  926.5 112.3 %reduce-scatter.2.cloned.1.call-done.slots_ref.refs_0_ = bf16[128,128,128]{2,1,0:T(8,128)(2,1)} async-done(((bf16[512,128,128]{2,1,0:T(8,128)(2,1)}), bf16[128,128,128]{2,1,0:T(8,128)(2,1)}) %reduce-scatter.2.cloned.1.call-update) | async-done | bytes 4194320 | tf_op jit(solution)/shard_map/reduce_scatter | solution.py:1550
  1038.8 14.2 %total.1 = f32[2,8,128]{2,1,0:T(8,128)} custom-call(bf16[128,128,128]{2,1,0:T(8,128)(2,1)} %reduce-scatter.2.cloned.1.call-done.slots_ref.refs_0_, f32[2,8,128]{2,1,0:T(8,128)} %scatter.13.more_ref), custom_call_target="tpu_custom_call" | custom-call | tf_op jit(solution)/shard_map/total/pallas_call | solution.py:869
  1055.8 63.1 %owner_step.1 = (f32[128,128,128]{2,1,0:T(8,128)}, bf16[128,128,128]{2,1,0:T(8,128)(2,1)}, f32[128,128,128]{2,1,0:T(8,128)}, f32[128,128,128]{2,1,0:T(8,128)}, f...) custom-call(f32[1,1]{1,0:T(1,128)} %bitcast.53.factor_ref, ...), custom_call_target="tpu_custom_call" | custom-call | tf_op jit(solution)/shard_map/owner_step/pallas_call | solution.py:1053
  (265 shorter events, 151.6 us)
Async XLA Ops:
  7.2 318.9 %all-gather.2.cloned.1.call-start = ((), (), s32[]{:S(2)}) async-start(), calls=%async_computation.3 | async-start | bytes 20971520 | tf_op jit(solution)/shard_map/all_gather | solution.py:1301
  13.8 15.1 %collective-permute-start.2 = (s32[2,1537]{1,0:T(2,128)S(1)}, s32[2,1537]{1,0:T(2,128)S(1)}, u32[]{:S(2)}, u32[]{:S(2)}) collective-permute-start(s32[2,1537]{1,0:T(2,128)S(1)} %pad_add_fusion.1), channel_id=1, source_target_pairs={{0,24},{8,16},{16,8},{24,0},{1,25},{9,17},{17,9},{25,1},{2,26},{10... | collective-permute-start | bytes 36896 | tf_op jit(solution)/shard_map/ppermute | solution.py:52
  19.0 10.0 collective-permute-start.1
  19.0 10.0 collective-permute-start
  74.8 7.2 collective-permute-start.3
  85.8 25.4 %collective-permute-start.4 = (bf16[2,2,256,512]{3,2,1,0:T(8,128)(2,1)S(1)}, bf16[2,2,256,512]{3,2,1,0:T(8,128)(2,1)}, u32[]{:S(2)}, u32[]{:S(2)}) collective-permute-start(bf16[2,2,256,512]{3,2,1,0:T(8,128)(2,1)S(1)} %slice.155), channel_id=1, source_target_pairs={{0,2},{1,3},{2,0},{3,1},{4,6},{5,7},{6,4},{7,5},{8,10},{9,11},{10,... | collective-permute-start | bytes 3145736 | tf_op jit(solution)/shard_map/ppermute | solution.py:52
  91.0 26.4 %collective-permute-start.7 = (bf16[2,2,256,512]{3,2,1,0:T(8,128)(2,1)}, bf16[2,2,256,512]{3,2,1,0:T(8,128)(2,1)}, u32[]{:S(2)}, u32[]{:S(2)}) collective-permute-start(bf16[2,2,256,512]{3,2,1,0:T(8,128)(2,1)} %slice.207), channel_id=1, source_target_pairs={{0,4},{1,5},{2,6},{3,7},{4,0},{5,1},{6,2},{7,3},{8,12},{9,13},{10,... | collective-permute-start | bytes 3145736 | tf_op jit(solution)/shard_map/ppermute | solution.py:52
  92.5 7.5 collective-permute-start.11
  93.7 6.3 collective-permute-start.12
  96.8 5.5 collective-permute-start.13
  112.8 14.6 %collective-permute-start.5 = (bf16[2,256,512]{2,1,0:T(8,128)(2,1)S(1)}, bf16[2,256,512]{2,1,0:T(8,128)(2,1)S(1)}, u32[]{:S(2)}, u32[]{:S(2)}) collective-permute-start(bf16[2,256,512]{2,1,0:T(8,128)(2,1)S(1)} %fusion.6), channel_id=1, source_target_pairs={{0,4},{1,5},{2,6},{3,7},{4,0},{5,1},{6,2},{7,3},{8,12},{9,13},{10,... | collective-permute-start | bytes 1572872 | tf_op jit(solution)/shard_map/ppermute | solution.py:52
  119.3 11.8 %collective-permute-start.8 = (bf16[2,256,512]{2,1,0:T(8,128)(2,1)S(1)}, bf16[2,256,512]{2,1,0:T(8,128)(2,1)S(1)}, u32[]{:S(2)}, u32[]{:S(2)}) collective-permute-start(bf16[2,256,512]{2,1,0:T(8,128)(2,1)S(1)} %fusion.7), channel_id=1, source_target_pairs={{0,2},{1,3},{2,0},{3,1},{4,6},{5,7},{6,4},{7,5},{8,10},{9,11},{10,... | collective-permute-start | bytes 1572872 | tf_op jit(solution)/shard_map/ppermute | solution.py:52
  127.5 28.9 %collective-permute-start.6 = (bf16[256,512]{1,0:T(8,128)(2,1)S(1)}, bf16[256,512]{1,0:T(8,128)(2,1)S(1)}, u32[]{:S(2)}, u32[]{:S(2)}) collective-permute-start(bf16[256,512]{1,0:T(8,128)(2,1)S(1)} %slice_bitcast_fusion.4), channel_id=1, source_target_pairs={{0,8},{8,0},{16,24},{24,16},{1,9},{9,1},{17,25},{25,17},{2,10},{10... | collective-permute-start | bytes 786440 | tf_op jit(solution)/shard_map/ppermute | solution.py:52
  131.3 25.2 %collective-permute-start.9 = (bf16[256,512]{1,0:T(8,128)(2,1)S(1)}, bf16[256,512]{1,0:T(8,128)(2,1)S(1)}, u32[]{:S(2)}, u32[]{:S(2)}) collective-permute-start(bf16[256,512]{1,0:T(8,128)(2,1)S(1)} %get-tuple-element.126), channel_id=1, source_target_pairs={{0,16},{8,24},{16,0},{24,8},{1,17},{9,25},{17,1},{25,9},{2,18},{10... | collective-permute-start | bytes 786440 | tf_op jit(solution)/shard_map/ppermute | solution.py:52
  133.3 32.6 %collective-permute-start.10 = (bf16[256,512]{1,0:T(8,128)(2,1)S(1)}, bf16[256,512]{1,0:T(8,128)(2,1)S(1)}, u32[]{:S(2)}, u32[]{:S(2)}) collective-permute-start(bf16[256,512]{1,0:T(8,128)(2,1)S(1)} %get-tuple-element.125), channel_id=1, source_target_pairs={{0,24},{8,16},{16,8},{24,0},{1,25},{9,17},{17,9},{25,1},{2,26},{10... | collective-permute-start | bytes 786440 | tf_op jit(solution)/shard_map/ppermute | solution.py:52
  167.6 23.6 %collective-permute-start.15 = (bf16[256,2048]{1,0:T(8,128)(2,1)S(1)}, bf16[256,2048]{1,0:T(8,128)(2,1)S(1)}, u32[]{:S(2)}, u32[]{:S(2)}) collective-permute-start(bf16[256,2048]{1,0:T(8,128)(2,1)S(1)} %get-tuple-element.120), channel_id=1, source_target_pairs={{0,4},{1,5},{2,6},{3,7},{4,0},{5,1},{6,2},{7,3},{8,12},{9,13},{10,... | collective-permute-start | bytes 3145736 | tf_op jit(solution)/shard_map/ppermute | solution.py:52
  169.1 24.1 %collective-permute-start.14 = (bf16[256,2048]{1,0:T(8,128)(2,1)S(1)}, bf16[256,2048]{1,0:T(8,128)(2,1)S(1)}, u32[]{:S(2)}, u32[]{:S(2)}) collective-permute-start(bf16[256,2048]{1,0:T(8,128)(2,1)S(1)} %get-tuple-element.120), channel_id=1, source_target_pairs={{0,2},{1,3},{2,0},{3,1},{4,6},{5,7},{6,4},{7,5},{8,10},{9,11},{10,... | collective-permute-start | bytes 3145736 | tf_op jit(solution)/shard_map/ppermute | solution.py:52
  191.2 12.4 %collective-permute-start.17 = (bf16[128,2048]{1,0:T(8,128)(2,1)S(1)}, bf16[128,2048]{1,0:T(8,128)(2,1)S(1)}, u32[]{:S(2)}, u32[]{:S(2)}) collective-permute-start(bf16[128,2048]{1,0:T(8,128)(2,1)S(1)} %slice.214), channel_id=1, source_target_pairs={{0,2},{1,3},{2,0},{3,1},{4,6},{5,7},{6,4},{7,5},{8,10},{9,11},{10,... | collective-permute-start | bytes 1572872 | tf_op jit(solution)/shard_map/ppermute | solution.py:52
  193.2 10.6 collective-permute-start.16
  204.5 7.2 collective-permute-start.18
  326.1 144.2 %all-to-all-start = ((bf16[4,1536,512]{2,1,0:T(8,128)(2,1)}), bf16[4,1536,512]{2,1,0:T(8,128)(2,1)}, u32[]{:S(2)}, u32[]{:S(2)}) async-start(bf16[4,1536,512]{2,1,0:T(8,128)(2,1)} %bitcast.122), calls=%async_computation | async-start | bytes 12582912 | tf_op jit(solution)/shard_map/all_to_all | solution.py:1364
  615.7 142.6 %all-to-all-start.1 = ((bf16[4,1152,512]{2,1,0:T(8,128)(2,1)}), bf16[4,1152,512]{2,1,0:T(8,128)(2,1)}, u32[]{:S(2)}, u32[]{:S(2)}) async-start(bf16[4,1152,512]{2,1,0:T(8,128)(2,1)} %get-tuple-element.94), calls=%async_computation.1 | async-start | bytes 9437184 | tf_op jit(solution)/shard_map/all_to_all | solution.py:1491
  623.8 415.0 %reduce-scatter.2.cloned.1.call-start = ((), (), s32[]{:S(2)}) async-start(), calls=%async_computation.4 | async-start | bytes 20971520 | tf_op jit(solution)/shard_map/reduce_scatter | solution.py:1550
  759.5 25.0 %collective-permute-start.19 = (bf16[1024,512]{1,0:T(8,128)(2,1)S(1)}, bf16[1024,512]{1,0:T(8,128)(2,1)S(1)}, u32[]{:S(2)}, u32[]{:S(2)}) collective-permute-start(bf16[1024,512]{1,0:T(8,128)(2,1)S(1)} %bitcast.125), channel_id=1, source_target_pairs={{0,2},{1,3},{2,0},{3,1},{4,6},{5,7},{6,4},{7,5},{8,10},{9,11},{10,... | collective-permute-start | bytes 3145736 | tf_op jit(solution)/shard_map/ppermute | solution.py:52
  760.9 25.2 %collective-permute-start.20 = (bf16[1024,512]{1,0:T(8,128)(2,1)S(1)}, bf16[1024,512]{1,0:T(8,128)(2,1)S(1)}, u32[]{:S(2)}, u32[]{:S(2)}) collective-permute-start(bf16[1024,512]{1,0:T(8,128)(2,1)S(1)} %bitcast.126), channel_id=1, source_target_pairs={{0,4},{1,5},{2,6},{3,7},{4,0},{5,1},{6,2},{7,3},{8,12},{9,13},{10,... | collective-permute-start | bytes 3145736 | tf_op jit(solution)/shard_map/ppermute | solution.py:52
  784.6 13.1 %collective-permute-start.21 = (bf16[512,512]{1,0:T(8,128)(2,1)S(1)}, bf16[512,512]{1,0:T(8,128)(2,1)S(1)}, u32[]{:S(2)}, u32[]{:S(2)}) collective-permute-start(bf16[512,512]{1,0:T(8,128)(2,1)S(1)} %slice.218), channel_id=1, source_target_pairs={{0,4},{1,5},{2,6},{3,7},{4,0},{5,1},{6,2},{7,3},{8,12},{9,13},{10,... | collective-permute-start | bytes 1572872 | tf_op jit(solution)/shard_map/ppermute | solution.py:52
  786.1 13.0 %collective-permute-start.22 = (bf16[512,512]{1,0:T(8,128)(2,1)S(1)}, bf16[512,512]{1,0:T(8,128)(2,1)S(1)}, u32[]{:S(2)}, u32[]{:S(2)}) collective-permute-start(bf16[512,512]{1,0:T(8,128)(2,1)S(1)} %slice.219), channel_id=1, source_target_pairs={{0,2},{1,3},{2,0},{3,1},{4,6},{5,7},{6,4},{7,5},{8,10},{9,11},{10,... | collective-permute-start | bytes 1572872 | tf_op jit(solution)/shard_map/ppermute | solution.py:52
  802.4 32.5 %collective-permute-start.23 = (bf16[4,1024,512]{2,1,0:T(8,128)(2,1)}, bf16[4,1024,512]{2,1,0:T(8,128)(2,1)}, u32[]{:S(2)}, u32[]{:S(2)}) collective-permute-start(bf16[4,1024,512]{2,1,0:T(8,128)(2,1)} %pad_maximum_fusion.2), channel_id=1, source_target_pairs={{0,1},{1,0},{2,3},{3,2},{4,5},{5,4},{6,7},{7,6},{8,9},{9,8},{10,11... | collective-permute-start | bytes 12582920 | tf_op jit(solution)/shard_map/ppermute | solution.py:52
  802.6 6.7 collective-permute-start.24
  809.3 4.0 collective-permute-start.25
  817.3 5.1 collective-permute-start.27
  822.5 6.9 collective-permute-start.28
  (27 other events, 768.3 us)
Sparse Core Ops, SparseCore 0:
  13.8 312.2 all-gather.1
  758.5 280.2 reduce-scatter.1

commit v3 on v2

--- a/solution.py
+++ b/solution.py
@@ -445,12 +445,15 @@
         copy.wait()
 
 
-def head_kernel(n_dp, rows_ref, target_ref, scale_ref, *refs):
-    head_ref, final_out, dlogits_out, seen, final, head, mine, logits, *refs = refs
+def head_kernel(n_dp, rows_ref, target_ref, scale_ref, late_ref, *refs):
+    head_ref, final_out, dlogits_out, head_out, seen, final, head, mine, logits, *refs = refs
     stats, plane, mid, line, dlogits, sems, own_sems = refs
     rows, vocab = rows_ref.shape[0], logits.shape[2]
     wide = head.shape[2]
-    load = pltpu.make_async_copy(head_ref, head, own_sems.at[0])
+    count = late_ref.shape[1]
+    soon, late = pl.ds(0, vocab - count), pl.ds(vocab - count, count)
+    load = pltpu.make_async_copy(head_ref, head.at[:, soon], own_sems.at[0])
+    store_head = pltpu.make_async_copy(head, head_out, own_sems.at[2 + n_dp])
     store = pltpu.make_async_copy(final, final_out, own_sems.at[1])
     load.start()
     a = lax.axis_index("dp")
@@ -465,21 +468,26 @@
     across[0].start()
     across[1].start()
     blocks = [PlaneSpread(mine, final, sems, 13 * o, o * rows, rows) for o in range(n_dp)]
-    tile = 512 if vocab % 512 == 0 else vocab
-
-    def use(b):
+    late_rows = [
+        peer_copy(late_ref.at[a ^ o], head.at[a, late], sems, 15 * n_dp + 5 + o, dp=a ^ o)
+        for o in range(1, n_dp)
+    ]
+
+    def multiply(b, first, number):
         part = pl.ds(b * rows, rows)
 
-        @pl.loop(0, vocab // tile)
+        @pl.loop(0, number // 256)
         def _(v):
-            at = pl.ds(pl.multiple_of(v * tile, tile), tile)
+            at = pl.ds(pl.multiple_of(first + v * 256, 256), 256)
             value = None
             for p in range(n_dp):
                 x = flat(final[:, part, pl.ds(p * wide, wide)])
                 term = mm(x, head[p, at, :], CONTRACT_LAST)
                 value = term if value is None else value + term
-            logits[:, part, at] = value.reshape(8, rows, tile)
-
+            logits[:, part, at] = value.reshape(8, rows, 256)
+
+    def use(b):
+        part = pl.ds(b * rows, rows)
         value = flat(logits[:, part, :])
         top = jnp.max(value, axis=1, keepdims=True)
         expo = jnp.sum(jnp.exp(value - top), axis=1, keepdims=True)
@@ -490,12 +498,15 @@
         for k in range(3):
             stats[k, b : b + 1, :] = packed[k : k + 1]
 
+    most = vocab - count
     blocks[0].begin()
     across[0].wait_recv()
     blocks[1].begin()
     blocks[0].relay()
     across[1].wait_recv()
     across[2].start()
+    for copy in late_rows:
+        copy.start()
     blocks[2].begin()
     blocks[1].relay()
     blocks[0].relay_far()
@@ -503,18 +514,26 @@
     blocks[3].begin()
     blocks[2].relay()
     blocks[1].relay_far()
+    head[a, late] = late_ref[a]
     blocks[0].arrive()
     load.wait()
-    use(0)
+    multiply(0, 0, most)
     blocks[3].relay()
     blocks[2].relay_far()
     blocks[1].arrive()
-    use(1)
+    multiply(1, 0, most)
     blocks[3].relay_far()
     blocks[2].arrive()
-    use(2)
+    multiply(2, 0, most)
+    for copy in late_rows:
+        copy.wait_recv()
+    store_head.start()
+    for b in range(3):
+        multiply(b, most, count)
+        use(b)
     blocks[3].arrive()
     store.start()
+    multiply(3, 0, vocab)
     use(3)
     stats_steps(n_dp, stats, seen, plane, mid, line, sems, 14 * n_dp)
 
@@ -540,23 +559,28 @@
         copy.wait_send()
     for each in blocks:
         each.close()
+    for copy in late_rows:
+        copy.wait_send()
     store.wait()
-
-
-def head_call(n_dp, rows, head, target, scale):
+    store_head.wait()
+
+
+def head_call(n_dp, rows, head, late, target, scale):
     total = n_dp * rows.shape[0]
-    vocab = head.shape[1]
+    vocab = head.shape[1] + late.shape[1]
+    whole = (n_dp, vocab, head.shape[2])
     stats = (3, n_dp, 8 * rows.shape[0])
-    outs = [((8, total, D), BF16), ((8, total, vocab), BF16), ((2,) + stats[1:], F32)]
+    outs = [((8, total, D), BF16), ((8, total, vocab), BF16), (whole, BF16)]
+    outs.append(((2,) + stats[1:], F32))
     anywhere = pl.BlockSpec(memory_space=pl.ANY)
     return pl.pallas_call(
         functools.partial(head_kernel, n_dp),
         out_shape=[jax.ShapeDtypeStruct(shape, dtype) for shape, dtype in outs],
-        in_specs=[pl.BlockSpec(memory_space=pltpu.VMEM)] * 3 + [anywhere],
-        out_specs=[anywhere, anywhere, pl.BlockSpec(memory_space=pltpu.VMEM)],
+        in_specs=[pl.BlockSpec(memory_space=pltpu.VMEM)] * 4 + [anywhere],
+        out_specs=[anywhere] * 3 + [pl.BlockSpec(memory_space=pltpu.VMEM)],
         scratch_shapes=[
             pltpu.VMEM((8, total, D), BF16),
-            pltpu.VMEM(head.shape, BF16),
+            pltpu.VMEM(whole, BF16),
             pltpu.VMEM((total, D), BF16),
             pltpu.VMEM((8, total, vocab), F32),
             pltpu.VMEM(stats, F32),
@@ -564,15 +588,15 @@
             pltpu.VMEM(stats, F32),
             pltpu.VMEM((n_dp - 1,) + stats, F32),
             pltpu.VMEM((8, total, vocab), BF16),
-            pltpu.SemaphoreType.DMA((2, 14 * n_dp + 6 + n_dp)),
-            pltpu.SemaphoreType.DMA((2 + n_dp,)),
+            pltpu.SemaphoreType.DMA((2, 16 * n_dp + 5)),
+            pltpu.SemaphoreType.DMA((3 + n_dp,)),
         ],
         compiler_params=pltpu.CompilerParams(
-            collective_id=5, has_side_effects=True, vmem_limit_bytes=56 << 20
+            collective_id=5, has_side_effects=True, vmem_limit_bytes=60 << 20
         ),
         cost_estimate=pl.CostEstimate(flops=0, bytes_accessed=1 << 20, transcendentals=0),
         name="head",
-    )(rows, target, scale, head)
+    )(rows, target, scale, late, head)
 
 
 def head_back_kernel(n_dp, cut, dlogits, head, x_in, gain, final_ref, *refs):
@@ -1360,8 +1384,10 @@
 
     wqkv, wout, wgate, wdown = place_tiles(slot_of, slots, shapes)
 
-    table_late = after(table_low, slots, h1)
-    head_parts = lax.all_to_all(table_late.reshape(n_dp, sub, cols), "dp", 0, 0)
+    soon = sub - 256 if fused else sub
+    by_part = table_low.reshape(n_dp, sub, cols)
+    table_late = after(by_part[:, :soon], slots, h1)
+    head_parts = lax.all_to_all(table_late, "dp", 0, 0)
 
     half = HD // 2
     freq = ROPE_BASE ** (-jnp.arange(half).astype(F32) * 2.0 / HD)
@@ -1428,8 +1454,10 @@
 
     first = mp * vocab_part + dp * sub
     if fused:
-        final, dlogits, seen = head_call(
-            n_dp, final, head_parts, by_line(row_target - first), by_line(row_scale)
+        final, dlogits, head_parts, seen = head_call(
+            n_dp,
+            *(final, head_parts, by_part[:, soon:]),
+            *(by_line(row_target - first), by_line(row_scale)),
         )
         lse, picked = seen[0, 0], seen[1, 0]
         dlogits = dlogits.reshape(-1, sub)

time: 1140 us -> 1120 us (0.982)
  waiting for transfers between devices: 400 us -> 372 us
    all_to_all x1, waiting for transfers between devices: 21.3 us -> 0.01 us  [body(): head_parts = lax.all_to_all(table_late, 'dp', 0, 0)]
  transfers between devices with their start and end apart: 33 -> 33, of which waited for: 25 -> 24; matrix products, arithmetic and copies ran while one was open for 18% -> 19% of each run, Pallas kernels for 19% -> 20%
where the time goes in v3:
time: 1120 us; the launch traced here: 1110 us
  Pallas kernels  445 us (40%)
  waiting for transfers between devices  372 us (33%)
  other arithmetic  136 us (12%)
  local copies, waits for them, and re-layouts  92.1 us (8%)
  starting transfers between devices  45.4 us (4%)
  between operations  21.6 us (2%)
    pallas_call x5, Pallas kernels, exchange(): pl.pallas_call(kernel, out_shape=[jax.ShapeDtypeStruct(shape, dtype) for...  240 us
    ppermute x29, waiting for transfers between devices, swap(): return lax.ppermute(x, axis, [(i, i ^ bit) for i in range(n)])  151 us
    all_gather x1, waiting for transfers between devices, body(): lax.all_gather(block_master[0].astype(BF16), 'dp', axis=0, tiled=True)  112 us
    reduce_scatter x1, waiting for transfers between devices, body(): own_slots = lax.psum_scatter(slots, 'dp', scatter_dimension=0, tiled=True)  109 us
    pallas_call x1, Pallas kernels, head_call(): pl.pallas_call(functools.partial(head_kernel, n_dp), out_shape=[jax.Shape...  78.7 us
    scatter-add x1, other arithmetic, body(): table_grad.reshape(vocab_part, cols).astype(F32).at[safe.reshape(-1)]  63.5 us
    pallas_call x1, Pallas kernels, owner_step(): pl.pallas_call(functools.partial(owner_step_kernel, steps), grid=(steps +...  63.1 us
    gather x1, local copies, waits for them, and re-layouts, body(): looked = jnp.where(valid[..., None], jnp.take(table_low, safe, axis=0), 0)  38.1 us
  transfers between devices with their start and end apart: 33, of which 24 were waited for; matrix products, arithmetic and copies ran while one was open for 19% of the time, Pallas kernels for 20%

profile of v3, /device:TPU:0, one launch (start us, length us, event | category | flops | bytes accessed | tf_op | source)
XLA Modules:
  0.0 1111.9 jit_solution(7494097480714359551)
XLA Ops:
  7.3 6.4 bitcast_convert_fusion.1
  19.6 9.3 convert_element_type.95
  31.1 38.1 %gather_fusion.2 = bf16[8192,512]{1,0:T(8,128)(2,1)} fusion(bf16[6144,512]{1,0:T(8,128)(2,1)} %convert_element_type.95, s32[8192]{0:T(1024)S(1)} %broadcast_clamp_fusion), kind=kCustom, calls=%fused_computation.2 | custom fusion | bytes 16809984 | tf_op jit(solution)/shard_map/jit(_take)/gather | solution.py:1374
  74.9 7.1 collective-permute-done.3
  102.3 8.8 collective-permute-done.4
  120.0 7.3 collective-permute-done.5
  135.3 21.2 %collective-permute-done.6 = bf16[256,512]{1,0:T(8,128)(2,1)S(1)} collective-permute-done((bf16[256,512]{1,0:T(8,128)(2,1)S(1)}, bf16[256,512]{1,0:T(8,128)(2,1)S(1)}, u32[]{:S(2)}, u32[]{:S(2)}) %collective-permute-start.6) | collective-permute-done | bytes 262176 | tf_op jit(solution)/shard_map/ppermute | solution.py:52
  156.6 9.4 collective-permute-done.10
  169.6 21.6 %collective-permute-done.15 = bf16[256,2048]{1,0:T(8,128)(2,1)S(1)} collective-permute-done((bf16[256,2048]{1,0:T(8,128)(2,1)S(1)}, bf16[256,2048]{1,0:T(8,128)(2,1)S(1)}, u32[]{:S(2)}, u32[]{:S(2)}) %collective-permute-start.15) | collective-permute-done | bytes 1048608 | tf_op jit(solution)/shard_map/ppermute | solution.py:52
  193.3 10.3 collective-permute-done.17
  214.1 112.0 %all-gather.2.cloned.1.call-done.slots_ref.refs_1_ = bf16[512,128,128]{2,1,0:T(8,128)(2,1)} async-done(((bf16[128,128,128]{2,1,0:T(8,128)(2,1)}), bf16[512,128,128]{2,1,0:T(8,128)(2,1)}) %all-gather.2.cloned.1.call-update) | async-done | bytes 16777232 | tf_op jit(solution)/shard_map/all_gather | solution.py:1325
  326.1 5.4 all-to-all-start
  359.4 9.0 place_tiles.1
  373.1 19.3 %attend.1 = (bf16[8,64,256]{2,1,0:T(8,128)(2,1)}, bf16[8,64,256]{2,1,0:T(8,128)(2,1)}, bf16[8,256,256]{2,1,0:T(8,128)(2,1)}, bf16[8,256,256]{2,1,0:T(8,128)(2,1)}) custom-call(bf16[8,256,2048]{2,1,0:T(8,128)(2,1)} %constant_dynamic-update-slice_fusion.h1_ref.refs_2_, bf16[2048,768]{1,0:T(8,128)(2,1)} %copy-done.1, ...), custom_call_target="tpu_custom_call" | custom-call | bytes 1024 | tf_op jit(solution)/shard_map/attend/pallas_call | solution.py:1261
  392.4 29.7 %attend_sum.1 = (f32[64,2048]{1,0:T(8,128)}, bf16[8,64,2048]{2,1,0:T(8,128)(2,1)}) custom-call(bf16[8,64,256]{2,1,0:T(8,128)(2,1)} %get-tuple-element.73.o, bf16[256,2048]{1,0:T(8,128)(2,1)} %copy-done.2, f32[64,2048]{1,0:T(8,128)} %slice.223.res, f32[1,2048]{1,0:T(1,128)} %get-tuple-element.135.gain), custom_call_target="tpu_custom_call" | custom-call | bytes 1024 | tf_op jit(solution)/shard_map/attend_sum/pallas_call | solution.py:799
  422.1 28.9 %units_sum.1 = (f32[64,2048]{1,0:T(8,128)}, f32[512,2048]{1,0:T(8,128)}, bf16[512,1024]{1,0:T(8,128)(2,1)}, bf16[64,2048]{1,0:T(8,128)(2,1)}) custom-call(bf16[8,64,2048]{2,1,0:T(8,128)(2,1)} %get-tuple-element.75.h2.h2_ref, bf16[2048,2048]{1,0:T(8,128)(2,1)} %get-tuple-element.76.wgate, bf16[1024,2048]{1,0:T(8,128)(2,1)} %copy-done, ...), custom_call_target="tpu_custom_call" | custom-call | bytes 1024 | tf_op jit(solution)/shard_map/units_sum/pallas_call | solution.py:799
  451.0 78.7 %head.1 = (bf16[8,256,2048]{2,1,0:T(8,128)(2,1)}, bf16[8,256,1536]{2,1,0:T(8,128)(2,1)}, bf16[4,1536,512]{2,1,0:T(8,128)(2,1)}, f32[2,4,512]{2,1,0:T(4,128)}) custom-call(bf16[64,2048]{1,0:T(8,128)(2,1)} %get-tuple-element.79.rows_ref, s32[4,512,1]{2,1,0:T(8,128)} %reshape.503.target_ref, f32[4,512,1]{2,1,0:T(8,128)} %reshape.504.scale_ref, ...), custom_call_target="tpu_custom_call" | custom-call | bytes 1048576 | tf_op jit(solution)/shard_map/head/pallas_call | solution.py:576
  529.7 71.2 %head_sum.1 = (f32[64,2048]{1,0:T(8,128)}, f32[1,2048]{1,0:T(1,128)}, bf16[8,64,2048]{2,1,0:T(8,128)(2,1)}, bf16[4,384,512]{2,1,0:T(8,128)(2,1)}, bf16[4,1152,512]{2,1,0:T(8,128)(2,1)}) custom-call(bf16[8,256,1536]{2,1,0:T(8,128)(2,1)} %get-tuple-element.80.dlogits, bf16[4,1536,512]{2,1,0:T(8,128)(2,1)} %get-tuple-element.81.head, ...), custom_call_target="tpu_custom_call" | custom-call | bytes 1024 | tf_op jit(solution)/shard_map/head_sum/pallas_call | solution.py:799
  600.9 7.7 all-to-all-start.1
  610.2 41.7 %gate_sum.1 = (f32[64,2048]{1,0:T(8,128)}, f32[1,2048]{1,0:T(1,128)}, bf16[512,2048]{1,0:T(8,128)(2,1)}, bf16[8,64,2048]{2,1,0:T(8,128)(2,1)}, bf16[1024,2048]{1,0:T(8,128)(2,1)}, /*index=5*/bf16[2048,2048]{1,0:T(8,128)(2,1)}) custom-call(bf16[8,64,2048]{2,1,0:T(8,128)(2,1)} %get-tuple-element.84.down_in, bf16[1024,2048]{1,0:T(8,128)(2,1)} %copy-done, ...), custom_call_target="tpu_custom_call" | custom-call | bytes 1024 | tf_op jit(solution)/shard_map/gate_sum/pallas_call | solution.py:799
  651.9 17.8 %attend_back.1 = (bf16[8,256,768]{2,1,0:T(8,128)(2,1)}, bf16[256,2048]{1,0:T(8,128)(2,1)}, bf16[512,128,128]{2,1,0:T(8,128)(2,1)}) custom-call(s32[512]{0:T(512)} %copy-done.5, bf16[8,64,256]{2,1,0:T(8,128)(2,1)} %get-tuple-element.70.refs_0_, bf16[8,256,256]{2,1,0:T(8,128)(2,1)} %get-tuple-element.71.refs_1_, ...), custom_call_target="tpu_custom_call" | custom-call | bytes 1024 | tf_op jit(solution)/shard_map/attend_back/pallas_call | solution.py:1242
  669.7 68.8 %input_sum.1 = (bf16[4,256,512]{2,1,0:T(8,128)(2,1)}, f32[1,2048]{1,0:T(1,128)}, bf16[2048,768]{1,0:T(8,128)(2,1)}) custom-call(bf16[8,256,768]{2,1,0:T(8,128)(2,1)} %get-tuple-element.91.dqkv, bf16[2048,768]{1,0:T(8,128)(2,1)} %copy-done.1, f32[256,2048]{1,0:T(8,128)} %convert_element_type.107.x_in, f32[1,2048]{1,0:T(1,128)} %copy-done.11, ...), custom_call_target="tpu_custom_call" | custom-call | bytes 1024 | tf_op jit(solution)/shard_map/input_sum/pallas_call | solution.py:799
  746.3 23.1 %collective-permute-done.19 = bf16[1024,512]{1,0:T(8,128)(2,1)S(1)} collective-permute-done((bf16[1024,512]{1,0:T(8,128)(2,1)S(1)}, bf16[1024,512]{1,0:T(8,128)(2,1)S(1)}, u32[]{:S(2)}, u32[]{:S(2)}) %collective-permute-start.19) | collective-permute-done | bytes 1048608 | tf_op jit(solution)/shard_map/ppermute | solution.py:52
  771.6 11.1 collective-permute-done.21
  787.6 6.1 collective-permute-done.24
  824.6 7.6 bitcast_select_fusion
  835.0 6.8 bitcast_convert_fusion
  841.8 63.5 %scatter_custom_fusion.1.refs_6_ = f32[6144,512]{1,0:T(8,128)} fusion(f32[6144,512]{1,0:T(8,128)} %bitcast_convert_fusion, s32[8192]{0:T(1024)S(1)} %bitcast.162, bf16[8192,512]{1,0:T(8,128)(2,1)} %bitcast_select_fusion), kind=kCustom, calls=%fused_computation.8 | custom fusion | flops 8388608 | bytes 20971520 | tf_op jit(solution)/shard_map/scatter-add | solution.py:1584
  905.2 8.4 multiply_reduce_fusion
  915.1 108.5 %reduce-scatter.2.cloned.1.call-done.slots_ref.refs_0_ = bf16[128,128,128]{2,1,0:T(8,128)(2,1)} async-done(((bf16[512,128,128]{2,1,0:T(8,128)(2,1)}), bf16[128,128,128]{2,1,0:T(8,128)(2,1)}) %reduce-scatter.2.cloned.1.call-update) | async-done | bytes 4194320 | tf_op jit(solution)/shard_map/reduce_scatter | solution.py:1578
  1023.6 14.2 %total.1 = f32[2,8,128]{2,1,0:T(8,128)} custom-call(bf16[128,128,128]{2,1,0:T(8,128)(2,1)} %reduce-scatter.2.cloned.1.call-done.slots_ref.refs_0_, f32[2,8,128]{2,1,0:T(8,128)} %scatter.13.more_ref), custom_call_target="tpu_custom_call" | custom-call | tf_op jit(solution)/shard_map/total/pallas_call | solution.py:893
  1040.6 63.1 %owner_step.1 = (f32[128,128,128]{2,1,0:T(8,128)}, bf16[128,128,128]{2,1,0:T(8,128)(2,1)}, f32[128,128,128]{2,1,0:T(8,128)}, f32[128,128,128]{2,1,0:T(8,128)}, f...) custom-call(f32[1,1]{1,0:T(1,128)} %bitcast.53.factor_ref, ...), custom_call_target="tpu_custom_call" | custom-call | tf_op jit(solution)/shard_map/owner_step/pallas_call | solution.py:1077
  (272 shorter events, 147.9 us)
Async XLA Ops:
  7.2 318.9 %all-gather.2.cloned.1.call-start = ((), (), s32[]{:S(2)}) async-start(), calls=%async_computation.3 | async-start | bytes 20971520 | tf_op jit(solution)/shard_map/all_gather | solution.py:1325
  13.8 15.1 %collective-permute-start.2 = (s32[2,1537]{1,0:T(2,128)S(1)}, s32[2,1537]{1,0:T(2,128)S(1)}, u32[]{:S(2)}, u32[]{:S(2)}) collective-permute-start(s32[2,1537]{1,0:T(2,128)S(1)} %pad_add_fusion.1), channel_id=1, source_target_pairs={{0,24},{8,16},{16,8},{24,0},{1,25},{9,17},{17,9},{25,1},{2,26},{10... | collective-permute-start | bytes 36896 | tf_op jit(solution)/shard_map/ppermute | solution.py:52
  19.0 10.0 collective-permute-start.1
  19.0 10.0 collective-permute-start
  74.8 7.2 collective-permute-start.3
  85.8 25.4 %collective-permute-start.4 = (bf16[2,2,256,512]{3,2,1,0:T(8,128)(2,1)S(1)}, bf16[2,2,256,512]{3,2,1,0:T(8,128)(2,1)}, u32[]{:S(2)}, u32[]{:S(2)}) collective-permute-start(bf16[2,2,256,512]{3,2,1,0:T(8,128)(2,1)S(1)} %slice.161), channel_id=1, source_target_pairs={{0,2},{1,3},{2,0},{3,1},{4,6},{5,7},{6,4},{7,5},{8,10},{9,11},{10,... | collective-permute-start | bytes 3145736 | tf_op jit(solution)/shard_map/ppermute | solution.py:52
  91.0 26.4 %collective-permute-start.7 = (bf16[2,2,256,512]{3,2,1,0:T(8,128)(2,1)}, bf16[2,2,256,512]{3,2,1,0:T(8,128)(2,1)}, u32[]{:S(2)}, u32[]{:S(2)}) collective-permute-start(bf16[2,2,256,512]{3,2,1,0:T(8,128)(2,1)} %slice.215), channel_id=1, source_target_pairs={{0,4},{1,5},{2,6},{3,7},{4,0},{5,1},{6,2},{7,3},{8,12},{9,13},{10,... | collective-permute-start | bytes 3145736 | tf_op jit(solution)/shard_map/ppermute | solution.py:52
  92.5 7.5 collective-permute-start.11
  93.7 6.3 collective-permute-start.12
  96.8 5.5 collective-permute-start.13
  112.8 14.6 %collective-permute-start.5 = (bf16[2,256,512]{2,1,0:T(8,128)(2,1)S(1)}, bf16[2,256,512]{2,1,0:T(8,128)(2,1)S(1)}, u32[]{:S(2)}, u32[]{:S(2)}) collective-permute-start(bf16[2,256,512]{2,1,0:T(8,128)(2,1)S(1)} %fusion.6), channel_id=1, source_target_pairs={{0,4},{1,5},{2,6},{3,7},{4,0},{5,1},{6,2},{7,3},{8,12},{9,13},{10,... | collective-permute-start | bytes 1572872 | tf_op jit(solution)/shard_map/ppermute | solution.py:52
  119.3 11.8 %collective-permute-start.8 = (bf16[2,256,512]{2,1,0:T(8,128)(2,1)S(1)}, bf16[2,256,512]{2,1,0:T(8,128)(2,1)S(1)}, u32[]{:S(2)}, u32[]{:S(2)}) collective-permute-start(bf16[2,256,512]{2,1,0:T(8,128)(2,1)S(1)} %fusion.7), channel_id=1, source_target_pairs={{0,2},{1,3},{2,0},{3,1},{4,6},{5,7},{6,4},{7,5},{8,10},{9,11},{10,... | collective-permute-start | bytes 1572872 | tf_op jit(solution)/shard_map/ppermute | solution.py:52
  127.5 28.9 %collective-permute-start.6 = (bf16[256,512]{1,0:T(8,128)(2,1)S(1)}, bf16[256,512]{1,0:T(8,128)(2,1)S(1)}, u32[]{:S(2)}, u32[]{:S(2)}) collective-permute-start(bf16[256,512]{1,0:T(8,128)(2,1)S(1)} %slice_bitcast_fusion.4), channel_id=1, source_target_pairs={{0,8},{8,0},{16,24},{24,16},{1,9},{9,1},{17,25},{25,17},{2,10},{10... | collective-permute-start | bytes 786440 | tf_op jit(solution)/shard_map/ppermute | solution.py:52
  131.3 25.2 %collective-permute-start.9 = (bf16[256,512]{1,0:T(8,128)(2,1)S(1)}, bf16[256,512]{1,0:T(8,128)(2,1)S(1)}, u32[]{:S(2)}, u32[]{:S(2)}) collective-permute-start(bf16[256,512]{1,0:T(8,128)(2,1)S(1)} %get-tuple-element.128), channel_id=1, source_target_pairs={{0,16},{8,24},{16,0},{24,8},{1,17},{9,25},{17,1},{25,9},{2,18},{10... | collective-permute-start | bytes 786440 | tf_op jit(solution)/shard_map/ppermute | solution.py:52
  133.3 32.6 %collective-permute-start.10 = (bf16[256,512]{1,0:T(8,128)(2,1)S(1)}, bf16[256,512]{1,0:T(8,128)(2,1)S(1)}, u32[]{:S(2)}, u32[]{:S(2)}) collective-permute-start(bf16[256,512]{1,0:T(8,128)(2,1)S(1)} %get-tuple-element.127), channel_id=1, source_target_pairs={{0,24},{8,16},{16,8},{24,0},{1,25},{9,17},{17,9},{25,1},{2,26},{10... | collective-permute-start | bytes 786440 | tf_op jit(solution)/shard_map/ppermute | solution.py:52
  167.6 23.6 %collective-permute-start.15 = (bf16[256,2048]{1,0:T(8,128)(2,1)S(1)}, bf16[256,2048]{1,0:T(8,128)(2,1)S(1)}, u32[]{:S(2)}, u32[]{:S(2)}) collective-permute-start(bf16[256,2048]{1,0:T(8,128)(2,1)S(1)} %get-tuple-element.122), channel_id=1, source_target_pairs={{0,4},{1,5},{2,6},{3,7},{4,0},{5,1},{6,2},{7,3},{8,12},{9,13},{10,... | collective-permute-start | bytes 3145736 | tf_op jit(solution)/shard_map/ppermute | solution.py:52
  169.1 24.1 %collective-permute-start.14 = (bf16[256,2048]{1,0:T(8,128)(2,1)S(1)}, bf16[256,2048]{1,0:T(8,128)(2,1)S(1)}, u32[]{:S(2)}, u32[]{:S(2)}) collective-permute-start(bf16[256,2048]{1,0:T(8,128)(2,1)S(1)} %get-tuple-element.122), channel_id=1, source_target_pairs={{0,2},{1,3},{2,0},{3,1},{4,6},{5,7},{6,4},{7,5},{8,10},{9,11},{10,... | collective-permute-start | bytes 3145736 | tf_op jit(solution)/shard_map/ppermute | solution.py:52
  191.2 12.4 %collective-permute-start.17 = (bf16[128,2048]{1,0:T(8,128)(2,1)S(1)}, bf16[128,2048]{1,0:T(8,128)(2,1)S(1)}, u32[]{:S(2)}, u32[]{:S(2)}) collective-permute-start(bf16[128,2048]{1,0:T(8,128)(2,1)S(1)} %slice.222), channel_id=1, source_target_pairs={{0,2},{1,3},{2,0},{3,1},{4,6},{5,7},{6,4},{7,5},{8,10},{9,11},{10,... | collective-permute-start | bytes 1572872 | tf_op jit(solution)/shard_map/ppermute | solution.py:52
  193.3 10.6 collective-permute-start.16
  204.5 7.2 collective-permute-start.18
  326.1 124.9 %all-to-all-start = ((bf16[4,1280,512]{2,1,0:T(8,128)(2,1)}), bf16[4,1280,512]{2,1,0:T(8,128)(2,1)}, u32[]{:S(2)}, u32[]{:S(2)}) async-start(bf16[4,1280,512]{2,1,0:T(8,128)(2,1)} %after.2), calls=%async_computation | async-start | bytes 10485760 | tf_op jit(solution)/shard_map/all_to_all | solution.py:1390
  600.9 142.1 %all-to-all-start.1 = ((bf16[4,1152,512]{2,1,0:T(8,128)(2,1)}), bf16[4,1152,512]{2,1,0:T(8,128)(2,1)}, u32[]{:S(2)}, u32[]{:S(2)}) async-start(bf16[4,1152,512]{2,1,0:T(8,128)(2,1)} %get-tuple-element.96), calls=%async_computation.1 | async-start | bytes 9437184 | tf_op jit(solution)/shard_map/all_to_all | solution.py:1519
  608.6 415.0 %reduce-scatter.2.cloned.1.call-start = ((), (), s32[]{:S(2)}) async-start(), calls=%async_computation.4 | async-start | bytes 20971520 | tf_op jit(solution)/shard_map/reduce_scatter | solution.py:1578
  744.3 25.2 %collective-permute-start.19 = (bf16[1024,512]{1,0:T(8,128)(2,1)S(1)}, bf16[1024,512]{1,0:T(8,128)(2,1)S(1)}, u32[]{:S(2)}, u32[]{:S(2)}) collective-permute-start(bf16[1024,512]{1,0:T(8,128)(2,1)S(1)} %bitcast.128), channel_id=1, source_target_pairs={{0,2},{1,3},{2,0},{3,1},{4,6},{5,7},{6,4},{7,5},{8,10},{9,11},{10,... | collective-permute-start | bytes 3145736 | tf_op jit(solution)/shard_map/ppermute | solution.py:52
  745.3 25.2 %collective-permute-start.20 = (bf16[1024,512]{1,0:T(8,128)(2,1)S(1)}, bf16[1024,512]{1,0:T(8,128)(2,1)S(1)}, u32[]{:S(2)}, u32[]{:S(2)}) collective-permute-start(bf16[1024,512]{1,0:T(8,128)(2,1)S(1)} %bitcast.129), channel_id=1, source_target_pairs={{0,4},{1,5},{2,6},{3,7},{4,0},{5,1},{6,2},{7,3},{8,12},{9,13},{10,... | collective-permute-start | bytes 3145736 | tf_op jit(solution)/shard_map/ppermute | solution.py:52
  769.5 13.3 %collective-permute-start.21 = (bf16[512,512]{1,0:T(8,128)(2,1)S(1)}, bf16[512,512]{1,0:T(8,128)(2,1)S(1)}, u32[]{:S(2)}, u32[]{:S(2)}) collective-permute-start(bf16[512,512]{1,0:T(8,128)(2,1)S(1)} %slice.228), channel_id=1, source_target_pairs={{0,4},{1,5},{2,6},{3,7},{4,0},{5,1},{6,2},{7,3},{8,12},{9,13},{10,... | collective-permute-start | bytes 1572872 | tf_op jit(solution)/shard_map/ppermute | solution.py:52
  770.6 13.0 %collective-permute-start.22 = (bf16[512,512]{1,0:T(8,128)(2,1)S(1)}, bf16[512,512]{1,0:T(8,128)(2,1)S(1)}, u32[]{:S(2)}, u32[]{:S(2)}) collective-permute-start(bf16[512,512]{1,0:T(8,128)(2,1)S(1)} %slice.229), channel_id=1, source_target_pairs={{0,2},{1,3},{2,0},{3,1},{4,6},{5,7},{6,4},{7,5},{8,10},{9,11},{10,... | collective-permute-start | bytes 1572872 | tf_op jit(solution)/shard_map/ppermute | solution.py:52
  786.8 33.0 %collective-permute-start.23 = (bf16[4,1024,512]{2,1,0:T(8,128)(2,1)}, bf16[4,1024,512]{2,1,0:T(8,128)(2,1)}, u32[]{:S(2)}, u32[]{:S(2)}) collective-permute-start(bf16[4,1024,512]{2,1,0:T(8,128)(2,1)} %pad_maximum_fusion.2), channel_id=1, source_target_pairs={{0,1},{1,0},{2,3},{3,2},{4,5},{5,4},{6,7},{7,6},{8,9},{9,8},{10,11... | collective-permute-start | bytes 12582920 | tf_op jit(solution)/shard_map/ppermute | solution.py:52
  786.9 6.7 collective-permute-start.24
  793.7 4.0 collective-permute-start.25
  801.7 5.5 collective-permute-start.27
  807.3 7.0 collective-permute-start.28
  (29 other events, 813.0 us)
Sparse Core Ops, SparseCore 0:
  13.8 312.2 all-gather.1
  743.2 280.4 reduce-scatter.1
